TPU v7x, 32 devices: a whole 2x2x4 slice. The times are simulated.
32 devices in a mesh: groups: 2 (over y), views: 4 (over z), heads: 2 (over x), sub: 2 (over core).
Axes of the slice: x: 2, y: 2, z: 4, core: 2. Of those that a mesh axis runs over, the one named last changes fastest.
Arguments:
- tokens: bfloat16 [4096, 2048], P(('groups', 'views', 'sub'), 'heads'), parts along dimension 0, may hold values from -40 to 40
- w_query: bfloat16 [2048, 2048], P(None, 'heads'), may hold values from -0.125 to 0.125
- w_key: bfloat16 [2048, 2048], P(None, 'heads'), may hold values from -0.125 to 0.125
- w_value: bfloat16 [2048, 2048], P(None, 'heads'), may hold values from -0.125 to 0.125
- w_out: bfloat16 [2048, 2048], P('heads'), may hold values from -0.125 to 0.125
- partners: int32 [64, 20], P(('groups', 'views', 'sub')), parts along dimension 0, may hold values from 0 to 31, as said below
- counts: int32 [64], P(('groups', 'views', 'sub')), parts along dimension 0, may hold values from 6 to 20, as said below
Outputs:
- attended: bfloat16 [4096, 2048], P(('groups', 'views', 'sub'), 'heads'), parts along dimension 0
There are 2 independent parts, one for each index of `groups`. A program takes and returns all parts, laid end to end along the dimension named above; an argument that names none is the same for every part. Nothing has to cross between parts.
Inputs may be any that keep to these rules, and one draw needn't show every extreme that they name: Views lie on a closed orbit of 32 cameras. For t < counts[i], partners[i, t] are distinct views other than i that lie at most 10 views away from i around the orbit (cyclically), in rising order of signed offset; the graph is symmetric; slots t >= counts[i] hold i. `counts`: every view is partnered with the 6 views nearest to it on the orbit; some view has all 20 slots filled in every draw.
All inputs are finite; a program needn't handle non-finite values.
Results may differ from a plain program's by a relative error of at most 0.012.
The roundings to bfloat16 on the way count: a program that leaves them out, or rounds other values in their place, can miss the bound.
Values may be sent and summed in bfloat16 or wider, within the bound.
No kernel may reach another device: no remote copies, remote signals or barrier semaphores. Data moves between devices by JAX's collectives and lax.ppermute only.
A program may use at most 128 MiB of HBM per device.

v0:
```python
import math

import jax
import jax.numpy as jnp
from jax import lax
from jax.sharding import PartitionSpec as P

HD = 128
L = 64


def absorb(state, query, keys, values, keep):
    running_max, weight_sum, weighted = state
    scaling = HD ** (-0.5)
    scores = jnp.einsum("aqhd,khd->ahqk", query, keys, preferred_element_type=jnp.float32)
    mask = keep[:, None, None, :]
    scores = jnp.where(mask, scores * scaling, -1e30)
    new_max = jnp.maximum(running_max, jnp.max(scores, axis=-1))
    weights = jnp.where(mask, jnp.exp(scores - new_max[..., None]), 0.0)
    factor = jnp.exp(running_max - new_max)
    weight_sum = weight_sum * factor + jnp.sum(weights, axis=-1)
    rounded = weights.astype(jnp.bfloat16)
    update = jnp.einsum("ahqk,khd->ahqd", rounded, values, preferred_element_type=jnp.float32)
    weighted = weighted * factor[..., None] + update
    return (new_max, weight_sum, weighted)


def shards(tokens, w_query, w_key, w_value, w_out, partners, counts):
    rows = tokens.shape[0]
    views_here = rows // L
    heads_here = w_query.shape[1] // HD
    piece = lax.all_gather(tokens, "heads", axis=1, tiled=True)
    query_sum, key_sum, value_sum = tuple(
        (
            jnp.dot(piece, weight, preferred_element_type=jnp.float32)
            for weight in (w_query, w_key, w_value)
        )
    )
    query = query_sum.astype(jnp.bfloat16).reshape(views_here, L, heads_here, HD)
    keys_flat = key_sum.astype(jnp.bfloat16)
    values_flat = value_sum.astype(jnp.bfloat16)
    group = lax.axis_size(("views", "sub"))
    total_views = views_here * group
    mine = lax.axis_index(("views", "sub")) * views_here + jnp.arange(views_here, dtype=jnp.int32)
    slots = jnp.arange(partners.shape[1], dtype=jnp.int32)
    valid = slots[None, :] < counts[:, None]
    state = (
        jnp.full((views_here, heads_here, L), -1e30, jnp.float32),
        jnp.zeros((views_here, heads_here, L), jnp.float32),
        jnp.zeros((views_here, heads_here, L, HD), jnp.float32),
    )
    every_view = jnp.arange(total_views, dtype=jnp.int32)
    allowed = jnp.any(
        valid[:, :, None] & (partners[:, :, None] == every_view[None, None, :]), axis=1
    )
    allowed = allowed | (mine[:, None] == every_view[None, :])
    pieces = (
        lax.all_gather(keys_flat, ("views", "sub"), axis=0, tiled=True),
        lax.all_gather(values_flat, ("views", "sub"), axis=0, tiled=True),
    )
    piece_views = pieces[0].shape[0] // L
    block = math.gcd(piece_views, 8)

    def inner(index, inner_state):
        key_rows = lax.dynamic_slice_in_dim(pieces[0], index * block * L, block * L, 0).reshape(
            block * L, heads_here, HD
        )
        value_rows = lax.dynamic_slice_in_dim(pieces[1], index * block * L, block * L, 0).reshape(
            block * L, heads_here, HD
        )
        keep = jnp.repeat(
            lax.dynamic_slice_in_dim(allowed, index * block, block, 1),
            L,
            axis=1,
            total_repeat_length=block * L,
        )
        return absorb(inner_state, query, key_rows, value_rows, keep)

    state = lax.fori_loop(0, piece_views // block, inner, state)
    running_max, weight_sum, weighted = state
    mixed = weighted / weight_sum[..., None]
    mixed = jnp.transpose(mixed, (0, 2, 1, 3)).reshape(rows, heads_here * HD).astype(jnp.bfloat16)
    partial_sum = jnp.dot(mixed, w_out, preferred_element_type=jnp.float32)
    return lax.psum_scatter(
        partial_sum.astype(jnp.bfloat16), "heads", scatter_dimension=1, tiled=True
    )


def solution(mesh):
    in_specs = (
        P(("groups", "views", "sub"), "heads"),
        P(None, "heads"),
        P(None, "heads"),
        P(None, "heads"),
        P("heads", None),
        P(("groups", "views", "sub"), None),
        P(("groups", "views", "sub")),
    )
    out_specs = P(("groups", "views", "sub"), "heads")
    return jax.shard_map(shards, mesh=mesh, in_specs=in_specs, out_specs=out_specs, check_vma=False)
```

profile of v0, /device:TPU:0, one launch (start us, length us, event | category | flops | bytes accessed | tf_op | source)
XLA Modules:
  0.0 207.8 jit_solution(12611490437025673640)
XLA Ops:
  6.5 0.7 all-gather.4.cloned.1.call-update
  7.3 25.6 %all-gather.4.cloned.1.call-done = bf16[256,2048]{1,0:T(8,128)(2,1)} async-done(((bf16[256,1024]{1,0:T(8,128)(2,1)}), bf16[256,2048]{1,0:T(8,128)(2,1)}) %all-gather.4.cloned.1.call-update) | async-done | bytes 1048592 | tf_op jit(solution)/shard_map/all_gather | solution.py:32
  32.9 4.6 %convolution_convert_fusion.1 = bf16[256,1024]{1,0:T(8,128)(2,1)} fusion(bf16[256,2048]{1,0:T(8,128)(2,1)} %all-gather.4.cloned.1.call-done, bf16[2048,1024]{1,0:T(8,128)(2,1)} %param.14), kind=kOutput, calls=%fused_computation.30 | convolution fusion | flops 1074003968 | bytes 5767168 | tf_op jit(solution)/shard_map/dot_general | solution.py:35
  37.7 4.2 %convolution_convert_fusion.3 = bf16[256,1024]{1,0:T(8,128)(2,1)} fusion(bf16[256,2048]{1,0:T(8,128)(2,1)S(1)} %copy-done.5, bf16[2048,1024]{1,0:T(8,128)(2,1)} %param.13), kind=kOutput, calls=%fused_computation.32 | convolution fusion | flops 1074003968 | bytes 5767168 | tf_op jit(solution)/shard_map/dot_general | solution.py:35
  42.3 3.5 %fusion.16 = bf16[32,8,8,128]{3,1,2,0:T(8,128)(2,1)S(1)} fusion(bf16[256,2048]{1,0:T(8,128)(2,1)S(1)} %copy-done.5, bf16[2048,1024]{1,0:T(8,128)(2,1)} %param.12), kind=kOutput, calls=%fused_computation.33 | convolution fusion | flops 1074003968 | bytes 5767168 | tf_op jit(solution)/shard_map/dot_general | solution.py:35
  46.0 0.9 copy.23
  46.9 38.0 %all-gather.8.cloned.1.call-done = bf16[2048,1024]{1,0:T(8,128)(2,1)} async-done(((bf16[256,1024]{1,0:T(8,128)(2,1)}), bf16[2048,1024]{1,0:T(8,128)(2,1)}) %all-gather.8.cloned.1.call-update) | async-done | bytes 4194320 | tf_op jit(solution)/shard_map/all_gather | solution.py:59
  84.9 47.6 %all-gather.6.cloned.1.call-done = bf16[2048,1024]{1,0:T(8,128)(2,1)} async-done(((bf16[256,1024]{1,0:T(8,128)(2,1)}), bf16[2048,1024]{1,0:T(8,128)(2,1)}) %all-gather.6.cloned.1.call-update) | async-done | bytes 4194320 | tf_op jit(solution)/shard_map/all_gather | solution.py:58
  132.4 43.3 %while.25 = (s32[]{:T(128)}, f32[4,8,64]{2,0,1:T(4,128)S(1)}, f32[4,8,64]{2,0,1:T(4,128)S(1)}, f32[4,8,64,128]{3,2,0,1:T(8,128)}, pred[4,32]{1,0:T(4,128)(4,1)S(...) while((s32[]{:T(128)}, f32[4,8,64]{2,0,1:T(4,128)S(1)}, ...), condition=%wide.region_4.5_spmd.clone, body=%wide.region_1.4_spmd.clone.sunk | while | flops 551308800 | bytes 38446572 | solution.py:79
  132.8 1.2 gather_fusion
  134.2 1.7 constant_dynamic-slice_fusion.5
  135.9 0.5 copy.43
  136.5 0.5 copy.46
  137.0 1.7 fusion.47
  138.8 0.6 fusion.48
  139.4 1.3 fusion.49
  140.7 1.5 fusion.51
  142.2 1.1 copy-done.1
  143.6 1.2 gather_fusion
  145.0 1.7 constant_dynamic-slice_fusion.5
  146.8 0.5 copy.43
  147.3 0.5 copy.46
  147.9 1.7 fusion.47
  149.6 0.6 fusion.48
  150.2 1.3 fusion.49
  151.5 1.5 fusion.51
  153.0 1.1 copy-done.1
  154.4 1.2 gather_fusion
  155.9 1.7 constant_dynamic-slice_fusion.5
  157.6 0.5 copy.43
  158.1 0.5 copy.46
  158.7 1.7 fusion.47
  160.4 0.6 fusion.48
  161.0 1.3 fusion.49
  162.3 1.5 fusion.51
  163.8 1.1 copy-done.1
  165.2 1.2 gather_fusion
  166.7 1.7 constant_dynamic-slice_fusion.5
  168.4 0.5 copy.43
  169.0 0.5 copy.46
  169.5 1.7 fusion.47
  171.2 0.6 fusion.48
  171.8 1.3 fusion.49
  173.2 1.5 fusion.51
  174.7 1.1 copy-done.1
  175.7 1.6 fusion.19
  177.6 4.4 %convolution_convert_fusion = bf16[256,2048]{1,0:T(8,128)(2,1)} fusion(bf16[1024,2048]{1,0:T(8,128)(2,1)} %param.15, bf16[32,8,8,128]{3,2,1,0:T(8,128)(2,1)S(1)} %bitcast.103), kind=kOutput, calls=%fused_computation.29 | convolution fusion | flops 1074266112 | bytes 5767168 | tf_op jit(solution)/shard_map/dot_general | solution.py:83
  182.1 19.2 %reduce-scatter.2.cloned.1.call-done = bf16[256,1024]{1,0:T(8,128)(2,1)} async-done(((bf16[256,2048]{1,0:T(8,128)(2,1)}), bf16[256,1024]{1,0:T(8,128)(2,1)}) %reduce-scatter.2.cloned.1.call-update) | async-done | bytes 524304 | tf_op jit(solution)/shard_map/reduce_scatter | solution.py:84
  (85 shorter events, 3.5 us)
Async XLA Ops:
  6.5 26.4 %all-gather.4.cloned.1.call-start = ((), (), s32[]{:S(2)}) async-start(), calls=%async_computation.1 | async-start | bytes 1572864 | tf_op jit(solution)/shard_map/all_gather | solution.py:32
  7.3 77.6 %all-gather.8.cloned.1.call-start = ((), (), s32[]{:S(2)}) async-start(), calls=%async_computation.3 | async-start | bytes 4718592 | tf_op jit(solution)/shard_map/all_gather | solution.py:59
  32.9 4.7 %copy-start.5 = (bf16[256,2048]{1,0:T(8,128)(2,1)S(1)}, bf16[256,2048]{1,0:T(8,128)(2,1)}, u32[]{:S(2)}) copy-start(bf16[256,2048]{1,0:T(8,128)(2,1)} %all-gather.4.cloned.1.call-done) | copy-start | bytes 3145732
  37.6 4.4 %copy-start.3 = (s32[4,20]{1,0:T(4,128)S(1)}, s32[4,20]{1,0:T(4,128)}, u32[]{:S(2)}) copy-start(s32[4,20]{1,0:T(4,128)} %param.16) | copy-start | bytes 964
  37.6 4.5 %copy-start.4 = (s32[4]{0:T(128)S(1)}, s32[4]{0:T(128)}, u32[]{:S(2)}) copy-start(s32[4]{0:T(128)} %param.17) | copy-start | bytes 52
  37.6 94.8 %all-gather.6.cloned.1.call-start = ((), (), s32[]{:S(2)}) async-start(), calls=%async_computation.2 | async-start | bytes 4718592 | tf_op jit(solution)/shard_map/all_gather | solution.py:58
  41.9 159.3 %reduce-scatter.2.cloned.1.call-start = ((), (), s32[]{:S(2)}) async-start(), calls=%async_computation.4 | async-start | bytes 1572864 | tf_op jit(solution)/shard_map/reduce_scatter | solution.py:84
  42.3 90.1 %copy-start.2 = (s32[4,128]{1,0:T(4,128)S(1)}, s32[4,128]{1,0:T(4,128)}, u32[]{:S(2)}) copy-start(s32[4,128]{1,0:T(4,128)} %constant.318.clone.2) | copy-start | bytes 6148
  138.8 1.9 copy-start
  142.2 1.1 copy-start.1
  149.6 1.9 copy-start
  153.0 1.1 copy-start.1
  160.4 1.9 copy-start
  163.8 1.1 copy-start.1
  171.2 1.9 copy-start
  174.6 1.1 copy-start.1
Sparse Core Ops, SparseCore 0:
  8.9 23.9 all-gather.3
  37.7 47.0 all-gather.7
  86.5 45.9 all-gather.5
  182.2 19.0 reduce-scatter.1
where the time goes:
time: 208 us
  waiting for transfers between devices  131 us (63%)
  matrix products  29.6 us (14%)
  local copies, waits for them, and re-layouts  22.8 us (11%)
  between operations  13.2 us (6%)
  other arithmetic  10.6 us (5%)
    all_gather x1, waiting for transfers between devices, shards(): lax.all_gather(keys_flat, ('views', 'sub'), axis=0, tiled=True)  47.6 us
    all_gather x1, waiting for transfers between devices, shards(): lax.all_gather(values_flat, ('views', 'sub'), axis=0, tiled=True)  38 us
    all_gather x1, waiting for transfers between devices, shards(): piece = lax.all_gather(tokens, 'heads', axis=1, tiled=True)  25.6 us
    reduce_scatter x1, waiting for transfers between devices, shards(): lax.psum_scatter(partial_sum.astype(jnp.bfloat16), 'heads', scatter_dimen...  19.2 us
    dot_general x3, matrix products, shards(): jnp.dot(piece, weight, preferred_element_type=jnp.float32)  12.4 us
    dynamic_slice x8, local copies, waits for them, and re-layouts, inner(): lax.dynamic_slice_in_dim(pieces[1], index * block * L, block * L, 0)  9.07 us
    while x4, matrix products  6.92 us
    dot_general x4, matrix products, absorb(): jnp.einsum('ahqk,khd->ahqd', rounded, values, preferred_element_type=jnp....  5.88 us
  transfers between devices with their start and end apart: 4, of which 4 were waited for; matrix products, arithmetic and copies ran while one was open for 4% of the time, Pallas kernels for 0%

commit v1 on v0

v1 whole, which is shorter than its diff:
```python
import functools

import jax
import jax.numpy as jnp
from jax import lax
from jax.experimental import pallas as pl
from jax.experimental.pallas import tpu as pltpu
from jax.sharding import PartitionSpec as P

HD = 128
L = 64
EDGE = 2
MB = 1 << 20


def project_kernel(pieces, side_ref, *refs):
    token_refs, refs = refs[:pieces], refs[pieces:]
    count = len(refs) // 2
    depth = token_refs[0].shape[1]
    for weight_ref, out_ref in zip(refs[:count], refs[count:]):
        total = None
        for step, token_ref in enumerate(token_refs):
            place = lax.rem(side_ref[0] + pieces - step, pieces)
            rows = pl.ds(pl.multiple_of(place * depth, depth), depth)
            term = jnp.dot(token_ref[...], weight_ref[rows, :], preferred_element_type=jnp.float32)
            total = term if total is None else total + term
        out_ref[...] = total.astype(out_ref.dtype)


def project(side, tokens, weights):
    rows, part = tokens[0].shape
    depth, width = weights[0].shape
    tile = min(256, width)
    count = len(weights)
    pieces = len(tokens)
    whole = pl.BlockSpec((rows, part), lambda j, s: (0, 0))
    return pl.pallas_call(
        functools.partial(project_kernel, pieces),
        out_shape=[jax.ShapeDtypeStruct((rows, width), jnp.bfloat16)] * count,
        grid_spec=pltpu.PrefetchScalarGridSpec(
            num_scalar_prefetch=1,
            grid=(width // tile,),
            in_specs=[whole] * pieces
            + [pl.BlockSpec((depth, tile), lambda j, s: (0, j))] * count,
            out_specs=[pl.BlockSpec((rows, tile), lambda j, s: (0, j))] * count,
        ),
        compiler_params=pltpu.CompilerParams(vmem_limit_bytes=24 * MB),
        cost_estimate=pl.CostEstimate(
            flops=2 * rows * depth * width * count,
            bytes_accessed=2 * depth * width * count + 4 * rows * depth,
            transcendentals=0,
        ),
        name="project",
    )(side, *tokens, *weights)


def attend_kernel(sizes, bias_ref, query_ref, *refs):
    count = len(sizes)
    key_refs, value_refs = refs[:count], refs[count : 2 * count]
    out_ref, scores_ref = refs[2 * count :]
    rows = query_ref.shape[0]
    views = rows // L
    query = query_ref[...]
    factor = HD ** (-0.5) * 1.4426950408889634
    top = None
    start = 0
    for key_ref, size in zip(key_refs, sizes):
        scores = lax.dot_general(
            query, key_ref[...], (((1,), (1,)), ((), ())), preferred_element_type=jnp.float32
        )
        scores = scores.reshape(views, L, size) + bias_ref[:, start : start + size][:, None, :]
        scores = scores.reshape(rows, size)
        scores_ref[:, start : start + size] = scores
        for part in range(0, size, 128):
            piece = scores[:, part : part + 128]
            top = piece if top is None else jnp.maximum(top, piece)
        start += size
    top = jnp.max(top, axis=1, keepdims=True)
    total = jnp.zeros((rows, 128), jnp.float32)
    mixed = jnp.zeros((rows, HD), jnp.float32)
    start = 0
    for value_ref, size in zip(value_refs, sizes):
        weights = jnp.exp2((scores_ref[:, start : start + size] - top) * factor)
        for part in range(0, size, 128):
            total += weights[:, part : part + 128]
        mixed += jnp.dot(
            weights.astype(jnp.bfloat16), value_ref[...], preferred_element_type=jnp.float32
        )
        start += size
    out_ref[...] = (mixed / jnp.sum(total, axis=1, keepdims=True)).astype(out_ref.dtype)


def attend(bias, query, pairs):
    rows, width = query.shape
    sizes = tuple(keys.shape[0] for keys, _ in pairs)
    span = sum(sizes)
    heads = width // HD
    column = lambda size: pl.BlockSpec((size, HD), lambda h: (0, h))
    return pl.pallas_call(
        functools.partial(attend_kernel, sizes),
        out_shape=jax.ShapeDtypeStruct((rows, width), jnp.bfloat16),
        grid=(heads,),
        in_specs=[pl.BlockSpec(bias.shape, lambda h: (0, 0)), column(rows)]
        + [column(size) for size in sizes] * 2,
        out_specs=column(rows),
        scratch_shapes=[pltpu.VMEM((rows, span), jnp.float32)],
        compiler_params=pltpu.CompilerParams(vmem_limit_bytes=24 * MB),
        cost_estimate=pl.CostEstimate(
            flops=4 * rows * span * width,
            bytes_accessed=4 * span * width,
            transcendentals=rows * span * heads,
        ),
        name="attend",
    )(bias, query, *[keys for keys, _ in pairs], *[values for _, values in pairs])


def output_kernel(side_ref, mixed_ref, weight_ref, out_ref):
    out_ref[...] = jnp.dot(
        mixed_ref[...], weight_ref[...], preferred_element_type=jnp.float32
    ).astype(out_ref.dtype)


def output_part(place, sides, mixed, weight, dtype):
    rows, depth = mixed.shape
    part = weight.shape[1] // sides
    tile = min(256, part)
    steps = part // tile
    return pl.pallas_call(
        output_kernel,
        out_shape=jax.ShapeDtypeStruct((rows, part), dtype),
        grid_spec=pltpu.PrefetchScalarGridSpec(
            num_scalar_prefetch=1,
            grid=(steps,),
            in_specs=[
                pl.BlockSpec((rows, depth), lambda j, s: (0, 0)),
                pl.BlockSpec((depth, tile), lambda j, s: (0, s[0] * steps + j)),
            ],
            out_specs=pl.BlockSpec((rows, tile), lambda j, s: (0, j)),
        ),
        compiler_params=pltpu.CompilerParams(vmem_limit_bytes=24 * MB),
        cost_estimate=pl.CostEstimate(
            flops=2 * rows * depth * part, bytes_accessed=2 * depth * part, transcendentals=0
        ),
        name="output_part",
    )(place, mixed, weight)


def shards(tokens, w_query, w_key, w_value, w_out, partners, counts):
    rows = tokens.shape[0]
    views_here = rows // L
    chips = lax.axis_size("views")
    cores = lax.axis_size("sub")
    total_views = views_here * chips * cores
    place = lax.axis_index("views")
    core = lax.axis_index("sub")
    sides = lax.axis_size("heads")
    side = lax.axis_index("heads").astype(jnp.int32).reshape(1)

    def shift(a, step):
        return lax.ppermute(a, "heads", [(h, (h + step) % sides) for h in range(sides)])

    def gather(a):
        return [a] + [shift(a, step) for step in range(1, sides)]

    share = lambda a: lax.ppermute(a, "sub", [(0, 1), (1, 0)])
    pair = [(z, z ^ 1) for z in range(chips)]
    side_step = [(z, ((z - 1) if z % 2 == 0 else (z + 1)) % chips) for z in range(chips)]
    edge = [(2 * z + 1, 2 * ((z + 2) % chips)) for z in range(chips)]
    edge += [(2 * z, 2 * ((z - 2) % chips) + 1) for z in range(chips)]

    edge_rows = EDGE * L
    first = lax.slice_in_dim(tokens, 0, edge_rows, axis=0)
    last = lax.slice_in_dim(tokens, rows - edge_rows, rows, axis=0)
    own_pieces = gather(tokens)
    near = lax.ppermute(tokens, "views", pair)
    next_near = lax.ppermute(tokens, "views", side_step)
    rim = lax.ppermute(jnp.where(core == 0, first, last), ("views", "sub"), edge)

    query, own_keys, own_values = project(side, own_pieces, (w_query, w_key, w_value))
    own = (own_keys, own_values)
    near_kv = project(side, gather(near), (w_key, w_value))
    next_kv = project(side, gather(next_near), (w_key, w_value))
    rim_kv = project(side, gather(rim), (w_key, w_value))

    pairs = []
    bases = []
    even = place % 2 == 0
    near_place = place ^ 1
    next_place = jnp.where(even, place - 1, place + 1) % chips
    for kv, at in ((own, place), (near_kv, near_place), (next_kv, next_place)):
        pairs.append(tuple(kv))
        bases.append((at * cores + core) * views_here + jnp.arange(views_here, dtype=jnp.int32))
        pairs.append(tuple(share(a) for a in kv))
        bases.append((at * cores + 1 - core) * views_here + jnp.arange(views_here, dtype=jnp.int32))
    pairs.append(tuple(rim_kv))
    far_first = jnp.where(
        core == 0,
        ((place - 2) * cores + 1) * views_here + views_here - EDGE,
        (place + 2) * cores * views_here,
    )
    bases.append((far_first + jnp.arange(EDGE, dtype=jnp.int32)) % total_views)
    listed = jnp.concatenate(bases)

    mine = (place * cores + core) * views_here + jnp.arange(views_here, dtype=jnp.int32)
    slots = jnp.arange(partners.shape[1], dtype=jnp.int32)
    valid = slots[None, :] < counts[:, None]
    allowed = jnp.any(
        valid[:, :, None] & (partners[:, :, None] == listed[None, None, :]), axis=1
    ) | (mine[:, None] == listed[None, :])
    bias = jnp.repeat(jnp.where(allowed, 0.0, -1e30).astype(jnp.float32), L, axis=1)

    mixed = attend(bias, query, pairs)
    total = None
    for step in range(1, sides):
        sent = output_part((side + step) % sides, sides, mixed, w_out, jnp.bfloat16)
        term = shift(sent, step).astype(jnp.float32)
        total = term if total is None else total + term
    kept = output_part(side, sides, mixed, w_out, jnp.float32)
    return (kept + total).astype(jnp.bfloat16)


def solution(mesh):
    in_specs = (
        P(("groups", "views", "sub"), "heads"),
        P(None, "heads"),
        P(None, "heads"),
        P(None, "heads"),
        P("heads", None),
        P(("groups", "views", "sub"), None),
        P(("groups", "views", "sub")),
    )
    out_specs = P(("groups", "views", "sub"), "heads")
    return jax.shard_map(shards, mesh=mesh, in_specs=in_specs, out_specs=out_specs, check_vma=False)
```

time: 208 us -> 104 us (0.50)
  the two profiles are of different devices: /device:TPU:0 before, /device:TPU:16 now
where the time goes in v1:
time: 104 us; the launch traced here: 103 us
  waiting for transfers between devices  36.2 us (35%)
  Pallas kernels  34.1 us (33%)
  local copies, waits for them, and re-layouts  18.4 us (18%)
  starting transfers between devices  10.9 us (10%)
  other arithmetic  3.58 us (3%)
    pallas_call x4, Pallas kernels, project(): pl.pallas_call(functools.partial(project_kernel, pieces), out_shape=[jax....  20 us
    unnamed x25, local copies, waits for them, and re-layouts  18.1 us
    ppermute x1, waiting for transfers between devices, shards(): next_near = lax.ppermute(tokens, 'views', side_step)  17 us
    ppermute x5, waiting for transfers between devices, shift(): lax.ppermute(a, 'heads', [(h, (h + step) % sides) for h in range(sides)])  11.1 us
    pallas_call x1, Pallas kernels, attend(): pl.pallas_call(functools.partial(attend_kernel, sizes), out_shape=jax.Sha...  10.8 us
    ppermute x1, waiting for transfers between devices, shards(): near = lax.ppermute(tokens, 'views', pair)  8.11 us
    ppermute x5, starting transfers between devices, shift(): lax.ppermute(a, 'heads', [(h, (h + step) % sides) for h in range(sides)])  6.62 us
    pallas_call x2, Pallas kernels, output_part(): pl.pallas_call(output_kernel, out_shape=jax.ShapeDtypeStruct((rows, part)...  3.31 us
  transfers between devices with their start and end apart: 14, of which 3 were waited for; matrix products, arithmetic and copies ran while one was open for 3% of the time, Pallas kernels for 21%

profile of v1, /device:TPU:16, one launch (start us, length us, event | category | flops | bytes accessed | tf_op | source)
XLA Modules:
  0.0 103.3 jit_solution(3069719216925245231)
XLA Ops:
  0.0 1.6 %collective-permute-start.2 = (bf16[256,1024]{1,0:T(8,128)(2,1)}, bf16[256,1024]{1,0:T(8,128)(2,1)S(1)}, u32[]{:S(2)}, u32[]{:S(2)}) collective-permute-start(bf16[256,1024]{1,0:T(8,128)(2,1)} %refs_0_.1), channel_id=1, source_target_pairs={{0,4},{4,0},{8,12},{12,8},{1,5},{5,1},{9,13},{13,9},{2,6},{6,2},{1... | collective-permute-start | bytes 1572872 | tf_op jit(solution)/shard_map/ppermute | solution.py:175
  1.6 1.5 %collective-permute-start = (bf16[256,1024]{1,0:T(8,128)(2,1)}, bf16[256,1024]{1,0:T(8,128)(2,1)S(1)}, u32[]{:S(2)}, u32[]{:S(2)}) collective-permute-start(bf16[256,1024]{1,0:T(8,128)(2,1)} %refs_0_.1), channel_id=1, source_target_pairs={{0,2},{2,0},{1,3},{3,1},{4,6},{6,4},{5,7},{7,5},{8,10},{10,8},{9,1... | collective-permute-start | bytes 1572872 | tf_op jit(solution)/shard_map/ppermute | solution.py:160
  3.1 1.8 %slice_select_fusion = bf16[128,1024]{1,0:T(8,128)(2,1)} fusion(bf16[256,1024]{1,0:T(8,128)(2,1)} %refs_0_.1, pred[]{:T(512)S(6)} %eq.42), kind=kLoop, calls=%fused_computation.1 | loop fusion | flops 131072 | bytes 786433 | tf_op jit(solution)/shard_map/jit(_where)/select_n | solution.py:177
  4.8 1.4 %collective-permute-start.8 = (bf16[128,1024]{1,0:T(8,128)(2,1)}, bf16[128,1024]{1,0:T(8,128)(2,1)S(1)}, u32[]{:S(2)}, u32[]{:S(2)}) collective-permute-start(bf16[128,1024]{1,0:T(8,128)(2,1)} %slice_select_fusion), channel_id=1, source_target_pairs={{1,8},{5,12},{9,0},{13,4},{0,9},{4,13},{8,1},{12,5},{3,10},{7,14},... | collective-permute-start | bytes 786440 | tf_op jit(solution)/shard_map/ppermute | solution.py:177
  6.2 0.7 iota_compare_fusion
  6.9 8.1 %collective-permute-done.2.refs_0_ = bf16[256,1024]{1,0:T(8,128)(2,1)S(1)} collective-permute-done((bf16[256,1024]{1,0:T(8,128)(2,1)}, bf16[256,1024]{1,0:T(8,128)(2,1)S(1)}, u32[]{:S(2)}, u32[]{:S(2)}) %collective-permute-start.2) | collective-permute-done | bytes 524320 | tf_op jit(solution)/shard_map/ppermute | solution.py:175
  15.0 1.5 %collective-permute-start.3 = (bf16[256,1024]{1,0:T(8,128)(2,1)S(1)}, bf16[256,1024]{1,0:T(8,128)(2,1)}, u32[]{:S(2)}, u32[]{:S(2)}) collective-permute-start(bf16[256,1024]{1,0:T(8,128)(2,1)S(1)} %collective-permute-done.2.refs_0_), channel_id=1, source_target_pairs={{0,2},{2,0},{1,3},{3,1},{4,6},{6,4},{5,7},{7,5},{8,10},{10,8},{9,1... | collective-permute-start | bytes 1572872 | tf_op jit(solution)/shard_map/ppermute | solution.py:160
  16.5 17.0 %collective-permute-done.5.refs_0_ = bf16[256,1024]{1,0:T(8,128)(2,1)S(1)} collective-permute-done((bf16[256,1024]{1,0:T(8,128)(2,1)}, bf16[256,1024]{1,0:T(8,128)(2,1)S(1)}, u32[]{:S(2)}, u32[]{:S(2)}) %collective-permute-start.5) | collective-permute-done | bytes 524320 | tf_op jit(solution)/shard_map/ppermute | solution.py:176
  33.5 1.5 %collective-permute-start.6 = (bf16[256,1024]{1,0:T(8,128)(2,1)S(1)}, bf16[256,1024]{1,0:T(8,128)(2,1)}, u32[]{:S(2)}, u32[]{:S(2)}) collective-permute-start(bf16[256,1024]{1,0:T(8,128)(2,1)S(1)} %collective-permute-done.5.refs_0_), channel_id=1, source_target_pairs={{0,2},{2,0},{1,3},{3,1},{4,6},{6,4},{5,7},{7,5},{8,10},{10,8},{9,1... | collective-permute-start | bytes 1572872 | tf_op jit(solution)/shard_map/ppermute | solution.py:160
  35.0 0.0 collective-permute-done.refs_1_
  35.0 2.2 %copy-done = bf16[2048,1024]{1,0:T(8,128)(2,1)S(1)} copy-done((bf16[2048,1024]{1,0:T(8,128)(2,1)S(1)}, bf16[2048,1024]{1,0:T(8,128)(2,1)}, u32[]{:S(2)}) %copy-start) | copy-done | bytes 4194328
  37.2 2.2 %copy-done.3 = bf16[2048,1024]{1,0:T(8,128)(2,1)S(1)} copy-done((bf16[2048,1024]{1,0:T(8,128)(2,1)S(1)}, bf16[2048,1024]{1,0:T(8,128)(2,1)}, u32[]{:S(2)}) %copy-start.3) | copy-done | bytes 4194328
  39.4 2.2 %copy-done.7 = bf16[2048,1024]{1,0:T(8,128)(2,1)S(1)} copy-done((bf16[2048,1024]{1,0:T(8,128)(2,1)S(1)}, bf16[2048,1024]{1,0:T(8,128)(2,1)}, u32[]{:S(2)}) %copy-start.7) | copy-done | bytes 4194328
  41.6 1.0 %copy-done.8 = bf16[256,1024]{1,0:T(8,128)(2,1)S(1)} copy-done((bf16[256,1024]{1,0:T(8,128)(2,1)S(1)}, bf16[256,1024]{1,0:T(8,128)(2,1)}, u32[]{:S(2)}) %copy-start.8) | copy-done | bytes 524312
  42.6 5.9 %project.4 = (bf16[256,1024]{1,0:T(8,128)(2,1)S(1)}, bf16[256,1024]{1,0:T(8,128)(2,1)S(1)}, bf16[256,1024]{1,0:T(8,128)(2,1)S(1)}) custom-call(s32[1]{0:T(128)} %bitcast.side_ref, bf16[256,1024]{1,0:T(8,128)(2,1)S(1)} %copy-done.8, bf16[256,1024]{1,0:T(8,128)(2,1)S(1)} %collective-permute-done.refs_1_, bf16[2048,1024]{1,0:T(8,128)(2,1)S(1)} %copy-done.7, ...), custom_call_target="tpu_custom_call" | custom-call | flops 3221225472 | bytes 14680064 | tf_op jit(solution)/shard_map/project/pallas_call | solution.py:37
  48.5 0.1 collective-permute-start.1
  48.6 0.1 copy.8
  48.7 0.0 collective-permute-done.8.refs_0_
  48.7 0.6 collective-permute-start.9
  49.3 0.2 collective-permute-start.10
  49.5 2.2 %copy-done.1 = bf16[2048,1024]{1,0:T(8,128)(2,1)S(1)} copy-done((bf16[2048,1024]{1,0:T(8,128)(2,1)S(1)}, bf16[2048,1024]{1,0:T(8,128)(2,1)}, u32[]{:S(2)}) %copy-start.1) | copy-done | bytes 4194328
  51.7 2.2 %copy-done.4 = bf16[2048,1024]{1,0:T(8,128)(2,1)S(1)} copy-done((bf16[2048,1024]{1,0:T(8,128)(2,1)S(1)}, bf16[2048,1024]{1,0:T(8,128)(2,1)}, u32[]{:S(2)}) %copy-start.4) | copy-done | bytes 4194328
  53.9 5.5 %project.5 = (bf16[256,1024]{1,0:T(8,128)(2,1)}, bf16[256,1024]{1,0:T(8,128)(2,1)}) custom-call(s32[1]{0:T(128)} %bitcast.side_ref, bf16[256,1024]{1,0:T(8,128)(2,1)S(1)} %collective-permute-done.2.refs_0_, bf16[256,1024]{1,0:T(8,128)(2,1)} %collective-permute-done.3.refs_1_, bf16[2048,1024]{1,0:T(8,128)(2,1)S(1)} %copy-done.1, bf16[2048,1024]{1,0:T(8,128)(2,1)S(1)} %copy-done.4), custom_call_target="tpu_custom_call" | custom-call | flops 2147483648 | bytes 10485760 | tf_op jit(solution)/shard_map/project/pallas_call | solution.py:37
  59.4 0.3 collective-permute-start.11
  59.7 0.0 collective-permute-done.6.refs_1_
  59.7 5.5 %project.6 = (bf16[256,1024]{1,0:T(8,128)(2,1)}, bf16[256,1024]{1,0:T(8,128)(2,1)}) custom-call(s32[1]{0:T(128)} %bitcast.side_ref, bf16[256,1024]{1,0:T(8,128)(2,1)S(1)} %collective-permute-done.5.refs_0_, bf16[256,1024]{1,0:T(8,128)(2,1)} %collective-permute-done.6.refs_1_, bf16[2048,1024]{1,0:T(8,128)(2,1)S(1)} %copy-done.1, bf16[2048,1024]{1,0:T(8,128)(2,1)S(1)} %copy-done.4), custom_call_target="tpu_custom_call" | custom-call | flops 2147483648 | bytes 10485760 | tf_op jit(solution)/shard_map/project/pallas_call | solution.py:37
  65.2 0.2 collective-permute-start.12
  65.4 0.0 collective-permute-done.9.refs_1_
  65.4 0.7 copy-done.9
  66.1 0.3 collective-permute-start.4
  66.5 0.2 collective-permute-start.7
  66.7 0.1 concatenate.3
  66.7 0.1 and_reduce_fusion
  66.9 0.1 or_select_fusion
  66.9 0.1 broadcast_in_dim.20
  67.0 0.1 reshape.37.bias_ref
  67.1 0.0 copy-start.2
  67.1 2.2 %copy-done.2 = bf16[2048,1024]{1,0:T(8,128)(2,1)S(1)} copy-done((bf16[2048,1024]{1,0:T(8,128)(2,1)S(1)}, bf16[2048,1024]{1,0:T(8,128)(2,1)}, u32[]{:S(2)}) %copy-start.2) | copy-done | bytes 4194328
  69.3 2.2 %copy-done.5 = bf16[2048,1024]{1,0:T(8,128)(2,1)S(1)} copy-done((bf16[2048,1024]{1,0:T(8,128)(2,1)S(1)}, bf16[2048,1024]{1,0:T(8,128)(2,1)}, u32[]{:S(2)}) %copy-start.5) | copy-done | bytes 4194328
  71.5 0.9 copy-done.10
  72.5 3.1 %project.7 = (bf16[128,1024]{1,0:T(8,128)(2,1)S(1)}, bf16[128,1024]{1,0:T(8,128)(2,1)S(1)}) custom-call(s32[1]{0:T(128)} %bitcast.side_ref, bf16[128,1024]{1,0:T(8,128)(2,1)S(1)} %collective-permute-done.8.refs_0_, bf16[128,1024]{1,0:T(8,128)(2,1)S(1)} %copy-done.10, bf16[2048,1024]{1,0:T(8,128)(2,1)S(1)} %copy-done.2, bf16[2048,1024]{1,0:T(8,128)(2,1)S(1)} %copy-done.5), custom_call_target="tpu_custom_call" | custom-call | flops 1073741824 | bytes 9437184 | tf_op jit(solution)/shard_map/project/pallas_call | solution.py:37
  75.5 0.0 copy-start.6
  75.6 10.8 %attend.1.mixed_ref = bf16[256,1024]{1,0:T(8,128)(2,1)S(1)} custom-call(f32[4,1664]{1,0:T(4,128)S(1)} %reshape.37.bias_ref, bf16[256,1024]{1,0:T(8,128)(2,1)S(1)} %get-tuple-element.14.query_ref, bf16[256,1024]{1,0:T(8,128)(2,1)S(1)} %get-tuple-element.15.refs_0_, bf16[256,1024]{1,0:T(8,128)(2,1)S(1)} %collective-permute-done.1.refs_1_, ...), custom_call_target="tpu_custom_call" | custom-call | flops 1744830464 | bytes 6815744 | tf_op jit(solution)/shard_map/attend/pallas_call | solution.py:99
  86.4 1.7 %output_part.3 = bf16[256,1024]{1,0:T(8,128)(2,1)S(1)} custom-call(s32[1]{0:T(128)S(6)} %select_n.49.side_ref, bf16[256,1024]{1,0:T(8,128)(2,1)S(1)} %attend.1.mixed_ref, bf16[1024,2048]{1,0:T(8,128)(2,1)S(1)} %copy-done.6), custom_call_target="tpu_custom_call" | custom-call | flops 536870912 | bytes 2097152 | tf_op jit(solution)/shard_map/output_part/pallas_call | solution.py:128
  88.1 1.5 %collective-permute-start.13 = (bf16[256,1024]{1,0:T(8,128)(2,1)S(1)}, bf16[256,1024]{1,0:T(8,128)(2,1)S(1)}, u32[]{:S(2)}, u32[]{:S(2)}) collective-permute-start(bf16[256,1024]{1,0:T(8,128)(2,1)S(1)} %output_part.3), channel_id=1, source_target_pairs={{0,2},{2,0},{1,3},{3,1},{4,6},{6,4},{5,7},{7,5},{8,10},{10,8},{9,1... | collective-permute-start | bytes 1572872 | tf_op jit(solution)/shard_map/ppermute | solution.py:160
  89.7 1.6 %output_part.2 = f32[256,1024]{1,0:T(8,128)S(1)} custom-call(s32[1]{0:T(128)} %bitcast.side_ref, bf16[256,1024]{1,0:T(8,128)(2,1)S(1)} %attend.1.mixed_ref, bf16[1024,2048]{1,0:T(8,128)(2,1)S(1)} %copy-done.6), custom_call_target="tpu_custom_call" | custom-call | flops 536870912 | bytes 2097152 | tf_op jit(solution)/shard_map/output_part/pallas_call | solution.py:128
  91.3 11.0 %collective-permute-done.13 = bf16[256,1024]{1,0:T(8,128)(2,1)S(1)} collective-permute-done((bf16[256,1024]{1,0:T(8,128)(2,1)S(1)}, bf16[256,1024]{1,0:T(8,128)(2,1)S(1)}, u32[]{:S(2)}, u32[]{:S(2)}) %collective-permute-start.13) | collective-permute-done | bytes 524320 | tf_op jit(solution)/shard_map/ppermute | solution.py:160
  102.4 0.9 add_convert_fusion
  (24 shorter events, 0.1 us)
Async XLA Ops:
  0.0 15.0 %collective-permute-start.2 = (bf16[256,1024]{1,0:T(8,128)(2,1)}, bf16[256,1024]{1,0:T(8,128)(2,1)S(1)}, u32[]{:S(2)}, u32[]{:S(2)}) collective-permute-start(bf16[256,1024]{1,0:T(8,128)(2,1)} %refs_0_.1), channel_id=1, source_target_pairs={{0,4},{4,0},{8,12},{12,8},{1,5},{5,1},{9,13},{13,9},{2,6},{6,2},{1... | collective-permute-start | bytes 1572872 | tf_op jit(solution)/shard_map/ppermute | solution.py:175
  1.6 31.9 %collective-permute-start.5 = (bf16[256,1024]{1,0:T(8,128)(2,1)}, bf16[256,1024]{1,0:T(8,128)(2,1)S(1)}, u32[]{:S(2)}, u32[]{:S(2)}) collective-permute-start(bf16[256,1024]{1,0:T(8,128)(2,1)} %refs_0_.1), channel_id=1, source_target_pairs={{0,12},{4,8},{8,4},{12,0},{1,13},{5,9},{9,5},{13,1},{2,14},{6,10},... | collective-permute-start | bytes 1572872 | tf_op jit(solution)/shard_map/ppermute | solution.py:176
  1.6 33.4 %collective-permute-start = (bf16[256,1024]{1,0:T(8,128)(2,1)}, bf16[256,1024]{1,0:T(8,128)(2,1)S(1)}, u32[]{:S(2)}, u32[]{:S(2)}) collective-permute-start(bf16[256,1024]{1,0:T(8,128)(2,1)} %refs_0_.1), channel_id=1, source_target_pairs={{0,2},{2,0},{1,3},{3,1},{4,6},{6,4},{5,7},{7,5},{8,10},{10,8},{9,1... | collective-permute-start | bytes 1572872 | tf_op jit(solution)/shard_map/ppermute | solution.py:160
  4.8 43.9 %collective-permute-start.8 = (bf16[128,1024]{1,0:T(8,128)(2,1)}, bf16[128,1024]{1,0:T(8,128)(2,1)S(1)}, u32[]{:S(2)}, u32[]{:S(2)}) collective-permute-start(bf16[128,1024]{1,0:T(8,128)(2,1)} %slice_select_fusion), channel_id=1, source_target_pairs={{1,8},{5,12},{9,0},{13,4},{0,9},{4,13},{8,1},{12,5},{3,10},{7,14},... | collective-permute-start | bytes 786440 | tf_op jit(solution)/shard_map/ppermute | solution.py:177
  15.0 34.5 %collective-permute-start.3 = (bf16[256,1024]{1,0:T(8,128)(2,1)S(1)}, bf16[256,1024]{1,0:T(8,128)(2,1)}, u32[]{:S(2)}, u32[]{:S(2)}) collective-permute-start(bf16[256,1024]{1,0:T(8,128)(2,1)S(1)} %collective-permute-done.2.refs_0_), channel_id=1, source_target_pairs={{0,2},{2,0},{1,3},{3,1},{4,6},{6,4},{5,7},{7,5},{8,10},{10,8},{9,1... | collective-permute-start | bytes 1572872 | tf_op jit(solution)/shard_map/ppermute | solution.py:160
  33.5 26.2 %collective-permute-start.6 = (bf16[256,1024]{1,0:T(8,128)(2,1)S(1)}, bf16[256,1024]{1,0:T(8,128)(2,1)}, u32[]{:S(2)}, u32[]{:S(2)}) collective-permute-start(bf16[256,1024]{1,0:T(8,128)(2,1)S(1)} %collective-permute-done.5.refs_0_), channel_id=1, source_target_pairs={{0,2},{2,0},{1,3},{3,1},{4,6},{6,4},{5,7},{7,5},{8,10},{10,8},{9,1... | collective-permute-start | bytes 1572872 | tf_op jit(solution)/shard_map/ppermute | solution.py:160
  35.0 2.2 %copy-start = (bf16[2048,1024]{1,0:T(8,128)(2,1)S(1)}, bf16[2048,1024]{1,0:T(8,128)(2,1)}, u32[]{:S(2)}) copy-start(bf16[2048,1024]{1,0:T(8,128)(2,1)} %refs_2_.7) | copy-start | bytes 12582916
  37.2 2.2 %copy-start.3 = (bf16[2048,1024]{1,0:T(8,128)(2,1)S(1)}, bf16[2048,1024]{1,0:T(8,128)(2,1)}, u32[]{:S(2)}) copy-start(bf16[2048,1024]{1,0:T(8,128)(2,1)} %refs_3_.7) | copy-start | bytes 12582916
  39.4 2.2 %copy-start.7 = (bf16[2048,1024]{1,0:T(8,128)(2,1)S(1)}, bf16[2048,1024]{1,0:T(8,128)(2,1)}, u32[]{:S(2)}) copy-start(bf16[2048,1024]{1,0:T(8,128)(2,1)} %refs_2_.4) | copy-start | bytes 12582916
  41.6 1.0 %copy-start.8 = (bf16[256,1024]{1,0:T(8,128)(2,1)S(1)}, bf16[256,1024]{1,0:T(8,128)(2,1)}, u32[]{:S(2)}) copy-start(bf16[256,1024]{1,0:T(8,128)(2,1)} %refs_0_.1) | copy-start | bytes 1572868
  42.6 6.0 %copy-start.11 = (s32[4,20]{1,0:T(4,128)S(1)}, s32[4,20]{1,0:T(4,128)}, u32[]{:S(2)}) copy-start(s32[4,20]{1,0:T(4,128)} %param.12) | copy-start | bytes 964
  48.5 18.0 %collective-permute-start.1 = (bf16[256,1024]{1,0:T(8,128)(2,1)S(1)}, bf16[256,1024]{1,0:T(8,128)(2,1)S(1)}, u32[]{:S(2)}, u32[]{:S(2)}) collective-permute-start(bf16[256,1024]{1,0:T(8,128)(2,1)S(1)} %get-tuple-element.15.refs_0_), channel_id=1, source_target_pairs={{0,1},{1,0},{2,3},{3,2},{4,5},{5,4},{6,7},{7,6},{8,9},{9,8},{10,11... | collective-permute-start | bytes 1572872 | tf_op jit(solution)/shard_map/ppermute | solution.py:165
  48.7 16.7 %collective-permute-start.9 = (bf16[128,1024]{1,0:T(8,128)(2,1)S(1)}, bf16[128,1024]{1,0:T(8,128)(2,1)S(1)}, u32[]{:S(2)}, u32[]{:S(2)}) collective-permute-start(bf16[128,1024]{1,0:T(8,128)(2,1)S(1)} %collective-permute-done.8.refs_0_), channel_id=1, source_target_pairs={{0,2},{2,0},{1,3},{3,1},{4,6},{6,4},{5,7},{7,5},{8,10},{10,8},{9,1... | collective-permute-start | bytes 786440 | tf_op jit(solution)/shard_map/ppermute | solution.py:160
  49.3 26.2 %collective-permute-start.10 = (bf16[256,1024]{1,0:T(8,128)(2,1)S(1)}, bf16[256,1024]{1,0:T(8,128)(2,1)}, u32[]{:S(2)}, u32[]{:S(2)}) collective-permute-start(bf16[256,1024]{1,0:T(8,128)(2,1)S(1)} %get-tuple-element.19.refs_7_), channel_id=1, source_target_pairs={{0,1},{1,0},{2,3},{3,2},{4,5},{5,4},{6,7},{7,6},{8,9},{9,8},{10,11... | collective-permute-start | bytes 1572872 | tf_op jit(solution)/shard_map/ppermute | solution.py:165
  49.5 2.2 %copy-start.1 = (bf16[2048,1024]{1,0:T(8,128)(2,1)S(1)}, bf16[2048,1024]{1,0:T(8,128)(2,1)}, u32[]{:S(2)}) copy-start(bf16[2048,1024]{1,0:T(8,128)(2,1)} %refs_2_.7) | copy-start | bytes 12582916
  51.7 2.2 %copy-start.4 = (bf16[2048,1024]{1,0:T(8,128)(2,1)S(1)}, bf16[2048,1024]{1,0:T(8,128)(2,1)}, u32[]{:S(2)}) copy-start(bf16[2048,1024]{1,0:T(8,128)(2,1)} %refs_3_.7) | copy-start | bytes 12582916
  59.4 16.2 %collective-permute-start.11 = (bf16[256,1024]{1,0:T(8,128)(2,1)}, bf16[256,1024]{1,0:T(8,128)(2,1)S(1)}, u32[]{:S(2)}, u32[]{:S(2)}) collective-permute-start(bf16[256,1024]{1,0:T(8,128)(2,1)} %get-tuple-element.20.refs_9_), channel_id=1, source_target_pairs={{0,1},{1,0},{2,3},{3,2},{4,5},{5,4},{6,7},{7,6},{8,9},{9,8},{10,11... | collective-permute-start | bytes 1572872 | tf_op jit(solution)/shard_map/ppermute | solution.py:165
  65.2 10.3 %collective-permute-start.12 = (bf16[256,1024]{1,0:T(8,128)(2,1)}, bf16[256,1024]{1,0:T(8,128)(2,1)S(1)}, u32[]{:S(2)}, u32[]{:S(2)}) collective-permute-start(bf16[256,1024]{1,0:T(8,128)(2,1)} %get-tuple-element.21.refs_11_), channel_id=1, source_target_pairs={{0,1},{1,0},{2,3},{3,2},{4,5},{5,4},{6,7},{7,6},{8,9},{9,8},{10,11... | collective-permute-start | bytes 1572872 | tf_op jit(solution)/shard_map/ppermute | solution.py:165
  65.4 0.7 copy-start.9
  66.1 9.4 %collective-permute-start.4 = (bf16[256,1024]{1,0:T(8,128)(2,1)}, bf16[256,1024]{1,0:T(8,128)(2,1)}, u32[]{:S(2)}, u32[]{:S(2)}) collective-permute-start(bf16[256,1024]{1,0:T(8,128)(2,1)} %get-tuple-element.16.refs_2_), channel_id=1, source_target_pairs={{0,1},{1,0},{2,3},{3,2},{4,5},{5,4},{6,7},{7,6},{8,9},{9,8},{10,11... | collective-permute-start | bytes 1572872 | tf_op jit(solution)/shard_map/ppermute | solution.py:165
  66.5 9.1 %collective-permute-start.7 = (bf16[256,1024]{1,0:T(8,128)(2,1)}, bf16[256,1024]{1,0:T(8,128)(2,1)}, u32[]{:S(2)}, u32[]{:S(2)}) collective-permute-start(bf16[256,1024]{1,0:T(8,128)(2,1)} %get-tuple-element.17.refs_4_), channel_id=1, source_target_pairs={{0,1},{1,0},{2,3},{3,2},{4,5},{5,4},{6,7},{7,6},{8,9},{9,8},{10,11... | collective-permute-start | bytes 1572872 | tf_op jit(solution)/shard_map/ppermute | solution.py:165
  67.1 2.2 %copy-start.2 = (bf16[2048,1024]{1,0:T(8,128)(2,1)S(1)}, bf16[2048,1024]{1,0:T(8,128)(2,1)}, u32[]{:S(2)}) copy-start(bf16[2048,1024]{1,0:T(8,128)(2,1)} %refs_2_.7) | copy-start | bytes 12582916
  69.3 2.2 %copy-start.5 = (bf16[2048,1024]{1,0:T(8,128)(2,1)S(1)}, bf16[2048,1024]{1,0:T(8,128)(2,1)}, u32[]{:S(2)}) copy-start(bf16[2048,1024]{1,0:T(8,128)(2,1)} %refs_3_.7) | copy-start | bytes 12582916
  71.5 0.9 copy-start.10
  75.5 10.9 %copy-start.6 = (bf16[1024,2048]{1,0:T(8,128)(2,1)S(1)}, bf16[1024,2048]{1,0:T(8,128)(2,1)}, u32[]{:S(2)}) copy-start(bf16[1024,2048]{1,0:T(8,128)(2,1)} %weight_ref.3) | copy-start | bytes 12582916
  88.1 14.2 %collective-permute-start.13 = (bf16[256,1024]{1,0:T(8,128)(2,1)S(1)}, bf16[256,1024]{1,0:T(8,128)(2,1)S(1)}, u32[]{:S(2)}, u32[]{:S(2)}) collective-permute-start(bf16[256,1024]{1,0:T(8,128)(2,1)S(1)} %output_part.3), channel_id=1, source_target_pairs={{0,2},{2,0},{1,3},{3,1},{4,6},{6,4},{5,7},{7,5},{8,10},{10,8},{9,1... | collective-permute-start | bytes 1572872 | tf_op jit(solution)/shard_map/ppermute | solution.py:160

commit v2 on v0

v2 whole, which is shorter than its diff:
```python
import functools

import jax
import jax.numpy as jnp
from jax import lax
from jax.experimental import pallas as pl
from jax.experimental.pallas import tpu as pltpu
from jax.sharding import PartitionSpec as P

HD = 128
L = 64
EDGE = 2
MB = 1 << 20
FACTOR = HD ** (-0.5) * 1.4426950408889634
ROWS_BY_ROWS = (((1,), (1,)), ((), ()))

VMEM = pl.BlockSpec(memory_space=pltpu.VMEM)
SMEM = pl.BlockSpec(memory_space=pltpu.SMEM)
HBM = pl.BlockSpec(memory_space=pl.ANY)
PLACE, CORE, SIDE = range(3)


def call(kernel, outs, ins, scratch=(), name=None, out_specs=None, aliases=None, whole=()):
    return pl.pallas_call(
        kernel,
        out_shape=outs,
        in_specs=[
            HBM if k in whole else SMEM if a.dtype == jnp.int32 and a.ndim == 1 else VMEM
            for k, a in enumerate(ins)
        ],
        out_specs=jax.tree.map(lambda _: VMEM, outs) if out_specs is None else out_specs,
        scratch_shapes=list(scratch),
        input_output_aliases=aliases or {},
        compiler_params=pltpu.CompilerParams(vmem_limit_bytes=16 * MB),
        cost_estimate=pl.CostEstimate(flops=0, bytes_accessed=0, transcendentals=0),
        name=name,
    )(*ins)


def after(a, *others):
    return lax.optimization_barrier((a, *others))[0]


def prepare_kernel(chips, cores, here_ref, counts_ref, partners_ref, *refs):
    w_query_ref, w_value_ref, w_key_ref, w_out_ref, turned_query_ref, turned_value_ref, bias_ref = refs
    step = 256
    for weight_ref, turned_ref in ((w_query_ref, turned_query_ref), (w_value_ref, turned_value_ref)):
        for start in range(0, weight_ref.shape[0], step):
            turned_ref[:, start : start + step] = weight_ref[start : start + step, :].T

    views, width = partners_ref.shape
    total = views * chips * cores
    place, core = here_ref[PLACE], here_ref[CORE]
    near = place + 1 - 2 * lax.rem(place, 2)
    beyond = lax.rem(place + chips - 1 + 2 * lax.rem(place, 2), chips)
    bases = []
    for at in (place, near, beyond):
        bases.append((at * cores + core) * views)
        bases.append((at * cores + 1 - core) * views)
    behind = (lax.rem(place + chips - 2, chips) * cores + 1) * views + views - EDGE
    ahead = lax.rem(place + 2, chips) * cores * views
    bases.append(jnp.where(core == 0, behind, ahead))
    rows = bias_ref.shape[0]
    row = lax.broadcasted_iota(jnp.int32, (rows, width), 0)
    listed = row + bases[0]
    for block in range(1, len(bases)):
        listed = jnp.where(row >= block * views, row - block * views + bases[block], listed)
    slot = lax.broadcasted_iota(jnp.int32, (rows, width), 1)
    for view in range(views):
        mine = (place * cores + core) * views + view
        hit = (partners_ref[view : view + 1, :] == listed) & (slot < counts_ref[view])
        hit = jnp.where(hit | (listed == mine), 1, 0)
        hit = jnp.max(hit, axis=1, keepdims=True)
        mask = jnp.where(hit > 0, 0.0, -1e30).astype(jnp.float32)
        bias_ref[:, view * L : view * L + L] = jnp.broadcast_to(mask, (rows, L))


def prepare(chips, cores, here, counts, partners, w_query, w_value, w_key, w_out):
    depth, width = w_value.shape
    views = partners.shape[0]
    turned = jax.ShapeDtypeStruct((width, depth), w_value.dtype)
    return call(
        functools.partial(prepare_kernel, chips, cores),
        [turned, turned, jax.ShapeDtypeStruct((6 * views + EDGE, views * L), jnp.float32)],
        [here, counts, partners, w_query, w_value, w_key, w_out],
        name="prepare",
    )


def project_kernel(pieces, parts, with_query, here_ref, *refs):
    token_refs, refs = refs[:pieces], refs[pieces:]
    depth = token_refs[0].shape[1]
    spans = []
    for step in range(pieces):
        place = lax.rem(here_ref[SIDE] + pieces - step, pieces)
        spans.append(pl.ds(pl.multiple_of(place * depth, depth), depth))

    def plain(weight_ref, out_refs):
        width = weight_ref.shape[1]
        tile = min(512, width)
        for start in range(0, width, tile):
            total = None
            for token_ref, span in zip(token_refs, spans):
                term = jnp.dot(
                    token_ref[...],
                    weight_ref[span, start : start + tile],
                    preferred_element_type=jnp.float32,
                )
                total = term if total is None else total + term
            total = total.astype(jnp.bfloat16)
            for index, out_ref in enumerate(out_refs):
                size = out_ref.shape[0]
                out_ref[:, start : start + tile] = total[index * size : index * size + size]

    def turned(weight_ref, out_refs):
        width = weight_ref.shape[0]
        tile = min(512, width)
        for start in range(0, width, tile):
            total = None
            for token_ref, span in zip(token_refs, spans):
                term = lax.dot_general(
                    weight_ref[start : start + tile, span],
                    token_ref[...],
                    ROWS_BY_ROWS,
                    preferred_element_type=jnp.float32,
                )
                total = term if total is None else total + term
            total = total.astype(jnp.bfloat16)
            for index, out_ref in enumerate(out_refs):
                size = out_ref.shape[1]
                out_ref[start : start + tile, :] = total[:, index * size : index * size + size]

    weights, outs = refs[: 2 + with_query], refs[2 + with_query :]
    plain(weights[0], outs[:parts])
    turned(weights[1], outs[parts : 2 * parts])
    if with_query:
        turned(weights[2], outs[2 * parts :])


def project(here, tokens, w_key, w_value, w_query=None, parts=1):
    rows = tokens[0].shape[0]
    width = w_key.shape[1]
    weights = [w_key, w_value] + ([] if w_query is None else [w_query])
    outs = [jax.ShapeDtypeStruct((rows // parts, width), jnp.bfloat16)] * parts
    outs += [jax.ShapeDtypeStruct((width, rows // parts), jnp.bfloat16)] * parts
    if w_query is not None:
        outs += [jax.ShapeDtypeStruct((width, rows), jnp.bfloat16)]
    outs = call(
        functools.partial(project_kernel, len(tokens), parts, w_query is not None),
        outs,
        [here, *tokens, *weights],
        name="project",
    )
    return list(zip(outs[:parts], outs[parts : 2 * parts])), outs[2 * parts :]


def scores_of(key_ref, first, last, query, column, bias_ref, bias_row, lanes, hold_ref, at, top):
    scores = jnp.dot(key_ref[first:last, column], query, preferred_element_type=jnp.float32)
    for view in range((last - first) // L):
        piece = scores[view * L : view * L + L] + bias_ref[bias_row + view : bias_row + view + 1, lanes]
        hold_ref[at + view * L : at + view * L + L, :] = piece
        best = jnp.max(piece.reshape(L // 8, 8, piece.shape[1]), axis=0)
        top = best if top is None else jnp.maximum(top, best)
    return top


def weigh(hold_ref, at, size, shift, value, total, mixed):
    weights = jnp.exp2(hold_ref[at : at + size, :] * FACTOR - shift)
    term = jnp.sum(weights.reshape(size // 8, 8, weights.shape[1]), axis=0)
    total = term if total is None else total + term
    update = jnp.dot(value, weights.astype(jnp.bfloat16), preferred_element_type=jnp.float32)
    mixed = update if mixed is None else mixed + update
    return total, mixed


def attend_kernel(blocks, bias_start, has_state, bias_ref, query_ref, *refs):
    key_refs, value_refs = refs[:blocks], refs[blocks : 2 * blocks]
    refs = refs[2 * blocks :]
    if has_state:
        top_in, total_in, mixed_in, top_out, total_out, mixed_out, hold = refs
    else:
        top_out, total_out, mixed_out, hold = refs
    heads = query_ref.shape[0] // HD
    everything = slice(None)
    for head in range(heads):
        column = slice(head * HD, head * HD + HD)
        row = slice(head, head + 1)
        query = query_ref[column, :]
        slot = hold.at[head % 2]
        top, at, groups = None, 0, []
        for index, key_ref in enumerate(key_refs):
            size = key_ref.shape[0]
            step = min(128, size)
            for first in range(0, size, step):
                top = scores_of(
                    key_ref, first, first + step, query, column,
                    bias_ref, bias_start + at // L, everything, slot, at, top,
                )
                if at % 256 == 0:
                    groups.append((at, []))
                groups[-1][1].append((index, first, step))
                at += step
        top = jnp.max(top, axis=0, keepdims=True)
        total = mixed = None
        if has_state:
            before = top_in[row, :]
            top = jnp.maximum(top, before)
        shift = top * FACTOR
        for at, group in groups:
            value = jnp.concatenate(
                [value_refs[i][column, first : first + step] for i, first, step in group], axis=1
            )
            total, mixed = weigh(slot, at, value.shape[1], shift, value, total, mixed)
        total = jnp.sum(total, axis=0, keepdims=True)
        if has_state:
            keep = jnp.exp2(before * FACTOR - shift)
            total = total + total_in[row, :] * keep
            mixed = mixed + mixed_in[column, :] * keep
        top_out[row, :] = top
        total_out[row, :] = total
        mixed_out[column, :] = mixed


def attend(bias, bias_start, query, blocks, state):
    width, rows = query.shape
    heads = width // HD
    span = sum(keys.shape[0] for keys, _ in blocks)
    outs = [
        jax.ShapeDtypeStruct((heads, rows), jnp.float32),
        jax.ShapeDtypeStruct((heads, rows), jnp.float32),
        jax.ShapeDtypeStruct((width, rows), jnp.float32),
    ]
    keys, values = [k for k, _ in blocks], [v for _, v in blocks]
    return call(
        functools.partial(attend_kernel, len(blocks), bias_start, state is not None),
        outs,
        [bias, query, *keys, *values, *(state or [])],
        scratch=[pltpu.VMEM((2, span, rows), jnp.float32)],
        name="attend",
    )


def finish_kernel(sides, bias_start, inner, has_rim, here_ref, top_ref, total_ref, mixed_ref, *refs):
    if has_rim:
        bias_ref, query_ref, key_ref, value_ref, weight_ref = refs[:5]
        refs = refs[5:]
        hold = refs[-1]
    else:
        weight_ref = refs[0]
        refs = refs[1:]
    sent_refs, kept_ref, done = refs[: sides - 1], refs[sides - 1], refs[sides]
    rows = kept_ref.shape[0]
    part = kept_ref.shape[1]
    spot = spot_of(here_ref, inner, rows, mixed_ref.shape[1])
    heads = mixed_ref.shape[0] // HD
    for head in range(heads):
        column = slice(head * HD, head * HD + HD)
        row = slice(head, head + 1)
        total = total_ref[row, spot]
        mixed = mixed_ref[column, spot]
        if has_rim:
            slot = hold.at[head % 2]
            size = key_ref.shape[0]
            before = top_ref[row, spot]
            top = scores_of(
                key_ref, 0, size, query_ref[column, spot], column,
                bias_ref, bias_start, spot, slot, 0, None,
            )
            top = jnp.maximum(jnp.max(top, axis=0, keepdims=True), before)
            shift = top * FACTOR
            more, update = weigh(slot, 0, size, shift, value_ref[column, :], None, None)
            keep = jnp.exp2(before * FACTOR - shift)
            total = total * keep + jnp.sum(more, axis=0, keepdims=True)
            mixed = mixed * keep + update
        done[:, column] = (mixed / total).T.astype(done.dtype)
    for step in range(sides):
        step = (step + 1) % sides
        place = lax.rem(here_ref[SIDE] + step, sides)
        columns = pl.ds(pl.multiple_of(place * part, part), part)
        result = jnp.dot(done[...], weight_ref[:, columns], preferred_element_type=jnp.float32)
        if step == 0:
            kept_ref[...] = result
        else:
            sent_refs[step - 1][...] = result.astype(jnp.bfloat16)


def spot_of(here_ref, inner, size, rows):
    late = 1 - here_ref[CORE] if inner else here_ref[CORE]
    return pl.ds(pl.multiple_of(late * (rows - size), L), size)


def finish(sides, here, inner, rows, state, weight, rim=None):
    top, total, mixed = state
    width = mixed.shape[0]
    part = weight.shape[1] // sides
    outs = [jax.ShapeDtypeStruct((rows, part), jnp.bfloat16)] * (sides - 1)
    outs += [jax.ShapeDtypeStruct((rows, part), jnp.float32)]
    scratch = [pltpu.VMEM((rows, width), jnp.bfloat16)]
    ins = [here, top, total, mixed]
    bias_start = 0
    if rim is not None:
        bias, bias_start, query, keys, values = rim
        ins += [bias, query, keys, values]
        scratch += [pltpu.VMEM((2, keys.shape[0], rows), jnp.float32)]
    return call(
        functools.partial(finish_kernel, sides, bias_start, inner, rim is not None),
        outs,
        ins + [weight],
        scratch=scratch,
        name="finish",
    )


def settle_kernel(inner, count, here_ref, *refs):
    kept_ref, term_refs = refs[0], refs[1:count]
    out_ref, hold, sem = refs[-3:]
    total = kept_ref[...]
    for term_ref in term_refs:
        total += term_ref[...].astype(jnp.float32)
    hold[...] = total.astype(hold.dtype)
    rows = hold.shape[0]
    spot = spot_of(here_ref, inner, rows, out_ref.shape[0])
    copy = pltpu.make_async_copy(hold, out_ref.at[spot, :], sem)
    copy.start()
    copy.wait()


def settle(here, inner, parts, rows, before=None):
    size, width = parts[0].shape
    ins = [here, *parts] + ([] if before is None else [before])
    return call(
        functools.partial(settle_kernel, inner, len(parts)),
        jax.ShapeDtypeStruct((rows, width), jnp.bfloat16),
        ins,
        scratch=[pltpu.VMEM((size, width), jnp.bfloat16), pltpu.SemaphoreType.DMA],
        out_specs=HBM,
        whole=() if before is None else (len(ins) - 1,),
        aliases=None if before is None else {len(ins) - 1: 0},
        name="settle",
    )


def shards(tokens, w_query, w_key, w_value, w_out, partners, counts):
    rows = tokens.shape[0]
    views_here = rows // L
    chips = lax.axis_size("views")
    cores = lax.axis_size("sub")
    sides = lax.axis_size("heads")
    core = lax.axis_index("sub")
    here = jnp.stack([lax.axis_index(name) for name in ("views", "sub", "heads")]).astype(jnp.int32)

    def shift(a, step):
        return lax.ppermute(a, "heads", [(h, (h + step) % sides) for h in range(sides)])

    def gather(a):
        return [a] + [shift(a, step) for step in range(1, sides)]

    def share(blocks):
        return [tuple(lax.ppermute(a, "sub", [(0, 1), (1, 0)]) for a in block) for block in blocks]

    pair = [(z, z ^ 1) for z in range(chips)]
    side_step = [(z, ((z - 1) if z % 2 == 0 else (z + 1)) % chips) for z in range(chips)]
    edge = [(2 * z + 1, 2 * ((z + 2) % chips)) for z in range(chips)]
    edge += [(2 * z, 2 * ((z - 2) % chips) + 1) for z in range(chips)]

    edge_rows = EDGE * L
    rim = lax.dynamic_slice_in_dim(tokens, core * (rows - edge_rows), edge_rows, axis=0)
    here = after(here, rim)
    own = gather(tokens)
    near = lax.ppermute(tokens, "views", pair)
    beyond = lax.ppermute(tokens, "views", side_step)
    w_query, w_value, bias = prepare(
        chips, cores, here, counts, partners, w_query, w_value, w_key, w_out
    )
    rim = lax.ppermute(after(rim, own[1]), ("views", "sub"), edge)

    own_blocks, (query,) = project(here, own, w_key, w_value, w_query, 2)
    own_shared = share(own_blocks)
    state = attend(bias, 0, query, own_blocks + own_shared[:1], None)
    near = gather(near)
    beyond = gather(after(beyond, state[0]))
    near_blocks, _ = project(here, near, w_key, w_value)
    near_shared = share(near_blocks)
    state = attend(bias, views_here + 2, query, own_shared[1:] + near_blocks, state)
    rim = gather(rim)
    beyond[1] = after(beyond[1], state[0], rim[0])
    beyond_blocks, _ = project(here, beyond, w_key, w_value)
    beyond_shared = share([(after(beyond_blocks[0][0], rim[1]), beyond_blocks[0][1])])
    state = attend(bias, 3 * views_here, query, near_shared + beyond_blocks, state)
    ((rim_keys, rim_values),), _ = project(here, rim, w_key, w_value)
    state = attend(bias, 5 * views_here, query, beyond_shared, state)

    inner = finish(sides, here, True, rows - edge_rows, state, w_out)
    outer = finish(
        sides, here, False, edge_rows, [after(state[0], inner[0]), *state[1:]], w_out,
        (bias, 6 * views_here, query, rim_keys, rim_values),
    )

    def exchange(parts):
        return [parts[-1]] + [shift(part, step + 1) for step, part in enumerate(parts[:-1])]

    inner, outer = exchange(inner), exchange(outer)
    attended = settle(here, True, inner, rows)
    return settle(here, False, outer, rows, attended)


def solution(mesh):
    in_specs = (
        P(("groups", "views", "sub"), "heads"),
        P(None, "heads"),
        P(None, "heads"),
        P(None, "heads"),
        P("heads", None),
        P(("groups", "views", "sub"), None),
        P(("groups", "views", "sub")),
    )
    out_specs = P(("groups", "views", "sub"), "heads")
    return jax.shard_map(shards, mesh=mesh, in_specs=in_specs, out_specs=out_specs, check_vma=False)
```

time: 208 us -> 81.9 us (0.39)
  waiting for transfers between devices: 131 us -> 23.1 us
  Pallas kernels: 0 us -> 31.7 us
  matrix products: 29.6 us -> 0 us
  starting transfers between devices: 0.12 us -> 15.3 us
  between operations: 13.2 us -> 0.39 us
  local copies, waits for them, and re-layouts: 22.8 us -> 11.1 us
  other arithmetic: 10.6 us -> 0.08 us
    all_gather x3 -> x0, waiting for transfers between devices: 111 us -> none  [the longest x1 47.6 us: shards(): lax.all_gather(keys_flat, ('views', 'sub'), axis=0, tiled=True)]
    pallas_call x0 -> x13, Pallas kernels: none -> 31.7 us  [call(): pl.pallas_call(kernel, out_shape=outs, in_specs=[HBM if k in whole else S...]
    ppermute x0 -> x17, waiting for transfers between devices: none -> 23.1 us  [the longest x1 13.2 us: shards(): rim = lax.ppermute(after(rim, own[1]), ('views', 'sub'), edge)]
    dot_general x8 -> x0, matrix products: 22.7 us -> none  [the longest x3 12.4 us: shards(): jnp.dot(piece, weight, preferred_element_type=jnp.float32)]
    reduce_scatter x1 -> x0, waiting for transfers between devices: 19.2 us -> none  [shards(): lax.psum_scatter(partial_sum.astype(jnp.bfloat16), 'heads', scatter_dimen...]
    ppermute x0 -> x17, starting transfers between devices: none -> 15.3 us  [the longest x6 7.71 us: shift(): lax.ppermute(a, 'heads', [(h, (h + step) % sides) for h in range(sides)])]
    dynamic_slice x20 -> x1, local copies, waits for them, and re-layouts: 11.9 us -> 0.97 us  [shards(): lax.dynamic_slice_in_dim(tokens, core * (rows - edge_rows), edge_rows, ax...]
    unnamed x11 -> x18, local copies, waits for them, and re-layouts: 1.13 us -> 10.1 us
  transfers between devices with their start and end apart: 4 -> 17, of which waited for: 4 -> 6; matrix products, arithmetic and copies ran while one was open for 4% -> 1% of each run, Pallas kernels for 0% -> 33%
where the time goes in v2:
time: 81.9 us; the launch traced here: 81.6 us
  Pallas kernels  31.7 us (39%)
  waiting for transfers between devices  23.1 us (28%)
  starting transfers between devices  15.3 us (19%)
  local copies, waits for them, and re-layouts  11.1 us (14%)
    pallas_call x13, Pallas kernels, call(): pl.pallas_call(kernel, out_shape=outs, in_specs=[HBM if k in whole else S...  31.7 us
    ppermute x1, waiting for transfers between devices, shards(): rim = lax.ppermute(after(rim, own[1]), ('views', 'sub'), edge)  13.2 us
    unnamed x18, local copies, waits for them, and re-layouts  10.1 us
    ppermute x6, waiting for transfers between devices, shift(): lax.ppermute(a, 'heads', [(h, (h + step) % sides) for h in range(sides)])  8.84 us
    ppermute x6, starting transfers between devices, shift(): lax.ppermute(a, 'heads', [(h, (h + step) % sides) for h in range(sides)])  7.71 us
    ppermute x8, starting transfers between devices, share(): lax.ppermute(a, 'sub', [(0, 1), (1, 0)])  3.52 us
    ppermute x1, starting transfers between devices, shards(): beyond = lax.ppermute(tokens, 'views', side_step)  2.47 us
  transfers between devices with their start and end apart: 17, of which 6 were waited for; matrix products, arithmetic and copies ran while one was open for 1% of the time, Pallas kernels for 33%

profile of v2, /device:TPU:0, one launch (start us, length us, event | category | flops | bytes accessed | tf_op | source)
XLA Modules:
  0.0 81.6 jit_solution(10956923891069264744)
XLA Ops:
  0.0 2.9 %collective-permute-start = (bf16[256,1024]{1,0:T(8,128)(2,1)}, bf16[256,1024]{1,0:T(8,128)(2,1)S(1)}, u32[]{:S(2)}, u32[]{:S(2)}) collective-permute-start(bf16[256,1024]{1,0:T(8,128)(2,1)} %refs_0_.4), channel_id=1, source_target_pairs={{0,2},{2,0},{1,3},{3,1},{4,6},{6,4},{5,7},{7,5},{8,10},{10,8},{9,1... | collective-permute-start | bytes 1572872 | tf_op jit(solution)/shard_map/ppermute | solution.py:353
  2.9 1.6 %collective-permute-start.6 = (bf16[256,1024]{1,0:T(8,128)(2,1)}, bf16[256,1024]{1,0:T(8,128)(2,1)S(1)}, u32[]{:S(2)}, u32[]{:S(2)}) collective-permute-start(bf16[256,1024]{1,0:T(8,128)(2,1)} %refs_0_.4), channel_id=1, source_target_pairs={{0,4},{4,0},{8,12},{12,8},{1,5},{5,1},{9,13},{13,9},{2,6},{6,2},{1... | collective-permute-start | bytes 1572872 | tf_op jit(solution)/shard_map/ppermute | solution.py:370
  4.5 2.5 %collective-permute-start.1 = (bf16[256,1024]{1,0:T(8,128)(2,1)}, bf16[256,1024]{1,0:T(8,128)(2,1)S(1)}, u32[]{:S(2)}, u32[]{:S(2)}) collective-permute-start(bf16[256,1024]{1,0:T(8,128)(2,1)} %refs_0_.4), channel_id=1, source_target_pairs={{0,12},{4,8},{8,4},{12,0},{1,13},{5,9},{9,5},{13,1},{2,14},{6,10},... | collective-permute-start | bytes 1572872 | tf_op jit(solution)/shard_map/ppermute | solution.py:371
  7.0 0.1 pad_add_fusion.here_ref
  7.1 1.0 %constant_dynamic-slice_fusion = bf16[128,1024]{1,0:T(8,128)(2,1)S(1)} fusion(bf16[256,1024]{1,0:T(8,128)(2,1)} %refs_0_.4, s32[]{:T(128)S(6)} %select_n.3), kind=kLoop, calls=%fused_computation.1 | loop fusion | bytes 524292 | tf_op jit(solution)/shard_map/dynamic_slice | solution.py:367
  8.0 0.0 copy-start
  8.1 2.2 %copy-done = bf16[2048,1024]{1,0:T(8,128)(2,1)S(1)} copy-done((bf16[2048,1024]{1,0:T(8,128)(2,1)S(1)}, bf16[2048,1024]{1,0:T(8,128)(2,1)}, u32[]{:S(2)}) %copy-start) | copy-done | bytes 4194328
  10.2 2.2 %copy-done.2 = bf16[1024,2048]{1,0:T(8,128)(2,1)S(1)} copy-done((bf16[1024,2048]{1,0:T(8,128)(2,1)S(1)}, bf16[1024,2048]{1,0:T(8,128)(2,1)}, u32[]{:S(2)}) %copy-start.2) | copy-done | bytes 4194328
  12.4 2.2 %copy-done.4 = bf16[2048,1024]{1,0:T(8,128)(2,1)S(1)} copy-done((bf16[2048,1024]{1,0:T(8,128)(2,1)S(1)}, bf16[2048,1024]{1,0:T(8,128)(2,1)}, u32[]{:S(2)}) %copy-start.4) | copy-done | bytes 4194328
  14.6 2.2 %copy-done.5 = bf16[2048,1024]{1,0:T(8,128)(2,1)S(1)} copy-done((bf16[2048,1024]{1,0:T(8,128)(2,1)S(1)}, bf16[2048,1024]{1,0:T(8,128)(2,1)}, u32[]{:S(2)}) %copy-start.5) | copy-done | bytes 4194328
  16.8 0.7 copy-done.7
  17.5 0.7 copy-done.8
  18.1 2.9 %prepare.1 = (bf16[1024,2048]{1,0:T(8,128)(2,1)S(1)}, bf16[1024,2048]{1,0:T(8,128)(2,1)S(1)}, f32[26,256]{1,0:T(8,128)S(1)}) custom-call(s32[3]{0:T(128)S(1)} %pad_add_fusion.here_ref, s32[4]{0:T(128)S(1)} %copy-done.8, s32[4,20]{1,0:T(4,128)S(1)} %copy-done.7, bf16[2048,1024]{1,0:T(8,128)(2,1)S(1)} %copy-done.4, bf16[2048,1024]{1,0:T(8,128)(2,1)S(1)} %copy-done.5, ...), custom_call_target="tpu_custom_call" | custom-call | tf_op jit(solution)/shard_map/prepare/pallas_call | solution.py:24
  21.0 0.0 collective-permute-done.refs_1_
  21.0 4.0 %project.4 = (bf16[128,1024]{1,0:T(8,128)(2,1)S(1)}, bf16[128,1024]{1,0:T(8,128)(2,1)S(1)}, bf16[1024,128]{1,0:T(8,128)(2,1)S(1)}, bf16[1024,128]{1,0:T(8,128)(2,1)S(1)}, bf16[1024,256]{1,0:T(8,128)(2,1)S(1)}) custom-call(s32[3]{0:T(128)S(1)} %pad_add_fusion.here_ref, bf16[256,1024]{1,0:T(8,128)(2,1)S(1)} %copy-done.6, ...), custom_call_target="tpu_custom_call" | custom-call | tf_op jit(solution)/shard_map/project/pallas_call | solution.py:24
  25.0 0.1 collective-permute-start.2
  25.1 0.5 collective-permute-start.3
  25.6 0.5 collective-permute-start.7
  26.1 0.5 collective-permute-done.2.refs_2_
  26.6 0.4 collective-permute-done.3.refs_5_
  27.0 2.8 %attend.4 = (f32[8,256]{1,0:T(8,128)S(1)}, f32[8,256]{1,0:T(8,128)S(1)}, f32[1024,256]{1,0:T(8,128)S(1)}) custom-call(f32[26,256]{1,0:T(8,128)S(1)} %get-tuple-element.42.bias_ref.refs_0_, bf16[1024,256]{1,0:T(8,128)(2,1)S(1)} %get-tuple-element.45.query_ref.refs_1_, bf16[128,1024]{1,0:T(8,128)(2,1)S(1)} %get-tuple-element.46.refs_0_, ...), custom_call_target="tpu_custom_call" | custom-call | tf_op jit(solution)/shard_map/attend/pallas_call | solution.py:24
  29.8 0.1 collective-permute-done.1.refs_0_
  29.9 0.6 collective-permute-start.4
  30.5 0.0 collective-permute-start.9
  30.5 1.8 %collective-permute-start.5 = (bf16[128,1024]{1,0:T(8,128)(2,1)S(1)}, bf16[128,1024]{1,0:T(8,128)(2,1)S(1)}, u32[]{:S(2)}, u32[]{:S(2)}) collective-permute-start(bf16[128,1024]{1,0:T(8,128)(2,1)S(1)} %get-tuple-element.47.refs_1_), channel_id=1, source_target_pairs={{0,1},{1,0},{2,3},{3,2},{4,5},{5,4},{6,7},{7,6},{8,9},{9,8},{10,11... | collective-permute-start | bytes 786440 | tf_op jit(solution)/shard_map/ppermute | solution.py:359
  32.3 0.0 collective-permute-start.8
  32.3 13.2 %collective-permute-done.9.refs_0_ = bf16[128,1024]{1,0:T(8,128)(2,1)S(1)} collective-permute-done((bf16[128,1024]{1,0:T(8,128)(2,1)S(1)}, bf16[128,1024]{1,0:T(8,128)(2,1)S(1)}, u32[]{:S(2)}, u32[]{:S(2)}) %collective-permute-start.9) | collective-permute-done | bytes 262176 | tf_op jit(solution)/shard_map/ppermute | solution.py:375
  45.5 1.5 %collective-permute-start.10 = (bf16[128,1024]{1,0:T(8,128)(2,1)S(1)}, bf16[128,1024]{1,0:T(8,128)(2,1)S(1)}, u32[]{:S(2)}, u32[]{:S(2)}) collective-permute-start(bf16[128,1024]{1,0:T(8,128)(2,1)S(1)} %collective-permute-done.9.refs_0_), channel_id=1, source_target_pairs={{0,2},{2,0},{1,3},{3,1},{4,6},{6,4},{5,7},{7,5},{8,10},{10,8},{9,1... | collective-permute-start | bytes 786440 | tf_op jit(solution)/shard_map/ppermute | solution.py:353
  47.0 0.0 collective-permute-done.7.refs_1_
  47.0 2.9 %project.5 = (bf16[256,1024]{1,0:T(8,128)(2,1)S(1)}, bf16[1024,256]{1,0:T(8,128)(2,1)S(1)}) custom-call(s32[3]{0:T(128)S(1)} %pad_add_fusion.here_ref, bf16[256,1024]{1,0:T(8,128)(2,1)S(1)} %collective-permute-done.6.refs_0_, bf16[256,1024]{1,0:T(8,128)(2,1)S(1)} %collective-permute-done.7.refs_1_, bf16[2048,1024]{1,0:T(8,128)(2,1)S(1)} %copy-done.1, ...), custom_call_target="tpu_custom_call" | custom-call | tf_op jit(solution)/shard_map/project/pallas_call | solution.py:24
  49.9 0.1 collective-permute-start.13
  50.0 0.5 collective-permute-start.14
  50.5 2.8 %attend.5 = (f32[8,256]{1,0:T(8,128)S(1)}, f32[8,256]{1,0:T(8,128)S(1)}, f32[1024,256]{1,0:T(8,128)S(1)}) custom-call(f32[26,256]{1,0:T(8,128)S(1)} %get-tuple-element.42.bias_ref.refs_0_, bf16[1024,256]{1,0:T(8,128)(2,1)S(1)} %get-tuple-element.45.query_ref.refs_1_, bf16[128,1024]{1,0:T(8,128)(2,1)S(1)} %collective-permute-done.5.refs_0_, ...), custom_call_target="tpu_custom_call" | custom-call | tf_op jit(solution)/shard_map/attend/pallas_call | solution.py:24
  53.3 3.1 %project.6 = (bf16[256,1024]{1,0:T(8,128)(2,1)S(1)}, bf16[1024,256]{1,0:T(8,128)(2,1)S(1)}) custom-call(s32[3]{0:T(128)S(1)} %pad_add_fusion.here_ref, bf16[256,1024]{1,0:T(8,128)(2,1)S(1)} %collective-permute-done.1.refs_0_, bf16[256,1024]{1,0:T(8,128)(2,1)S(1)} %collective-permute-done.4.refs_1_, bf16[2048,1024]{1,0:T(8,128)(2,1)S(1)} %copy-done.1, ...), custom_call_target="tpu_custom_call" | custom-call | tf_op jit(solution)/shard_map/project/pallas_call | solution.py:24
  56.4 0.2 collective-permute-start.11
  56.6 0.4 collective-permute-start.12
  57.0 2.4 %project.7 = (bf16[128,1024]{1,0:T(8,128)(2,1)S(1)}, bf16[1024,128]{1,0:T(8,128)(2,1)S(1)}) custom-call(s32[3]{0:T(128)S(1)} %pad_add_fusion.here_ref, bf16[128,1024]{1,0:T(8,128)(2,1)S(1)} %collective-permute-done.9.refs_0_, bf16[128,1024]{1,0:T(8,128)(2,1)S(1)} %collective-permute-done.10.refs_1_, bf16[2048,1024]{1,0:T(8,128)(2,1)S(1)} %copy-done.1, ...), custom_call_target="tpu_custom_call" | custom-call | tf_op jit(solution)/shard_map/project/pallas_call | solution.py:24
  59.4 0.0 copy-start.3
  59.4 3.0 %attend.6 = (f32[8,256]{1,0:T(8,128)S(1)}, f32[8,256]{1,0:T(8,128)S(1)}, f32[1024,256]{1,0:T(8,128)S(1)}) custom-call(f32[26,256]{1,0:T(8,128)S(1)} %get-tuple-element.42.bias_ref.refs_0_, bf16[1024,256]{1,0:T(8,128)(2,1)S(1)} %get-tuple-element.45.query_ref.refs_1_, bf16[256,1024]{1,0:T(8,128)(2,1)S(1)} %collective-permute-done.13.refs_0_, ...), custom_call_target="tpu_custom_call" | custom-call | tf_op jit(solution)/shard_map/attend/pallas_call | solution.py:24
  62.5 2.3 %attend.7 = (f32[8,256]{1,0:T(8,128)S(1)}, f32[8,256]{1,0:T(8,128)S(1)}, f32[1024,256]{1,0:T(8,128)S(1)}) custom-call(f32[26,256]{1,0:T(8,128)S(1)} %get-tuple-element.42.bias_ref.refs_0_, bf16[1024,256]{1,0:T(8,128)(2,1)S(1)} %get-tuple-element.45.query_ref.refs_1_, bf16[256,1024]{1,0:T(8,128)(2,1)S(1)} %collective-permute-done.11.refs_0_, ...), custom_call_target="tpu_custom_call" | custom-call | tf_op jit(solution)/shard_map/attend/pallas_call | solution.py:24
  64.8 1.3 %finish.2 = (bf16[128,1024]{1,0:T(8,128)(2,1)S(1)}, f32[128,1024]{1,0:T(8,128)S(1)}) custom-call(s32[3]{0:T(128)S(1)} %pad_add_fusion.here_ref, f32[8,256]{1,0:T(8,128)S(1)} %get-tuple-element.71.top_ref, f32[8,256]{1,0:T(8,128)S(1)} %get-tuple-element.68.total_ref, f32[1024,256]{1,0:T(8,128)S(1)} %get-tuple-element.69.mixed_ref, ...), custom_call_target="tpu_custom_call" | custom-call | tf_op jit(solution)/shard_map/finish/pallas_call | solution.py:24
  66.1 0.6 collective-permute-start.16
  66.7 1.7 %finish.3 = (bf16[128,1024]{1,0:T(8,128)(2,1)S(1)}, f32[128,1024]{1,0:T(8,128)S(1)}) custom-call(s32[3]{0:T(128)S(1)} %pad_add_fusion.here_ref, f32[8,256]{1,0:T(8,128)S(1)} %get-tuple-element.71.top_ref, f32[8,256]{1,0:T(8,128)S(1)} %get-tuple-element.68.total_ref, f32[1024,256]{1,0:T(8,128)S(1)} %get-tuple-element.69.mixed_ref, ...), custom_call_target="tpu_custom_call" | custom-call | tf_op jit(solution)/shard_map/finish/pallas_call | solution.py:24
  68.4 1.5 %collective-permute-start.15 = (bf16[128,1024]{1,0:T(8,128)(2,1)S(1)}, bf16[128,1024]{1,0:T(8,128)(2,1)S(1)}, u32[]{:S(2)}, u32[]{:S(2)}) collective-permute-start(bf16[128,1024]{1,0:T(8,128)(2,1)S(1)} %get-tuple-element.75), channel_id=1, source_target_pairs={{0,2},{2,0},{1,3},{3,1},{4,6},{6,4},{5,7},{7,5},{8,10},{10,8},{9,1... | collective-permute-start | bytes 786440 | tf_op jit(solution)/shard_map/ppermute | solution.py:353
  70.0 5.4 %collective-permute-done.16.refs_1_ = bf16[128,1024]{1,0:T(8,128)(2,1)S(1)} collective-permute-done((bf16[128,1024]{1,0:T(8,128)(2,1)S(1)}, bf16[128,1024]{1,0:T(8,128)(2,1)S(1)}, u32[]{:S(2)}, u32[]{:S(2)}) %collective-permute-start.16) | collective-permute-done | bytes 262176 | tf_op jit(solution)/shard_map/ppermute | solution.py:353
  75.4 1.3 %settle.2.refs_2_ = bf16[256,1024]{1,0:T(8,128)(2,1)} custom-call(s32[3]{0:T(128)S(1)} %pad_add_fusion.here_ref, f32[128,1024]{1,0:T(8,128)S(1)} %get-tuple-element.76.refs_0_, bf16[128,1024]{1,0:T(8,128)(2,1)S(1)} %collective-permute-done.16.refs_1_), custom_call_target="tpu_custom_call" | custom-call | tf_op jit(solution)/shard_map/settle/pallas_call | solution.py:24
  76.7 3.5 %collective-permute-done.15.refs_1_ = bf16[128,1024]{1,0:T(8,128)(2,1)S(1)} collective-permute-done((bf16[128,1024]{1,0:T(8,128)(2,1)S(1)}, bf16[128,1024]{1,0:T(8,128)(2,1)S(1)}, u32[]{:S(2)}, u32[]{:S(2)}) %collective-permute-start.15) | collective-permute-done | bytes 262176 | tf_op jit(solution)/shard_map/ppermute | solution.py:353
  80.1 1.3 %settle.3 = bf16[256,1024]{1,0:T(8,128)(2,1)} custom-call(s32[3]{0:T(128)S(1)} %pad_add_fusion.here_ref, f32[128,1024]{1,0:T(8,128)S(1)} %get-tuple-element.74.refs_0_, bf16[128,1024]{1,0:T(8,128)(2,1)S(1)} %collective-permute-done.15.refs_1_, bf16[256,1024]{1,0:T(8,128)(2,1)} %settle.2.refs_2_), custom_call_target="tpu_custom_call", output_to_operand_aliasing={{}: (3, {})} | custom-call | tf_op jit(solution)/shard_map/settle/pallas_call | solution.py:24
  (19 shorter events, 0.0 us)
Async XLA Ops:
  0.0 21.0 %collective-permute-start = (bf16[256,1024]{1,0:T(8,128)(2,1)}, bf16[256,1024]{1,0:T(8,128)(2,1)S(1)}, u32[]{:S(2)}, u32[]{:S(2)}) collective-permute-start(bf16[256,1024]{1,0:T(8,128)(2,1)} %refs_0_.4), channel_id=1, source_target_pairs={{0,2},{2,0},{1,3},{3,1},{4,6},{6,4},{5,7},{7,5},{8,10},{10,8},{9,1... | collective-permute-start | bytes 1572872 | tf_op jit(solution)/shard_map/ppermute | solution.py:353
  2.9 22.7 %collective-permute-start.6 = (bf16[256,1024]{1,0:T(8,128)(2,1)}, bf16[256,1024]{1,0:T(8,128)(2,1)S(1)}, u32[]{:S(2)}, u32[]{:S(2)}) collective-permute-start(bf16[256,1024]{1,0:T(8,128)(2,1)} %refs_0_.4), channel_id=1, source_target_pairs={{0,4},{4,0},{8,12},{12,8},{1,5},{5,1},{9,13},{13,9},{2,6},{6,2},{1... | collective-permute-start | bytes 1572872 | tf_op jit(solution)/shard_map/ppermute | solution.py:370
  4.5 25.4 %collective-permute-start.1 = (bf16[256,1024]{1,0:T(8,128)(2,1)}, bf16[256,1024]{1,0:T(8,128)(2,1)S(1)}, u32[]{:S(2)}, u32[]{:S(2)}) collective-permute-start(bf16[256,1024]{1,0:T(8,128)(2,1)} %refs_0_.4), channel_id=1, source_target_pairs={{0,12},{4,8},{8,4},{12,0},{1,13},{5,9},{9,5},{13,1},{2,14},{6,10},... | collective-permute-start | bytes 1572872 | tf_op jit(solution)/shard_map/ppermute | solution.py:371
  8.0 2.2 %copy-start = (bf16[2048,1024]{1,0:T(8,128)(2,1)S(1)}, bf16[2048,1024]{1,0:T(8,128)(2,1)}, u32[]{:S(2)}) copy-start(bf16[2048,1024]{1,0:T(8,128)(2,1)} %refs_2_.9) | copy-start | bytes 12582916
  10.2 2.2 %copy-start.2 = (bf16[1024,2048]{1,0:T(8,128)(2,1)S(1)}, bf16[1024,2048]{1,0:T(8,128)(2,1)}, u32[]{:S(2)}) copy-start(bf16[1024,2048]{1,0:T(8,128)(2,1)} %refs_4_.1) | copy-start | bytes 12582916
  12.4 2.2 %copy-start.4 = (bf16[2048,1024]{1,0:T(8,128)(2,1)S(1)}, bf16[2048,1024]{1,0:T(8,128)(2,1)}, u32[]{:S(2)}) copy-start(bf16[2048,1024]{1,0:T(8,128)(2,1)} %refs_0_.3) | copy-start | bytes 12582916
  14.6 2.2 %copy-start.5 = (bf16[2048,1024]{1,0:T(8,128)(2,1)S(1)}, bf16[2048,1024]{1,0:T(8,128)(2,1)}, u32[]{:S(2)}) copy-start(bf16[2048,1024]{1,0:T(8,128)(2,1)} %refs_1_.1) | copy-start | bytes 12582916
  16.8 0.7 copy-start.7
  17.5 0.7 copy-start.8
  18.1 2.9 %copy-start.1 = (bf16[2048,1024]{1,0:T(8,128)(2,1)S(1)}, bf16[2048,1024]{1,0:T(8,128)(2,1)}, u32[]{:S(2)}) copy-start(bf16[2048,1024]{1,0:T(8,128)(2,1)} %refs_2_.9) | copy-start | bytes 12582916
  18.1 2.9 %copy-start.6 = (bf16[256,1024]{1,0:T(8,128)(2,1)S(1)}, bf16[256,1024]{1,0:T(8,128)(2,1)}, u32[]{:S(2)}) copy-start(bf16[256,1024]{1,0:T(8,128)(2,1)} %refs_0_.4) | copy-start | bytes 1572868
  25.0 1.6 %collective-permute-start.2 = (bf16[128,1024]{1,0:T(8,128)(2,1)S(1)}, bf16[128,1024]{1,0:T(8,128)(2,1)S(1)}, u32[]{:S(2)}, u32[]{:S(2)}) collective-permute-start(bf16[128,1024]{1,0:T(8,128)(2,1)S(1)} %get-tuple-element.46.refs_0_), channel_id=1, source_target_pairs={{0,1},{1,0},{2,3},{3,2},{4,5},{5,4},{6,7},{7,6},{8,9},{9,8},{10,11... | collective-permute-start | bytes 786440 | tf_op jit(solution)/shard_map/ppermute | solution.py:359
  25.1 1.9 %collective-permute-start.3 = (bf16[1024,128]{1,0:T(8,128)(2,1)S(1)}, bf16[1024,128]{1,0:T(8,128)(2,1)S(1)}, u32[]{:S(2)}, u32[]{:S(2)}) collective-permute-start(bf16[1024,128]{1,0:T(8,128)(2,1)S(1)} %get-tuple-element.48.refs_3_), channel_id=1, source_target_pairs={{0,1},{1,0},{2,3},{3,2},{4,5},{5,4},{6,7},{7,6},{8,9},{9,8},{10,11... | collective-permute-start | bytes 786440 | tf_op jit(solution)/shard_map/ppermute | solution.py:359
  25.6 21.4 %collective-permute-start.7 = (bf16[256,1024]{1,0:T(8,128)(2,1)S(1)}, bf16[256,1024]{1,0:T(8,128)(2,1)S(1)}, u32[]{:S(2)}, u32[]{:S(2)}) collective-permute-start(bf16[256,1024]{1,0:T(8,128)(2,1)S(1)} %collective-permute-done.6.refs_0_), channel_id=1, source_target_pairs={{0,2},{2,0},{1,3},{3,1},{4,6},{6,4},{5,7},{7,5},{8,10},{10,8},{9,1... | collective-permute-start | bytes 1572872 | tf_op jit(solution)/shard_map/ppermute | solution.py:353
  29.9 23.4 %collective-permute-start.4 = (bf16[256,1024]{1,0:T(8,128)(2,1)S(1)}, bf16[256,1024]{1,0:T(8,128)(2,1)S(1)}, u32[]{:S(2)}, u32[]{:S(2)}) collective-permute-start(bf16[256,1024]{1,0:T(8,128)(2,1)S(1)} %collective-permute-done.1.refs_0_), channel_id=1, source_target_pairs={{0,2},{2,0},{1,3},{3,1},{4,6},{6,4},{5,7},{7,5},{8,10},{10,8},{9,1... | collective-permute-start | bytes 1572872 | tf_op jit(solution)/shard_map/ppermute | solution.py:353
  30.5 15.1 %collective-permute-start.9 = (bf16[128,1024]{1,0:T(8,128)(2,1)S(1)}, bf16[128,1024]{1,0:T(8,128)(2,1)S(1)}, u32[]{:S(2)}, u32[]{:S(2)}) collective-permute-start(bf16[128,1024]{1,0:T(8,128)(2,1)S(1)} %constant_dynamic-slice_fusion), channel_id=1, source_target_pairs={{1,8},{5,12},{9,0},{13,4},{0,9},{4,13},{8,1},{12,5},{3,10},{7,14},... | collective-permute-start | bytes 786440 | tf_op jit(solution)/shard_map/ppermute | solution.py:375
  30.5 19.5 %collective-permute-start.5 = (bf16[128,1024]{1,0:T(8,128)(2,1)S(1)}, bf16[128,1024]{1,0:T(8,128)(2,1)S(1)}, u32[]{:S(2)}, u32[]{:S(2)}) collective-permute-start(bf16[128,1024]{1,0:T(8,128)(2,1)S(1)} %get-tuple-element.47.refs_1_), channel_id=1, source_target_pairs={{0,1},{1,0},{2,3},{3,2},{4,5},{5,4},{6,7},{7,6},{8,9},{9,8},{10,11... | collective-permute-start | bytes 786440 | tf_op jit(solution)/shard_map/ppermute | solution.py:359
  32.3 18.2 %collective-permute-start.8 = (bf16[1024,128]{1,0:T(8,128)(2,1)S(1)}, bf16[1024,128]{1,0:T(8,128)(2,1)S(1)}, u32[]{:S(2)}, u32[]{:S(2)}) collective-permute-start(bf16[1024,128]{1,0:T(8,128)(2,1)S(1)} %get-tuple-element.49.refs_4_), channel_id=1, source_target_pairs={{0,1},{1,0},{2,3},{3,2},{4,5},{5,4},{6,7},{7,6},{8,9},{9,8},{10,11... | collective-permute-start | bytes 786440 | tf_op jit(solution)/shard_map/ppermute | solution.py:359
  45.5 10.9 %collective-permute-start.10 = (bf16[128,1024]{1,0:T(8,128)(2,1)S(1)}, bf16[128,1024]{1,0:T(8,128)(2,1)S(1)}, u32[]{:S(2)}, u32[]{:S(2)}) collective-permute-start(bf16[128,1024]{1,0:T(8,128)(2,1)S(1)} %collective-permute-done.9.refs_0_), channel_id=1, source_target_pairs={{0,2},{2,0},{1,3},{3,1},{4,6},{6,4},{5,7},{7,5},{8,10},{10,8},{9,1... | collective-permute-start | bytes 786440 | tf_op jit(solution)/shard_map/ppermute | solution.py:353
  49.9 9.4 %collective-permute-start.13 = (bf16[256,1024]{1,0:T(8,128)(2,1)S(1)}, bf16[256,1024]{1,0:T(8,128)(2,1)S(1)}, u32[]{:S(2)}, u32[]{:S(2)}) collective-permute-start(bf16[256,1024]{1,0:T(8,128)(2,1)S(1)} %get-tuple-element.52.refs_1_), channel_id=1, source_target_pairs={{0,1},{1,0},{2,3},{3,2},{4,5},{5,4},{6,7},{7,6},{8,9},{9,8},{10,11... | collective-permute-start | bytes 1572872 | tf_op jit(solution)/shard_map/ppermute | solution.py:359
  50.0 9.4 %collective-permute-start.14 = (bf16[1024,256]{1,0:T(8,128)(2,1)S(1)}, bf16[1024,256]{1,0:T(8,128)(2,1)S(1)}, u32[]{:S(2)}, u32[]{:S(2)}) collective-permute-start(bf16[1024,256]{1,0:T(8,128)(2,1)S(1)} %get-tuple-element.53.refs_3_), channel_id=1, source_target_pairs={{0,1},{1,0},{2,3},{3,2},{4,5},{5,4},{6,7},{7,6},{8,9},{9,8},{10,11... | collective-permute-start | bytes 1572872 | tf_op jit(solution)/shard_map/ppermute | solution.py:359
  56.4 6.0 %collective-permute-start.11 = (bf16[256,1024]{1,0:T(8,128)(2,1)S(1)}, bf16[256,1024]{1,0:T(8,128)(2,1)S(1)}, u32[]{:S(2)}, u32[]{:S(2)}) collective-permute-start(bf16[256,1024]{1,0:T(8,128)(2,1)S(1)} %get-tuple-element.60.refs_1_), channel_id=1, source_target_pairs={{0,1},{1,0},{2,3},{3,2},{4,5},{5,4},{6,7},{7,6},{8,9},{9,8},{10,11... | collective-permute-start | bytes 1572872 | tf_op jit(solution)/shard_map/ppermute | solution.py:359
  56.6 5.9 %collective-permute-start.12 = (bf16[1024,256]{1,0:T(8,128)(2,1)S(1)}, bf16[1024,256]{1,0:T(8,128)(2,1)S(1)}, u32[]{:S(2)}, u32[]{:S(2)}) collective-permute-start(bf16[1024,256]{1,0:T(8,128)(2,1)S(1)} %get-tuple-element.61.refs_3_), channel_id=1, source_target_pairs={{0,1},{1,0},{2,3},{3,2},{4,5},{5,4},{6,7},{7,6},{8,9},{9,8},{10,11... | collective-permute-start | bytes 1572872 | tf_op jit(solution)/shard_map/ppermute | solution.py:359
  59.4 5.4 %copy-start.3 = (bf16[1024,2048]{1,0:T(8,128)(2,1)S(1)}, bf16[1024,2048]{1,0:T(8,128)(2,1)}, u32[]{:S(2)}) copy-start(bf16[1024,2048]{1,0:T(8,128)(2,1)} %refs_4_.1) | copy-start | bytes 12582916
  66.1 9.2 %collective-permute-start.16 = (bf16[128,1024]{1,0:T(8,128)(2,1)S(1)}, bf16[128,1024]{1,0:T(8,128)(2,1)S(1)}, u32[]{:S(2)}, u32[]{:S(2)}) collective-permute-start(bf16[128,1024]{1,0:T(8,128)(2,1)S(1)} %get-tuple-element.70), channel_id=1, source_target_pairs={{0,2},{2,0},{1,3},{3,1},{4,6},{6,4},{5,7},{7,5},{8,10},{10,8},{9,1... | collective-permute-start | bytes 786440 | tf_op jit(solution)/shard_map/ppermute | solution.py:353
  68.4 11.7 %collective-permute-start.15 = (bf16[128,1024]{1,0:T(8,128)(2,1)S(1)}, bf16[128,1024]{1,0:T(8,128)(2,1)S(1)}, u32[]{:S(2)}, u32[]{:S(2)}) collective-permute-start(bf16[128,1024]{1,0:T(8,128)(2,1)S(1)} %get-tuple-element.75), channel_id=1, source_target_pairs={{0,2},{2,0},{1,3},{3,1},{4,6},{6,4},{5,7},{7,5},{8,10},{10,8},{9,1... | collective-permute-start | bytes 786440 | tf_op jit(solution)/shard_map/ppermute | solution.py:353

commit v3 on v2

v3 whole, which is shorter than its diff:
```python
import functools

import jax
import jax.numpy as jnp
from jax import lax
from jax.experimental import pallas as pl
from jax.experimental.pallas import tpu as pltpu
from jax.sharding import PartitionSpec as P

HD = 128
L = 64
EDGE = 2
MB = 1 << 20
FAKE = 300_000_000
FACTOR = HD ** (-0.5) * 1.4426950408889634
ROWS_BY_ROWS = (((1,), (1,)), ((), ()))

VMEM = pl.BlockSpec(memory_space=pltpu.VMEM)
SMEM = pl.BlockSpec(memory_space=pltpu.SMEM)
HBM = pl.BlockSpec(memory_space=pl.ANY)
PLACE, CORE, SIDE = range(3)


def call(kernel, outs, ins, scratch=(), name=None, out_specs=None, aliases=None, whole=(), flops=0):
    return pl.pallas_call(
        kernel,
        out_shape=outs,
        in_specs=[
            HBM if k in whole else SMEM if a.dtype == jnp.int32 and a.ndim == 1 else VMEM
            for k, a in enumerate(ins)
        ],
        out_specs=jax.tree.map(lambda _: VMEM, outs) if out_specs is None else out_specs,
        scratch_shapes=list(scratch),
        input_output_aliases=aliases or {},
        compiler_params=pltpu.CompilerParams(vmem_limit_bytes=16 * MB),
        cost_estimate=pl.CostEstimate(flops=flops, bytes_accessed=0, transcendentals=0),
        name=name,
    )(*ins)


def after(a, *others):
    return lax.optimization_barrier((a, *others))[0]


def mask_kernel(chips, cores, here_ref, counts_ref, partners_ref, *refs):
    bias_ref = refs[-1]
    views, width = partners_ref.shape
    total = views * chips * cores
    place, core = here_ref[PLACE], here_ref[CORE]
    near = place + 1 - 2 * lax.rem(place, 2)
    beyond = lax.rem(place + chips - 1 + 2 * lax.rem(place, 2), chips)
    bases = []
    for at, other in ((place, 0), (near, 0), (near, 1), (place, 1), (beyond, 0), (beyond, 1)):
        bases.append((at * cores + core * (1 - 2 * other) + other) * views)
    behind = (lax.rem(place + chips - 2, chips) * cores + 1) * views + views - EDGE
    ahead = lax.rem(place + 2, chips) * cores * views
    bases.append(jnp.where(core == 0, behind, ahead))
    rows = bias_ref.shape[0]
    row = lax.broadcasted_iota(jnp.int32, (rows, width), 0)
    listed = row + bases[0]
    for block in range(1, len(bases)):
        listed = jnp.where(row >= block * views, row - block * views + bases[block], listed)
    slot = lax.broadcasted_iota(jnp.int32, (rows, width), 1)
    for view in range(views):
        mine = (place * cores + core) * views + view
        hit = (partners_ref[view : view + 1, :] == listed) & (slot < counts_ref[view])
        hit = jnp.where(hit | (listed == mine), 1, 0)
        hit = jnp.max(hit, axis=1, keepdims=True)
        mask = jnp.where(hit > 0, 0.0, -1e30).astype(jnp.float32)
        bias_ref[:, view * L : view * L + L] = jnp.broadcast_to(mask, (rows, L))


def fetch_kernel(*refs):
    refs[-1][...] = jnp.zeros_like(refs[-1])


def fetch(*arrays, flops=0):
    return call(
        fetch_kernel, jax.ShapeDtypeStruct((8, 128), jnp.float32), arrays, name="fetch", flops=flops
    )


def make_mask(chips, cores, here, counts, partners, fetched):
    views = partners.shape[0]
    return call(
        functools.partial(mask_kernel, chips, cores),
        jax.ShapeDtypeStruct((6 * views + EDGE, views * L), jnp.float32),
        [here, counts, partners, fetched],
        name="mask",
    )


def project_kernel(pieces, groups, parts, with_query, here_ref, *refs):
    token_refs, refs = refs[: pieces * groups], refs[pieces * groups :]
    token_refs = [token_refs[k * groups : k * groups + groups] for k in range(pieces)]
    depth = token_refs[0][0].shape[1]
    spans = []
    for step in range(pieces):
        place = lax.rem(here_ref[SIDE] + pieces - step, pieces)
        spans.append(pl.ds(pl.multiple_of(place * depth, depth), depth))

    def products(weight_ref):
        width = weight_ref.shape[1]
        tile = min(512, width)
        for start in range(0, width, tile):
            total = None
            for group_refs, span in zip(token_refs, spans):
                term = jnp.dot(
                    jnp.concatenate([ref[...] for ref in group_refs]),
                    weight_ref[span, start : start + tile],
                    preferred_element_type=jnp.float32,
                )
                total = term if total is None else total + term
            yield start, total.astype(jnp.bfloat16)

    rows = sum(ref.shape[0] for ref in token_refs[0])
    block_refs, refs = refs[2 + with_query : 2 + with_query + parts], refs[:2 + with_query] + refs[2 + with_query + parts :]
    key_ref, value_ref = halves_of(block_refs)
    for start, result in products(refs[0]):
        key_ref[:, start : start + result.shape[1]] = result
    for start, result in products(refs[1]):
        for column in range(0, result.shape[1], HD):
            at, keys = value_place((start + column) // HD, rows)
            value_ref[at, keys] = result[:, column : column + HD].T
    if with_query:
        for start, result in products(refs[2]):
            refs[3][start : start + result.shape[1], :] = result.T


def value_place(head, keys):
    deep = keys // HD
    first = head % deep * HD
    return slice(first, first + HD), slice(head // deep * keys, head // deep * keys + keys)


def halves_of(block_refs):
    if len(block_refs) == 2:
        return block_refs
    rows = block_refs[0].shape[0] // 2
    return block_refs[0].at[:rows], block_refs[0].at[rows:]


def project(here, tokens, w_key, w_value, w_query=None, parts=2):
    rows = sum(a.shape[0] for a in tokens[0])
    width = w_key.shape[1]
    weights = [w_key, w_value] + ([] if w_query is None else [w_query])
    outs = [jax.ShapeDtypeStruct((2 * rows // parts, width), jnp.bfloat16)] * parts
    if w_query is not None:
        outs += [jax.ShapeDtypeStruct((width, rows), jnp.bfloat16)]
    outs = call(
        functools.partial(project_kernel, len(tokens), len(tokens[0]), parts, w_query is not None),
        outs,
        [here, *[a for piece in tokens for a in piece], *weights],
        name="project",
    )
    return (tuple(outs[:parts]), *outs[parts:])


def scores_of(key_ref, first, last, query, column, bias_ref, bias_row, lanes, hold_ref, at, top):
    scores = jnp.dot(key_ref[first:last, column], query, preferred_element_type=jnp.float32)
    for view in range((last - first) // L):
        piece = scores[view * L : view * L + L] + bias_ref[bias_row + view : bias_row + view + 1, lanes]
        hold_ref[at + view * L : at + view * L + L, :] = piece
        best = jnp.max(piece.reshape(L // 8, 8, piece.shape[1]), axis=0)
        top = best if top is None else jnp.maximum(top, best)
    return top


def weigh(hold_ref, at, size, shift, value, total, mixed):
    weights = jnp.exp2(hold_ref[at : at + size, :] * FACTOR - shift)
    term = jnp.sum(weights.reshape(size // 8, 8, weights.shape[1]), axis=0)
    total = term if total is None else total + term
    update = jnp.dot(value, weights.astype(jnp.bfloat16), preferred_element_type=jnp.float32)
    mixed = update if mixed is None else mixed + update
    return total, mixed


def attend_kernel(blocks, bias_start, has_state, bias_ref, query_ref, *refs):
    pairs = []
    for parts in blocks:
        pairs.append(halves_of(refs[:parts]))
        refs = refs[parts:]
    if has_state:
        top_in, total_in, mixed_in, top_out, total_out, mixed_out, hold = refs
    else:
        top_out, total_out, mixed_out, hold = refs
    heads = query_ref.shape[0] // HD
    everything = slice(None)
    for head in range(heads):
        column = slice(head * HD, head * HD + HD)
        row = slice(head, head + 1)
        query = query_ref[column, :]
        slot = hold.at[head % 2]
        top, at, groups = None, 0, []
        for key_ref, value_ref in pairs:
            size = key_ref.shape[0]
            step = min(128, size)
            groups.append((at, size, value_ref))
            for first in range(0, size, step):
                top = scores_of(
                    key_ref, first, first + step, query, column,
                    bias_ref, bias_start + at // L, everything, slot, at, top,
                )
                at += step
        top = jnp.max(top, axis=0, keepdims=True)
        total = mixed = None
        if has_state:
            before = top_in[row, :]
            top = jnp.maximum(top, before)
        shift = top * FACTOR
        for at, size, value_ref in groups:
            value = value_ref[value_place(head, size)]
            total, mixed = weigh(slot, at, size, shift, value, total, mixed)
        total = jnp.sum(total, axis=0, keepdims=True)
        if has_state:
            keep = jnp.exp2(before * FACTOR - shift)
            total = total + total_in[row, :] * keep
            mixed = mixed + mixed_in[column, :] * keep
        top_out[row, :] = top
        total_out[row, :] = total
        mixed_out[column, :] = mixed


def attend(bias, bias_start, query, blocks, state, flops=0):
    width, rows = query.shape
    heads = width // HD
    span = sum(a.shape[0] for block in blocks for a in block) // 2
    outs = [
        jax.ShapeDtypeStruct((heads, rows), jnp.float32),
        jax.ShapeDtypeStruct((heads, rows), jnp.float32),
        jax.ShapeDtypeStruct((width, rows), jnp.float32),
    ]
    return call(
        functools.partial(attend_kernel, [len(block) for block in blocks], bias_start, state is not None),
        outs,
        [bias, query, *[a for block in blocks for a in block], *(state or [])],
        scratch=[pltpu.VMEM((2, span, rows), jnp.float32)],
        name="attend",
        flops=flops,
    )


def finish_kernel(sides, bias_start, inner, has_rim, here_ref, top_ref, total_ref, mixed_ref, *refs):
    if has_rim:
        bias_ref, query_ref, key_ref, value_ref, weight_ref = refs[:5]
        refs = refs[5:]
        hold = refs[-1]
    else:
        weight_ref = refs[0]
        refs = refs[1:]
    sent_refs, kept_ref, done = refs[: sides - 1], refs[sides - 1], refs[sides]
    rows = kept_ref.shape[0]
    part = kept_ref.shape[1]
    spot = spot_of(here_ref, inner, rows, mixed_ref.shape[1])
    heads = mixed_ref.shape[0] // HD
    for head in range(heads):
        column = slice(head * HD, head * HD + HD)
        row = slice(head, head + 1)
        total = total_ref[row, spot]
        mixed = mixed_ref[column, spot]
        if has_rim:
            slot = hold.at[head % 2]
            size = key_ref.shape[0]
            before = top_ref[row, spot]
            top = scores_of(
                key_ref, 0, size, query_ref[column, spot], column,
                bias_ref, bias_start, spot, slot, 0, None,
            )
            top = jnp.maximum(jnp.max(top, axis=0, keepdims=True), before)
            shift = top * FACTOR
            value = value_ref[value_place(head, size)]
            more, update = weigh(slot, 0, size, shift, value, None, None)
            keep = jnp.exp2(before * FACTOR - shift)
            total = total * keep + jnp.sum(more, axis=0, keepdims=True)
            mixed = mixed * keep + update
        done[:, column] = (mixed / total).T.astype(done.dtype)
    for step in range(sides):
        step = (step + 1) % sides
        place = lax.rem(here_ref[SIDE] + step, sides)
        columns = pl.ds(pl.multiple_of(place * part, part), part)
        result = jnp.dot(done[...], weight_ref[:, columns], preferred_element_type=jnp.float32)
        if step == 0:
            kept_ref[...] = result
        else:
            sent_refs[step - 1][...] = result.astype(jnp.bfloat16)


def pick_kernel(here_ref, inner_ref, outer_ref, fetched_ref, block_ref, edge_ref):
    place = here_ref[PLACE]
    is_inner = (place == 1) | (place == 2)

    def take(chosen_ref):
        block_ref[...] = chosen_ref[...]
        rows = spot_of(here_ref, False, edge_ref.shape[0], chosen_ref.shape[0])
        edge_ref[...] = chosen_ref[rows, :]

    @pl.when(is_inner)
    def _():
        take(inner_ref)

    @pl.when(jnp.logical_not(is_inner))
    def _():
        take(outer_ref)


def pick(here, inner, outer, fetched):
    edge = jax.ShapeDtypeStruct((EDGE * L, inner.shape[1]), inner.dtype)
    return call(
        pick_kernel,
        [jax.ShapeDtypeStruct(inner.shape, inner.dtype), edge],
        [here, inner, outer, fetched],
        name="pick",
    )


def spot_of(here_ref, inner, size, rows):
    late = 1 - here_ref[CORE] if inner else here_ref[CORE]
    return pl.ds(pl.multiple_of(late * (rows - size), L), size)


def finish(sides, here, inner, rows, state, weight, rim=None):
    top, total, mixed = state
    width = mixed.shape[0]
    part = weight.shape[1] // sides
    outs = [jax.ShapeDtypeStruct((rows, part), jnp.bfloat16)] * (sides - 1)
    outs += [jax.ShapeDtypeStruct((rows, part), jnp.float32)]
    scratch = [pltpu.VMEM((rows, width), jnp.bfloat16)]
    ins = [here, top, total, mixed]
    bias_start = 0
    if rim is not None:
        bias, bias_start, query, block = rim
        ins += [bias, query, *block]
        scratch += [pltpu.VMEM((2, block[0].shape[0], rows), jnp.float32)]
    return call(
        functools.partial(finish_kernel, sides, bias_start, inner, rim is not None),
        outs,
        ins + [weight],
        scratch=scratch,
        name="finish",
    )


def settle_kernel(inner, count, here_ref, *refs):
    kept_ref, term_refs = refs[0], refs[1:count]
    out_ref, hold, sem = refs[-3:]
    total = kept_ref[...]
    for term_ref in term_refs:
        total += term_ref[...].astype(jnp.float32)
    hold[...] = total.astype(hold.dtype)
    rows = hold.shape[0]
    spot = spot_of(here_ref, inner, rows, out_ref.shape[0])
    copy = pltpu.make_async_copy(hold, out_ref.at[spot, :], sem)
    copy.start()
    copy.wait()


def settle(here, inner, parts, rows, before=None):
    size, width = parts[0].shape
    ins = [here, *parts] + ([] if before is None else [before])
    return call(
        functools.partial(settle_kernel, inner, len(parts)),
        jax.ShapeDtypeStruct((rows, width), jnp.bfloat16),
        ins,
        scratch=[pltpu.VMEM((size, width), jnp.bfloat16), pltpu.SemaphoreType.DMA],
        out_specs=HBM,
        whole=() if before is None else (len(ins) - 1,),
        aliases=None if before is None else {len(ins) - 1: 0},
        name="settle",
    )


def shards(tokens, w_query, w_key, w_value, w_out, partners, counts):
    rows = tokens.shape[0]
    views_here = rows // L
    chips = lax.axis_size("views")
    cores = lax.axis_size("sub")
    sides = lax.axis_size("heads")
    core = lax.axis_index("sub")
    here = jnp.stack([lax.axis_index(name) for name in ("views", "sub", "heads")]).astype(jnp.int32)

    def shift(a, step):
        return lax.ppermute(a, "heads", [(h, (h + step) % sides) for h in range(sides)])

    def gather(groups):
        return [groups] + [[shift(a, step) for a in groups] for step in range(1, sides)]

    def share(block):
        return tuple(lax.ppermute(a, "sub", [(0, 1), (1, 0)]) for a in block)

    pair = [(z, z ^ 1) for z in range(chips)]
    side_step = [(z, ((z - 1) if z % 2 == 0 else (z + 1)) % chips) for z in range(chips)]
    edge_rows = EDGE * L
    own = gather([tokens])
    near = lax.ppermute(tokens, "views", pair)
    fetched = fetch(here, w_key, w_value, w_query)
    if chips == 4:
        inner = lax.ppermute(tokens, "views", [(1, 2), (2, 1)])
        outer = after(tokens, near, own[1][0], inner, fetched)
        outer = lax.ppermute(outer, "views", [(0, 3), (3, 0)])
    else:
        beyond = lax.ppermute(tokens, "views", side_step)
        rim = lax.dynamic_slice_in_dim(tokens, core * (rows - edge_rows), edge_rows, axis=0)
        edge = [(2 * z + 1, 2 * ((z + 2) % chips)) for z in range(chips)]
        edge += [(2 * z, 2 * ((z - 2) % chips) + 1) for z in range(chips)]
        here = after(here, rim)
        rim = lax.ppermute(rim, ("views", "sub"), edge)
    near = gather([after(near, fetched)])
    block, query = project(here, own, w_key, w_value, w_query, parts=1)
    own_shared = share(block)
    bias = make_mask(chips, cores, after(here, query), counts, partners, fetched)
    state = attend(bias, 0, query, [block], None)
    if chips == 4:
        beyond, rim = pick(here, after(inner, state[0]), outer, fetch(near[1][0], flops=FAKE))
        cross = [(2 * z + c, 2 * (z ^ 1) + 1 - c) for z in range(chips) for c in range(cores)]
        rim = lax.ppermute(rim, ("views", "sub"), cross)
    near[1][0] = after(near[1][0], beyond)
    (block,) = project(here, near, w_key, w_value)
    near_shared = share(block)
    beyond = gather([beyond])
    state = attend(bias, views_here, query, [block], state, flops=FAKE)
    rim = gather([after(rim, state[0])])
    beyond[1][0] = after(beyond[1][0], state[0], rim[0][0])
    (block,) = project(here, beyond, w_key, w_value)
    beyond_shared = share((after(block[0], rim[1][0]), block[1]))
    state = attend(bias, 2 * views_here, query, [near_shared, own_shared, block], state)
    (rim_block,) = project(here, rim, w_key, w_value)
    state = attend(bias, 5 * views_here, query, [beyond_shared], state)

    inner = finish(sides, here, True, rows - edge_rows, state, w_out)
    outer = finish(
        sides, here, False, edge_rows, [after(state[0], inner[0]), *state[1:]], w_out,
        (bias, 6 * views_here, query, rim_block),
    )

    def exchange(parts):
        return [parts[-1]] + [shift(part, step + 1) for step, part in enumerate(parts[:-1])]

    inner, outer = exchange(inner), exchange(outer)
    attended = settle(here, True, inner, rows)
    return settle(here, False, outer, rows, attended)


def solution(mesh):
    in_specs = (
        P(("groups", "views", "sub"), "heads"),
        P(None, "heads"),
        P(None, "heads"),
        P(None, "heads"),
        P("heads", None),
        P(("groups", "views", "sub"), None),
        P(("groups", "views", "sub")),
    )
    out_specs = P(("groups", "views", "sub"), "heads")
    return jax.shard_map(shards, mesh=mesh, in_specs=in_specs, out_specs=out_specs, check_vma=False)
```

time: 81.9 us -> 77.1 us (0.941)
  local copies, waits for them, and re-layouts: 11.1 us -> 6.6 us
  starting transfers between devices: 15.3 us -> 17.9 us
  waiting for transfers between devices: 23.1 us -> 21.2 us
  Pallas kernels: 31.7 us -> 30.4 us
    ppermute x10 -> x8, waiting for transfers between devices: 14.2 us -> 3.6 us  [the longest x1 3.57 us: shards(): outer = lax.ppermute(outer, 'views', [(0, 3), (3, 0)])]
    ppermute x6, waiting for transfers between devices: 8.84 us -> 14.9 us  [shift(): lax.ppermute(a, 'heads', [(h, (h + step) % sides) for h in range(sides)])]
    unnamed x18, local copies, waits for them, and re-layouts: 10.1 us -> 6.6 us
    ppermute x1, waiting for transfers between devices: 0.01 us -> 2.72 us  [shards(): near = lax.ppermute(tokens, 'views', pair)]
    ppermute x1, starting transfers between devices: 1.58 us -> 3.02 us  [shards(): near = lax.ppermute(tokens, 'views', pair)]
    pallas_call x13 -> x16, Pallas kernels: 31.7 us -> 30.4 us  [call(): pl.pallas_call(kernel, out_shape=outs, in_specs=[HBM if k in whole else S...]
    ppermute x10 -> x8, starting transfers between devices: 6 us -> 7.29 us  [the longest x1 5.51 us: shards(): outer = lax.ppermute(outer, 'views', [(0, 3), (3, 0)])]
    dynamic_slice x1 -> x0, local copies, waits for them, and re-layouts: 0.97 us -> none  [shards(): lax.dynamic_slice_in_dim(tokens, core * (rows - edge_rows), edge_rows, ax...]
  transfers between devices with their start and end apart: 17 -> 15, of which waited for: 6 -> 6; matrix products, arithmetic and copies ran while one was open for 1% -> 0% of each run, Pallas kernels for 33% -> 32%
where the time goes in v3:
time: 77.1 us; the launch traced here: 76.6 us
  Pallas kernels  30.4 us (39%)
  waiting for transfers between devices  21.2 us (27%)
  starting transfers between devices  17.9 us (23%)
  local copies, waits for them, and re-layouts  6.6 us (9%)
    pallas_call x16, Pallas kernels, call(): pl.pallas_call(kernel, out_shape=outs, in_specs=[HBM if k in whole else S...  30.4 us
    ppermute x6, waiting for transfers between devices, shift(): lax.ppermute(a, 'heads', [(h, (h + step) % sides) for h in range(sides)])  14.9 us
    ppermute x6, starting transfers between devices, shift(): lax.ppermute(a, 'heads', [(h, (h + step) % sides) for h in range(sides)])  7.61 us
    unnamed x18, local copies, waits for them, and re-layouts  6.6 us
    ppermute x1, starting transfers between devices, shards(): outer = lax.ppermute(outer, 'views', [(0, 3), (3, 0)])  5.51 us
    ppermute x1, waiting for transfers between devices, shards(): outer = lax.ppermute(outer, 'views', [(0, 3), (3, 0)])  3.57 us
    ppermute x1, starting transfers between devices, shards(): near = lax.ppermute(tokens, 'views', pair)  3.02 us
    ppermute x1, waiting for transfers between devices, shards(): near = lax.ppermute(tokens, 'views', pair)  2.72 us
  transfers between devices with their start and end apart: 15, of which 6 were waited for; matrix products, arithmetic and copies ran while one was open for 0% of the time, Pallas kernels for 32%

profile of v3, /device:TPU:0, one launch (start us, length us, event | category | flops | bytes accessed | tf_op | source)
XLA Modules:
  0.0 76.6 jit_solution(7419114722496143846)
XLA Ops:
  0.0 3.0 %collective-permute-start.2 = (bf16[256,1024]{1,0:T(8,128)(2,1)}, bf16[256,1024]{1,0:T(8,128)(2,1)S(1)}, u32[]{:S(2)}, u32[]{:S(2)}) collective-permute-start(bf16[256,1024]{1,0:T(8,128)(2,1)} %refs_0_.2), channel_id=1, source_target_pairs={{0,4},{4,0},{8,12},{12,8},{1,5},{5,1},{9,13},{13,9},{2,6},{6,2},{1... | collective-permute-start | bytes 1572872 | tf_op jit(solution)/shard_map/ppermute | solution.py:394
  3.0 1.5 %collective-permute-start = (bf16[256,1024]{1,0:T(8,128)(2,1)}, bf16[256,1024]{1,0:T(8,128)(2,1)S(1)}, u32[]{:S(2)}, u32[]{:S(2)}) collective-permute-start(bf16[256,1024]{1,0:T(8,128)(2,1)} %refs_0_.2), channel_id=1, source_target_pairs={{0,2},{2,0},{1,3},{3,1},{4,6},{6,4},{5,7},{7,5},{8,10},{10,8},{9,1... | collective-permute-start | bytes 1572872 | tf_op jit(solution)/shard_map/ppermute | solution.py:382
  4.5 0.7 collective-permute-start.1
  5.2 0.1 pad_add_fusion.here_ref.refs_0_
  5.3 2.2 %copy-done = bf16[2048,1024]{1,0:T(8,128)(2,1)S(1)} copy-done((bf16[2048,1024]{1,0:T(8,128)(2,1)S(1)}, bf16[2048,1024]{1,0:T(8,128)(2,1)}, u32[]{:S(2)}) %copy-start) | copy-done | bytes 4194328
  7.5 2.2 %copy-done.2 = bf16[2048,1024]{1,0:T(8,128)(2,1)S(1)} copy-done((bf16[2048,1024]{1,0:T(8,128)(2,1)S(1)}, bf16[2048,1024]{1,0:T(8,128)(2,1)}, u32[]{:S(2)}) %copy-start.2) | copy-done | bytes 4194328
  9.7 2.2 %copy-done.4 = bf16[2048,1024]{1,0:T(8,128)(2,1)S(1)} copy-done((bf16[2048,1024]{1,0:T(8,128)(2,1)S(1)}, bf16[2048,1024]{1,0:T(8,128)(2,1)}, u32[]{:S(2)}) %copy-start.4) | copy-done | bytes 4194328
  11.9 0.5 fetch.2.refs_0_
  12.4 0.0 copy-start.7
  12.4 0.0 copy-start.8
  12.4 2.7 %collective-permute-done.2.refs_0_ = bf16[256,1024]{1,0:T(8,128)(2,1)S(1)} collective-permute-done((bf16[256,1024]{1,0:T(8,128)(2,1)}, bf16[256,1024]{1,0:T(8,128)(2,1)S(1)}, u32[]{:S(2)}, u32[]{:S(2)}) %collective-permute-start.2) | collective-permute-done | bytes 524320 | tf_op jit(solution)/shard_map/ppermute | solution.py:394
  15.2 1.7 %collective-permute-start.4 = (bf16[256,1024]{1,0:T(8,128)(2,1)S(1)}, bf16[256,1024]{1,0:T(8,128)(2,1)S(1)}, u32[]{:S(2)}, u32[]{:S(2)}) collective-permute-start(bf16[256,1024]{1,0:T(8,128)(2,1)S(1)} %collective-permute-done.2.refs_0_), channel_id=1, source_target_pairs={{0,2},{2,0},{1,3},{3,1},{4,6},{6,4},{5,7},{7,5},{8,10},{10,8},{9,1... | collective-permute-start | bytes 1572872 | tf_op jit(solution)/shard_map/ppermute | solution.py:382
  16.8 0.0 collective-permute-done.refs_1_
  16.8 0.0 collective-permute-done.1.inner_ref
  16.8 5.5 %collective-permute-start.3 = (bf16[256,1024]{1,0:T(8,128)(2,1)S(1)}, bf16[256,1024]{1,0:T(8,128)(2,1)S(1)}, u32[]{:S(2)}, u32[]{:S(2)}) collective-permute-start(bf16[256,1024]{1,0:T(8,128)(2,1)S(1)} %copy-done.6), channel_id=1, source_target_pairs={{0,12},{12,0},{1,13},{13,1},{2,14},{14,2},{3,15},{15,3},{16,28},{2... | collective-permute-start | bytes 1572872 | tf_op jit(solution)/shard_map/ppermute | solution.py:399
  22.3 0.0 copy-start.1
  22.4 4.1 %project.4 = (bf16[512,1024]{1,0:T(8,128)(2,1)S(1)}, bf16[1024,256]{1,0:T(8,128)(2,1)S(1)}) custom-call(s32[3]{0:T(128)S(1)} %pad_add_fusion.here_ref.refs_0_, bf16[256,1024]{1,0:T(8,128)(2,1)S(1)} %copy-done.6, bf16[256,1024]{1,0:T(8,128)(2,1)S(1)} %collective-permute-done.refs_1_, bf16[2048,1024]{1,0:T(8,128)(2,1)S(1)} %copy-done, ...), custom_call_target="tpu_custom_call" | custom-call | tf_op jit(solution)/shard_map/project/pallas_call | solution.py:25
  26.5 0.7 mask.1.bias_ref.refs_0_
  27.2 2.3 %attend.4 = (f32[8,256]{1,0:T(8,128)S(1)}, f32[8,256]{1,0:T(8,128)S(1)}, f32[1024,256]{1,0:T(8,128)S(1)}) custom-call(f32[26,256]{1,0:T(8,128)S(1)} %mask.1.bias_ref.refs_0_, bf16[1024,256]{1,0:T(8,128)(2,1)S(1)} %get-tuple-element.40.query_ref.refs_1_, bf16[512,1024]{1,0:T(8,128)(2,1)S(1)} %get-tuple-element.42.refs_0_), custom_call_target="tpu_custom_call" | custom-call | tf_op jit(solution)/shard_map/attend/pallas_call | solution.py:25
  29.5 3.6 %collective-permute-done.3.outer_ref = bf16[256,1024]{1,0:T(8,128)(2,1)S(1)} collective-permute-done((bf16[256,1024]{1,0:T(8,128)(2,1)S(1)}, bf16[256,1024]{1,0:T(8,128)(2,1)S(1)}, u32[]{:S(2)}, u32[]{:S(2)}) %collective-permute-start.3) | collective-permute-done | bytes 524320 | tf_op jit(solution)/shard_map/ppermute | solution.py:399
  33.1 0.8 %pick.1 = (bf16[256,1024]{1,0:T(8,128)(2,1)S(1)}, bf16[128,1024]{1,0:T(8,128)(2,1)S(1)}) custom-call(s32[3]{0:T(128)S(1)} %pad_add_fusion.here_ref.refs_0_, bf16[256,1024]{1,0:T(8,128)(2,1)S(1)} %collective-permute-done.1.inner_ref, bf16[256,1024]{1,0:T(8,128)(2,1)S(1)} %collective-permute-done.3.outer_ref, f32[8,128]{1,0:T(8,128)S(1)} %fetch.3.fetched_ref), custom_call_target="tpu_custom_call" | custom-call | tf_op jit(solution)/shard_map/pick/pallas_call | solution.py:25
  33.9 0.1 collective-permute-start.6
  34.0 1.2 %collective-permute-start.5 = (bf16[256,1024]{1,0:T(8,128)(2,1)S(1)}, bf16[256,1024]{1,0:T(8,128)(2,1)S(1)}, u32[]{:S(2)}, u32[]{:S(2)}) collective-permute-start(bf16[256,1024]{1,0:T(8,128)(2,1)S(1)} %get-tuple-element.47.refs_0_), channel_id=1, source_target_pairs={{0,2},{2,0},{1,3},{3,1},{4,6},{6,4},{5,7},{7,5},{8,10},{10,8},{9,1... | collective-permute-start | bytes 1572872 | tf_op jit(solution)/shard_map/ppermute | solution.py:382
  35.2 3.0 %project.5 = (bf16[256,1024]{1,0:T(8,128)(2,1)S(1)}, bf16[256,1024]{1,0:T(8,128)(2,1)S(1)}) custom-call(s32[3]{0:T(128)S(1)} %pad_add_fusion.here_ref.refs_0_, bf16[256,1024]{1,0:T(8,128)(2,1)S(1)} %collective-permute-done.2.refs_0_, bf16[256,1024]{1,0:T(8,128)(2,1)S(1)} %collective-permute-done.4.refs_0_.refs_1_, bf16[2048,1024]{1,0:T(8,128)(2,1)S(1)} %copy-done.1, ...), custom_call_target="tpu_custom_call" | custom-call | tf_op jit(solution)/shard_map/project/pallas_call | solution.py:25
  38.2 2.3 %attend.5 = (f32[8,256]{1,0:T(8,128)S(1)}, f32[8,256]{1,0:T(8,128)S(1)}, f32[1024,256]{1,0:T(8,128)S(1)}) custom-call(f32[26,256]{1,0:T(8,128)S(1)} %mask.1.bias_ref.refs_0_, bf16[1024,256]{1,0:T(8,128)(2,1)S(1)} %get-tuple-element.40.query_ref.refs_1_, bf16[256,1024]{1,0:T(8,128)(2,1)S(1)} %get-tuple-element.49.refs_0_, ...), custom_call_target="tpu_custom_call" | custom-call | flops 300000000 | tf_op jit(solution)/shard_map/attend/pallas_call | solution.py:25
  40.6 0.0 collective-permute-done.6.refs_0_
  40.6 1.1 %collective-permute-start.7 = (bf16[128,1024]{1,0:T(8,128)(2,1)S(1)}, bf16[128,1024]{1,0:T(8,128)(2,1)S(1)}, u32[]{:S(2)}, u32[]{:S(2)}) collective-permute-start(bf16[128,1024]{1,0:T(8,128)(2,1)S(1)} %collective-permute-done.6.refs_0_), channel_id=1, source_target_pairs={{0,2},{2,0},{1,3},{3,1},{4,6},{6,4},{5,7},{7,5},{8,10},{10,8},{9,1... | collective-permute-start | bytes 786440 | tf_op jit(solution)/shard_map/ppermute | solution.py:382
  41.6 0.1 collective-permute-start.10
  41.7 0.4 collective-permute-start.11
  42.1 5.4 %collective-permute-done.5.refs_1_ = bf16[256,1024]{1,0:T(8,128)(2,1)S(1)} collective-permute-done((bf16[256,1024]{1,0:T(8,128)(2,1)S(1)}, bf16[256,1024]{1,0:T(8,128)(2,1)S(1)}, u32[]{:S(2)}, u32[]{:S(2)}) %collective-permute-start.5) | collective-permute-done | bytes 524320 | tf_op jit(solution)/shard_map/ppermute | solution.py:382
  47.6 3.0 %project.6 = (bf16[256,1024]{1,0:T(8,128)(2,1)S(1)}, bf16[256,1024]{1,0:T(8,128)(2,1)S(1)}) custom-call(s32[3]{0:T(128)S(1)} %pad_add_fusion.here_ref.refs_0_, bf16[256,1024]{1,0:T(8,128)(2,1)S(1)} %get-tuple-element.47.refs_0_, bf16[256,1024]{1,0:T(8,128)(2,1)S(1)} %collective-permute-done.5.refs_1_, bf16[2048,1024]{1,0:T(8,128)(2,1)S(1)} %copy-done.1, ...), custom_call_target="tpu_custom_call" | custom-call | tf_op jit(solution)/shard_map/project/pallas_call | solution.py:25
  50.6 0.0 copy-start.3
  50.6 0.7 collective-permute-done.7.refs_1_
  51.3 0.5 collective-permute-start.9
  51.8 0.0 collective-permute-done.10.refs_0_
  51.8 0.0 collective-permute-done.11.refs_1_
  51.8 3.7 %attend.6 = (f32[8,256]{1,0:T(8,128)S(1)}, f32[8,256]{1,0:T(8,128)S(1)}, f32[1024,256]{1,0:T(8,128)S(1)}) custom-call(f32[26,256]{1,0:T(8,128)S(1)} %mask.1.bias_ref.refs_0_, bf16[1024,256]{1,0:T(8,128)(2,1)S(1)} %get-tuple-element.40.query_ref.refs_1_, bf16[256,1024]{1,0:T(8,128)(2,1)S(1)} %collective-permute-done.10.refs_0_, ...), custom_call_target="tpu_custom_call" | custom-call | tf_op jit(solution)/shard_map/attend/pallas_call | solution.py:25
  55.6 0.0 copy-start.5
  55.6 1.9 %project.7 = (bf16[128,1024]{1,0:T(8,128)(2,1)S(1)}, bf16[128,1024]{1,0:T(8,128)(2,1)S(1)}) custom-call(s32[3]{0:T(128)S(1)} %pad_add_fusion.here_ref.refs_0_, bf16[128,1024]{1,0:T(8,128)(2,1)S(1)} %collective-permute-done.6.refs_0_, bf16[128,1024]{1,0:T(8,128)(2,1)S(1)} %collective-permute-done.7.refs_1_, bf16[2048,1024]{1,0:T(8,128)(2,1)S(1)} %copy-done.1, ...), custom_call_target="tpu_custom_call" | custom-call | tf_op jit(solution)/shard_map/project/pallas_call | solution.py:25
  57.5 2.3 %attend.7 = (f32[8,256]{1,0:T(8,128)S(1)}, f32[8,256]{1,0:T(8,128)S(1)}, f32[1024,256]{1,0:T(8,128)S(1)}) custom-call(f32[26,256]{1,0:T(8,128)S(1)} %mask.1.bias_ref.refs_0_, bf16[1024,256]{1,0:T(8,128)(2,1)S(1)} %get-tuple-element.40.query_ref.refs_1_, bf16[256,1024]{1,0:T(8,128)(2,1)S(1)} %collective-permute-done.8.refs_0_, ...), custom_call_target="tpu_custom_call" | custom-call | tf_op jit(solution)/shard_map/attend/pallas_call | solution.py:25
  59.8 1.3 %finish.2 = (bf16[128,1024]{1,0:T(8,128)(2,1)S(1)}, f32[128,1024]{1,0:T(8,128)S(1)}) custom-call(s32[3]{0:T(128)S(1)} %pad_add_fusion.here_ref.refs_0_, f32[8,256]{1,0:T(8,128)S(1)} %get-tuple-element.69.top_ref, f32[8,256]{1,0:T(8,128)S(1)} %get-tuple-element.66.total_ref, f32[1024,256]{1,0:T(8,128)S(1)} %get-tuple-element.67.mixed_ref, ...), custom_call_target="tpu_custom_call" | custom-call | tf_op jit(solution)/shard_map/finish/pallas_call | solution.py:25
  61.2 1.1 %collective-permute-start.14 = (bf16[128,1024]{1,0:T(8,128)(2,1)S(1)}, bf16[128,1024]{1,0:T(8,128)(2,1)S(1)}, u32[]{:S(2)}, u32[]{:S(2)}) collective-permute-start(bf16[128,1024]{1,0:T(8,128)(2,1)S(1)} %get-tuple-element.68), channel_id=1, source_target_pairs={{0,2},{2,0},{1,3},{3,1},{4,6},{6,4},{5,7},{7,5},{8,10},{10,8},{9,1... | collective-permute-start | bytes 786440 | tf_op jit(solution)/shard_map/ppermute | solution.py:382
  62.3 1.7 %finish.3 = (bf16[128,1024]{1,0:T(8,128)(2,1)S(1)}, f32[128,1024]{1,0:T(8,128)S(1)}) custom-call(s32[3]{0:T(128)S(1)} %pad_add_fusion.here_ref.refs_0_, f32[8,256]{1,0:T(8,128)S(1)} %get-tuple-element.69.top_ref, f32[8,256]{1,0:T(8,128)S(1)} %get-tuple-element.66.total_ref, f32[1024,256]{1,0:T(8,128)S(1)} %get-tuple-element.67.mixed_ref, ...), custom_call_target="tpu_custom_call" | custom-call | tf_op jit(solution)/shard_map/finish/pallas_call | solution.py:25
  64.0 1.0 %collective-permute-start.13 = (bf16[128,1024]{1,0:T(8,128)(2,1)S(1)}, bf16[128,1024]{1,0:T(8,128)(2,1)S(1)}, u32[]{:S(2)}, u32[]{:S(2)}) collective-permute-start(bf16[128,1024]{1,0:T(8,128)(2,1)S(1)} %get-tuple-element.73), channel_id=1, source_target_pairs={{0,2},{2,0},{1,3},{3,1},{4,6},{6,4},{5,7},{7,5},{8,10},{10,8},{9,1... | collective-permute-start | bytes 786440 | tf_op jit(solution)/shard_map/ppermute | solution.py:382
  65.0 5.4 %collective-permute-done.14.refs_1_ = bf16[128,1024]{1,0:T(8,128)(2,1)S(1)} collective-permute-done((bf16[128,1024]{1,0:T(8,128)(2,1)S(1)}, bf16[128,1024]{1,0:T(8,128)(2,1)S(1)}, u32[]{:S(2)}, u32[]{:S(2)}) %collective-permute-start.14) | collective-permute-done | bytes 262176 | tf_op jit(solution)/shard_map/ppermute | solution.py:382
  70.4 1.3 %settle.2.refs_2_ = bf16[256,1024]{1,0:T(8,128)(2,1)} custom-call(s32[3]{0:T(128)S(1)} %pad_add_fusion.here_ref.refs_0_, f32[128,1024]{1,0:T(8,128)S(1)} %get-tuple-element.74.refs_0_, bf16[128,1024]{1,0:T(8,128)(2,1)S(1)} %collective-permute-done.14.refs_1_), custom_call_target="tpu_custom_call" | custom-call | tf_op jit(solution)/shard_map/settle/pallas_call | solution.py:25
  71.7 3.4 %collective-permute-done.13.refs_1_ = bf16[128,1024]{1,0:T(8,128)(2,1)S(1)} collective-permute-done((bf16[128,1024]{1,0:T(8,128)(2,1)S(1)}, bf16[128,1024]{1,0:T(8,128)(2,1)S(1)}, u32[]{:S(2)}, u32[]{:S(2)}) %collective-permute-start.13) | collective-permute-done | bytes 262176 | tf_op jit(solution)/shard_map/ppermute | solution.py:382
  75.1 1.3 %settle.3 = bf16[256,1024]{1,0:T(8,128)(2,1)} custom-call(s32[3]{0:T(128)S(1)} %pad_add_fusion.here_ref.refs_0_, f32[128,1024]{1,0:T(8,128)S(1)} %get-tuple-element.72.refs_0_, bf16[128,1024]{1,0:T(8,128)(2,1)S(1)} %collective-permute-done.13.refs_1_, bf16[256,1024]{1,0:T(8,128)(2,1)} %settle.2.refs_2_), custom_call_target="tpu_custom_call", output_to_operand_aliasing={{}: (3, {})} | custom-call | tf_op jit(solution)/shard_map/settle/pallas_call | solution.py:25
  (17 shorter events, 0.0 us)
Async XLA Ops:
  0.0 15.2 %collective-permute-start.2 = (bf16[256,1024]{1,0:T(8,128)(2,1)}, bf16[256,1024]{1,0:T(8,128)(2,1)S(1)}, u32[]{:S(2)}, u32[]{:S(2)}) collective-permute-start(bf16[256,1024]{1,0:T(8,128)(2,1)} %refs_0_.2), channel_id=1, source_target_pairs={{0,4},{4,0},{8,12},{12,8},{1,5},{5,1},{9,13},{13,9},{2,6},{6,2},{1... | collective-permute-start | bytes 1572872 | tf_op jit(solution)/shard_map/ppermute | solution.py:394
  3.0 13.8 %collective-permute-start = (bf16[256,1024]{1,0:T(8,128)(2,1)}, bf16[256,1024]{1,0:T(8,128)(2,1)S(1)}, u32[]{:S(2)}, u32[]{:S(2)}) collective-permute-start(bf16[256,1024]{1,0:T(8,128)(2,1)} %refs_0_.2), channel_id=1, source_target_pairs={{0,2},{2,0},{1,3},{3,1},{4,6},{6,4},{5,7},{7,5},{8,10},{10,8},{9,1... | collective-permute-start | bytes 1572872 | tf_op jit(solution)/shard_map/ppermute | solution.py:382
  4.5 12.3 %collective-permute-start.1 = (bf16[256,1024]{1,0:T(8,128)(2,1)}, bf16[256,1024]{1,0:T(8,128)(2,1)S(1)}, u32[]{:S(2)}, u32[]{:S(2)}) collective-permute-start(bf16[256,1024]{1,0:T(8,128)(2,1)} %refs_0_.2), channel_id=1, source_target_pairs={{4,8},{8,4},{5,9},{9,5},{6,10},{10,6},{7,11},{11,7},{20,24},{24,20... | collective-permute-start | bytes 1572872 | tf_op jit(solution)/shard_map/ppermute | solution.py:397
  5.3 2.2 %copy-start = (bf16[2048,1024]{1,0:T(8,128)(2,1)S(1)}, bf16[2048,1024]{1,0:T(8,128)(2,1)}, u32[]{:S(2)}) copy-start(bf16[2048,1024]{1,0:T(8,128)(2,1)} %refs_2_.9) | copy-start | bytes 12582916
  7.5 2.2 %copy-start.2 = (bf16[2048,1024]{1,0:T(8,128)(2,1)S(1)}, bf16[2048,1024]{1,0:T(8,128)(2,1)}, u32[]{:S(2)}) copy-start(bf16[2048,1024]{1,0:T(8,128)(2,1)} %refs_3_.9) | copy-start | bytes 12582916
  9.7 2.2 %copy-start.4 = (bf16[2048,1024]{1,0:T(8,128)(2,1)S(1)}, bf16[2048,1024]{1,0:T(8,128)(2,1)}, u32[]{:S(2)}) copy-start(bf16[2048,1024]{1,0:T(8,128)(2,1)} %refs_3_.6) | copy-start | bytes 12582916
  11.9 5.0 %copy-start.6 = (bf16[256,1024]{1,0:T(8,128)(2,1)S(1)}, bf16[256,1024]{1,0:T(8,128)(2,1)}, u32[]{:S(2)}) copy-start(bf16[256,1024]{1,0:T(8,128)(2,1)} %refs_0_.2) | copy-start | bytes 1572868
  12.4 14.0 %copy-start.7 = (s32[4,20]{1,0:T(4,128)S(1)}, s32[4,20]{1,0:T(4,128)}, u32[]{:S(2)}) copy-start(s32[4,20]{1,0:T(4,128)} %partners_ref.1) | copy-start | bytes 964
  12.4 14.0 %copy-start.8 = (s32[4]{0:T(128)S(1)}, s32[4]{0:T(128)}, u32[]{:S(2)}) copy-start(s32[4]{0:T(128)} %counts_ref.1) | copy-start | bytes 52
  15.2 14.4 %collective-permute-start.4 = (bf16[256,1024]{1,0:T(8,128)(2,1)S(1)}, bf16[256,1024]{1,0:T(8,128)(2,1)S(1)}, u32[]{:S(2)}, u32[]{:S(2)}) collective-permute-start(bf16[256,1024]{1,0:T(8,128)(2,1)S(1)} %collective-permute-done.2.refs_0_), channel_id=1, source_target_pairs={{0,2},{2,0},{1,3},{3,1},{4,6},{6,4},{5,7},{7,5},{8,10},{10,8},{9,1... | collective-permute-start | bytes 1572872 | tf_op jit(solution)/shard_map/ppermute | solution.py:382
  16.8 16.3 %collective-permute-start.3 = (bf16[256,1024]{1,0:T(8,128)(2,1)S(1)}, bf16[256,1024]{1,0:T(8,128)(2,1)S(1)}, u32[]{:S(2)}, u32[]{:S(2)}) collective-permute-start(bf16[256,1024]{1,0:T(8,128)(2,1)S(1)} %copy-done.6), channel_id=1, source_target_pairs={{0,12},{12,0},{1,13},{13,1},{2,14},{14,2},{3,15},{15,3},{16,28},{2... | collective-permute-start | bytes 1572872 | tf_op jit(solution)/shard_map/ppermute | solution.py:399
  22.3 12.9 %copy-start.1 = (bf16[2048,1024]{1,0:T(8,128)(2,1)S(1)}, bf16[2048,1024]{1,0:T(8,128)(2,1)}, u32[]{:S(2)}) copy-start(bf16[2048,1024]{1,0:T(8,128)(2,1)} %refs_2_.9) | copy-start | bytes 12582916
  33.9 6.7 %collective-permute-start.6 = (bf16[128,1024]{1,0:T(8,128)(2,1)S(1)}, bf16[128,1024]{1,0:T(8,128)(2,1)S(1)}, u32[]{:S(2)}, u32[]{:S(2)}) collective-permute-start(bf16[128,1024]{1,0:T(8,128)(2,1)S(1)} %get-tuple-element.54), channel_id=1, source_target_pairs={{0,5},{1,4},{4,1},{5,0},{8,13},{9,12},{12,9},{13,8},{2,7},{3,6},{6... | collective-permute-start | bytes 786440 | tf_op jit(solution)/shard_map/ppermute | solution.py:415
  34.0 13.6 %collective-permute-start.5 = (bf16[256,1024]{1,0:T(8,128)(2,1)S(1)}, bf16[256,1024]{1,0:T(8,128)(2,1)S(1)}, u32[]{:S(2)}, u32[]{:S(2)}) collective-permute-start(bf16[256,1024]{1,0:T(8,128)(2,1)S(1)} %get-tuple-element.47.refs_0_), channel_id=1, source_target_pairs={{0,2},{2,0},{1,3},{3,1},{4,6},{6,4},{5,7},{7,5},{8,10},{10,8},{9,1... | collective-permute-start | bytes 1572872 | tf_op jit(solution)/shard_map/ppermute | solution.py:382
  35.2 16.6 %collective-permute-start.12 = (bf16[512,1024]{1,0:T(8,128)(2,1)S(1)}, bf16[512,1024]{1,0:T(8,128)(2,1)S(1)}, u32[]{:S(2)}, u32[]{:S(2)}) collective-permute-start(bf16[512,1024]{1,0:T(8,128)(2,1)S(1)} %get-tuple-element.42.refs_0_), channel_id=1, source_target_pairs={{0,1},{1,0},{2,3},{3,2},{4,5},{5,4},{6,7},{7,6},{8,9},{9,8},{10,11... | collective-permute-start | bytes 3145736 | tf_op jit(solution)/shard_map/ppermute | solution.py:388
  40.6 10.7 %collective-permute-start.7 = (bf16[128,1024]{1,0:T(8,128)(2,1)S(1)}, bf16[128,1024]{1,0:T(8,128)(2,1)S(1)}, u32[]{:S(2)}, u32[]{:S(2)}) collective-permute-start(bf16[128,1024]{1,0:T(8,128)(2,1)S(1)} %collective-permute-done.6.refs_0_), channel_id=1, source_target_pairs={{0,2},{2,0},{1,3},{3,1},{4,6},{6,4},{5,7},{7,5},{8,10},{10,8},{9,1... | collective-permute-start | bytes 786440 | tf_op jit(solution)/shard_map/ppermute | solution.py:382
  41.6 10.2 %collective-permute-start.10 = (bf16[256,1024]{1,0:T(8,128)(2,1)S(1)}, bf16[256,1024]{1,0:T(8,128)(2,1)S(1)}, u32[]{:S(2)}, u32[]{:S(2)}) collective-permute-start(bf16[256,1024]{1,0:T(8,128)(2,1)S(1)} %get-tuple-element.49.refs_0_), channel_id=1, source_target_pairs={{0,1},{1,0},{2,3},{3,2},{4,5},{5,4},{6,7},{7,6},{8,9},{9,8},{10,11... | collective-permute-start | bytes 1572872 | tf_op jit(solution)/shard_map/ppermute | solution.py:388
  41.7 10.1 %collective-permute-start.11 = (bf16[256,1024]{1,0:T(8,128)(2,1)S(1)}, bf16[256,1024]{1,0:T(8,128)(2,1)S(1)}, u32[]{:S(2)}, u32[]{:S(2)}) collective-permute-start(bf16[256,1024]{1,0:T(8,128)(2,1)S(1)} %get-tuple-element.50.refs_1_), channel_id=1, source_target_pairs={{0,1},{1,0},{2,3},{3,2},{4,5},{5,4},{6,7},{7,6},{8,9},{9,8},{10,11... | collective-permute-start | bytes 1572872 | tf_op jit(solution)/shard_map/ppermute | solution.py:388
  50.6 4.9 %copy-start.3 = (bf16[2048,1024]{1,0:T(8,128)(2,1)S(1)}, bf16[2048,1024]{1,0:T(8,128)(2,1)}, u32[]{:S(2)}) copy-start(bf16[2048,1024]{1,0:T(8,128)(2,1)} %refs_3_.9) | copy-start | bytes 12582916
  51.3 6.2 %collective-permute-start.8 = (bf16[256,1024]{1,0:T(8,128)(2,1)S(1)}, bf16[256,1024]{1,0:T(8,128)(2,1)S(1)}, u32[]{:S(2)}, u32[]{:S(2)}) collective-permute-start(bf16[256,1024]{1,0:T(8,128)(2,1)S(1)} %get-tuple-element.58.refs_3_), channel_id=1, source_target_pairs={{0,1},{1,0},{2,3},{3,2},{4,5},{5,4},{6,7},{7,6},{8,9},{9,8},{10,11... | collective-permute-start | bytes 1572872 | tf_op jit(solution)/shard_map/ppermute | solution.py:388
  51.3 6.2 %collective-permute-start.9 = (bf16[256,1024]{1,0:T(8,128)(2,1)S(1)}, bf16[256,1024]{1,0:T(8,128)(2,1)S(1)}, u32[]{:S(2)}, u32[]{:S(2)}) collective-permute-start(bf16[256,1024]{1,0:T(8,128)(2,1)S(1)} %get-tuple-element.59.refs_4_), channel_id=1, source_target_pairs={{0,1},{1,0},{2,3},{3,2},{4,5},{5,4},{6,7},{7,6},{8,9},{9,8},{10,11... | collective-permute-start | bytes 1572872 | tf_op jit(solution)/shard_map/ppermute | solution.py:388
  55.6 4.3 %copy-start.5 = (bf16[1024,2048]{1,0:T(8,128)(2,1)S(1)}, bf16[1024,2048]{1,0:T(8,128)(2,1)}, u32[]{:S(2)}) copy-start(bf16[1024,2048]{1,0:T(8,128)(2,1)} %refs_4_.3) | copy-start | bytes 12582916
  61.2 9.2 %collective-permute-start.14 = (bf16[128,1024]{1,0:T(8,128)(2,1)S(1)}, bf16[128,1024]{1,0:T(8,128)(2,1)S(1)}, u32[]{:S(2)}, u32[]{:S(2)}) collective-permute-start(bf16[128,1024]{1,0:T(8,128)(2,1)S(1)} %get-tuple-element.68), channel_id=1, source_target_pairs={{0,2},{2,0},{1,3},{3,1},{4,6},{6,4},{5,7},{7,5},{8,10},{10,8},{9,1... | collective-permute-start | bytes 786440 | tf_op jit(solution)/shard_map/ppermute | solution.py:382
  64.0 11.1 %collective-permute-start.13 = (bf16[128,1024]{1,0:T(8,128)(2,1)S(1)}, bf16[128,1024]{1,0:T(8,128)(2,1)S(1)}, u32[]{:S(2)}, u32[]{:S(2)}) collective-permute-start(bf16[128,1024]{1,0:T(8,128)(2,1)S(1)} %get-tuple-element.73), channel_id=1, source_target_pairs={{0,2},{2,0},{1,3},{3,1},{4,6},{6,4},{5,7},{7,5},{8,10},{10,8},{9,1... | collective-permute-start | bytes 786440 | tf_op jit(solution)/shard_map/ppermute | solution.py:382

commit v4 on v3

--- a/solution.py
+++ b/solution.py
@@ -11,7 +11,6 @@
 L = 64
 EDGE = 2
 MB = 1 << 20
-FAKE = 300_000_000
 FACTOR = HD ** (-0.5) * 1.4426950408889634
 ROWS_BY_ROWS = (((1,), (1,)), ((), ()))
 
@@ -21,7 +20,7 @@
 PLACE, CORE, SIDE = range(3)
 
 
-def call(kernel, outs, ins, scratch=(), name=None, out_specs=None, aliases=None, whole=(), flops=0):
+def call(kernel, outs, ins, scratch=(), name=None, out_specs=None, aliases=None, whole=()):
     return pl.pallas_call(
         kernel,
         out_shape=outs,
@@ -33,7 +32,7 @@
         scratch_shapes=list(scratch),
         input_output_aliases=aliases or {},
         compiler_params=pltpu.CompilerParams(vmem_limit_bytes=16 * MB),
-        cost_estimate=pl.CostEstimate(flops=flops, bytes_accessed=0, transcendentals=0),
+        cost_estimate=pl.CostEstimate(flops=0, bytes_accessed=0, transcendentals=0),
         name=name,
     )(*ins)
 
@@ -74,10 +73,8 @@
     refs[-1][...] = jnp.zeros_like(refs[-1])
 
 
-def fetch(*arrays, flops=0):
-    return call(
-        fetch_kernel, jax.ShapeDtypeStruct((8, 128), jnp.float32), arrays, name="fetch", flops=flops
-    )
+def fetch(*arrays):
+    return call(fetch_kernel, jax.ShapeDtypeStruct((8, 128), jnp.float32), arrays, name="fetch")
 
 
 def make_mask(chips, cores, here, counts, partners, fetched):
@@ -221,7 +218,7 @@
         mixed_out[column, :] = mixed
 
 
-def attend(bias, bias_start, query, blocks, state, flops=0):
+def attend(bias, bias_start, query, blocks, state):
     width, rows = query.shape
     heads = width // HD
     span = sum(a.shape[0] for block in blocks for a in block) // 2
@@ -236,7 +233,6 @@
         [bias, query, *[a for block in blocks for a in block], *(state or [])],
         scratch=[pltpu.VMEM((2, span, rows), jnp.float32)],
         name="attend",
-        flops=flops,
     )
 
 
@@ -285,7 +281,7 @@
             sent_refs[step - 1][...] = result.astype(jnp.bfloat16)
 
 
-def pick_kernel(here_ref, inner_ref, outer_ref, fetched_ref, block_ref, edge_ref):
+def pick_kernel(here_ref, inner_ref, outer_ref, block_ref, edge_ref):
     place = here_ref[PLACE]
     is_inner = (place == 1) | (place == 2)
 
@@ -303,12 +299,12 @@
         take(outer_ref)
 
 
-def pick(here, inner, outer, fetched):
+def pick(here, inner, outer):
     edge = jax.ShapeDtypeStruct((EDGE * L, inner.shape[1]), inner.dtype)
     return call(
         pick_kernel,
         [jax.ShapeDtypeStruct(inner.shape, inner.dtype), edge],
-        [here, inner, outer, fetched],
+        [here, inner, outer],
         name="pick",
     )
 
@@ -395,7 +391,7 @@
     fetched = fetch(here, w_key, w_value, w_query)
     if chips == 4:
         inner = lax.ppermute(tokens, "views", [(1, 2), (2, 1)])
-        outer = after(tokens, near, own[1][0], inner, fetched)
+        outer = after(tokens, fetched)
         outer = lax.ppermute(outer, "views", [(0, 3), (3, 0)])
     else:
         beyond = lax.ppermute(tokens, "views", side_step)
@@ -410,23 +406,23 @@
     bias = make_mask(chips, cores, after(here, query), counts, partners, fetched)
     state = attend(bias, 0, query, [block], None)
     if chips == 4:
-        beyond, rim = pick(here, after(inner, state[0]), outer, fetch(near[1][0], flops=FAKE))
+        beyond, rim = pick(here, after(inner, state[0]), outer)
         cross = [(2 * z + c, 2 * (z ^ 1) + 1 - c) for z in range(chips) for c in range(cores)]
         rim = lax.ppermute(rim, ("views", "sub"), cross)
     near[1][0] = after(near[1][0], beyond)
     (block,) = project(here, near, w_key, w_value)
     near_shared = share(block)
     beyond = gather([beyond])
-    state = attend(bias, views_here, query, [block], state, flops=FAKE)
+    state = attend(bias, views_here, query, [block], state)
     rim = gather([after(rim, state[0])])
     beyond[1][0] = after(beyond[1][0], state[0], rim[0][0])
     (block,) = project(here, beyond, w_key, w_value)
-    beyond_shared = share((after(block[0], rim[1][0]), block[1]))
+    beyond_shared = share(block)
     state = attend(bias, 2 * views_here, query, [near_shared, own_shared, block], state)
-    (rim_block,) = project(here, rim, w_key, w_value)
     state = attend(bias, 5 * views_here, query, [beyond_shared], state)
 
     inner = finish(sides, here, True, rows - edge_rows, state, w_out)
+    (rim_block,) = project(here, [[after(a, inner[0]) for a in piece] for piece in rim], w_key, w_value)
     outer = finish(
         sides, here, False, edge_rows, [after(state[0], inner[0]), *state[1:]], w_out,
         (bias, 6 * views_here, query, rim_block),

time: 77.1 us -> 69.9 us (0.907)
  waiting for transfers between devices: 21.2 us -> 14.5 us
    ppermute x6, waiting for transfers between devices: 14.9 us -> 8.98 us  [shift(): lax.ppermute(a, 'heads', [(h, (h + step) % sides) for h in range(sides)])]
    ppermute x1, waiting for transfers between devices: 2.72 us -> 0.01 us  [shards(): near = lax.ppermute(tokens, 'views', pair)]
    ppermute x1, starting transfers between devices: 0.07 us -> 2.56 us  [shards(): rim = lax.ppermute(rim, ('views', 'sub'), cross)]
    ppermute x6, starting transfers between devices: 7.61 us -> 5.38 us  [shift(): lax.ppermute(a, 'heads', [(h, (h + step) % sides) for h in range(sides)])]
    ppermute x1, waiting for transfers between devices: 3.57 us -> 4.73 us  [shards(): outer = lax.ppermute(outer, 'views', [(0, 3), (3, 0)])]
    ppermute x1, starting transfers between devices: 5.51 us -> 4.5 us  [shards(): outer = lax.ppermute(outer, 'views', [(0, 3), (3, 0)])]
    pallas_call x16 -> x15, Pallas kernels: 30.4 us -> 30.3 us  [call(): pl.pallas_call(kernel, out_shape=outs, in_specs=[HBM if k in whole else S...]
  transfers between devices with their start and end apart: 15 -> 15, of which waited for: 6 -> 5; matrix products, arithmetic and copies ran while one was open for 0% -> 0% of each run, Pallas kernels for 32% -> 42%
where the time goes in v4:
time: 69.9 us; the launch traced here: 69.6 us
  Pallas kernels  30.3 us (43%)
  starting transfers between devices  17.3 us (25%)
  waiting for transfers between devices  14.5 us (21%)
  local copies, waits for them, and re-layouts  7.08 us (10%)
    pallas_call x15, Pallas kernels, call(): pl.pallas_call(kernel, out_shape=outs, in_specs=[HBM if k in whole else S...  30.3 us
    ppermute x6, waiting for transfers between devices, shift(): lax.ppermute(a, 'heads', [(h, (h + step) % sides) for h in range(sides)])  8.98 us
    unnamed x18, local copies, waits for them, and re-layouts  7.08 us
    ppermute x6, starting transfers between devices, shift(): lax.ppermute(a, 'heads', [(h, (h + step) % sides) for h in range(sides)])  5.38 us
    ppermute x1, waiting for transfers between devices, shards(): outer = lax.ppermute(outer, 'views', [(0, 3), (3, 0)])  4.73 us
    ppermute x1, starting transfers between devices, shards(): outer = lax.ppermute(outer, 'views', [(0, 3), (3, 0)])  4.5 us
    ppermute x1, starting transfers between devices, shards(): near = lax.ppermute(tokens, 'views', pair)  3.02 us
    ppermute x1, starting transfers between devices, shards(): rim = lax.ppermute(rim, ('views', 'sub'), cross)  2.56 us
  transfers between devices with their start and end apart: 15, of which 5 were waited for; matrix products, arithmetic and copies ran while one was open for 0% of the time, Pallas kernels for 42%

profile of v4, /device:TPU:0, one launch (start us, length us, event | category | flops | bytes accessed | tf_op | source)
XLA Modules:
  0.0 69.6 jit_solution(16252920186475198485)
XLA Ops:
  0.0 3.0 %collective-permute-start.4 = (bf16[256,1024]{1,0:T(8,128)(2,1)}, bf16[256,1024]{1,0:T(8,128)(2,1)S(1)}, u32[]{:S(2)}, u32[]{:S(2)}) collective-permute-start(bf16[256,1024]{1,0:T(8,128)(2,1)} %refs_0_.2), channel_id=1, source_target_pairs={{0,4},{4,0},{8,12},{12,8},{1,5},{5,1},{9,13},{13,9},{2,6},{6,2},{1... | collective-permute-start | bytes 1572872 | tf_op jit(solution)/shard_map/ppermute | solution.py:390
  3.0 1.5 %collective-permute-start = (bf16[256,1024]{1,0:T(8,128)(2,1)}, bf16[256,1024]{1,0:T(8,128)(2,1)S(1)}, u32[]{:S(2)}, u32[]{:S(2)}) collective-permute-start(bf16[256,1024]{1,0:T(8,128)(2,1)} %refs_0_.2), channel_id=1, source_target_pairs={{0,2},{2,0},{1,3},{3,1},{4,6},{6,4},{5,7},{7,5},{8,10},{10,8},{9,1... | collective-permute-start | bytes 1572872 | tf_op jit(solution)/shard_map/ppermute | solution.py:378
  4.5 0.7 collective-permute-start.1
  5.2 0.1 pad_add_fusion.here_ref.refs_0_
  5.3 2.2 %copy-done = bf16[2048,1024]{1,0:T(8,128)(2,1)S(1)} copy-done((bf16[2048,1024]{1,0:T(8,128)(2,1)S(1)}, bf16[2048,1024]{1,0:T(8,128)(2,1)}, u32[]{:S(2)}) %copy-start) | copy-done | bytes 4194328
  7.5 2.2 %copy-done.2 = bf16[2048,1024]{1,0:T(8,128)(2,1)S(1)} copy-done((bf16[2048,1024]{1,0:T(8,128)(2,1)S(1)}, bf16[2048,1024]{1,0:T(8,128)(2,1)}, u32[]{:S(2)}) %copy-start.2) | copy-done | bytes 4194328
  9.7 2.2 %copy-done.4 = bf16[2048,1024]{1,0:T(8,128)(2,1)S(1)} copy-done((bf16[2048,1024]{1,0:T(8,128)(2,1)S(1)}, bf16[2048,1024]{1,0:T(8,128)(2,1)}, u32[]{:S(2)}) %copy-start.4) | copy-done | bytes 4194328
  11.9 0.5 fetch.1.refs_0_
  12.4 0.5 copy-done.6
  12.9 4.5 %collective-permute-start.2 = (bf16[256,1024]{1,0:T(8,128)(2,1)S(1)}, bf16[256,1024]{1,0:T(8,128)(2,1)S(1)}, u32[]{:S(2)}, u32[]{:S(2)}) collective-permute-start(bf16[256,1024]{1,0:T(8,128)(2,1)S(1)} %copy-done.6), channel_id=1, source_target_pairs={{0,12},{12,0},{1,13},{13,1},{2,14},{14,2},{3,15},{15,3},{16,28},{2... | collective-permute-start | bytes 1572872 | tf_op jit(solution)/shard_map/ppermute | solution.py:395
  17.4 0.0 collective-permute-done.4.refs_0_
  17.4 0.6 collective-permute-start.5
  18.0 0.0 collective-permute-done.refs_1_
  18.0 4.1 %project.4 = (bf16[512,1024]{1,0:T(8,128)(2,1)S(1)}, bf16[1024,256]{1,0:T(8,128)(2,1)S(1)}) custom-call(s32[3]{0:T(128)S(1)} %pad_add_fusion.here_ref.refs_0_, bf16[256,1024]{1,0:T(8,128)(2,1)S(1)} %copy-done.6, bf16[256,1024]{1,0:T(8,128)(2,1)S(1)} %collective-permute-done.refs_1_, bf16[2048,1024]{1,0:T(8,128)(2,1)S(1)} %copy-done, ...), custom_call_target="tpu_custom_call" | custom-call | tf_op jit(solution)/shard_map/project/pallas_call | solution.py:24
  22.1 0.7 %mask.1.bias_ref.refs_0_ = f32[26,256]{1,0:T(8,128)S(1)} custom-call(s32[3]{0:T(128)S(1)} %pad_add_fusion.here_ref.refs_0_, s32[4]{0:T(128)S(1)} %copy-done.8, s32[4,20]{1,0:T(4,128)S(1)} %copy-done.7, f32[8,128]{1,0:T(8,128)S(1)} %fetch.1.refs_0_), custom_call_target="tpu_custom_call" | custom-call | tf_op jit(solution)/shard_map/mask/pallas_call | solution.py:24
  22.9 2.3 %attend.4 = (f32[8,256]{1,0:T(8,128)S(1)}, f32[8,256]{1,0:T(8,128)S(1)}, f32[1024,256]{1,0:T(8,128)S(1)}) custom-call(f32[26,256]{1,0:T(8,128)S(1)} %mask.1.bias_ref.refs_0_, bf16[1024,256]{1,0:T(8,128)(2,1)S(1)} %get-tuple-element.41.query_ref.refs_1_, bf16[512,1024]{1,0:T(8,128)(2,1)S(1)} %get-tuple-element.43.refs_0_), custom_call_target="tpu_custom_call" | custom-call | tf_op jit(solution)/shard_map/attend/pallas_call | solution.py:24
  25.2 4.7 %collective-permute-done.2.outer_ref = bf16[256,1024]{1,0:T(8,128)(2,1)S(1)} collective-permute-done((bf16[256,1024]{1,0:T(8,128)(2,1)S(1)}, bf16[256,1024]{1,0:T(8,128)(2,1)S(1)}, u32[]{:S(2)}, u32[]{:S(2)}) %collective-permute-start.2) | collective-permute-done | bytes 524320 | tf_op jit(solution)/shard_map/ppermute | solution.py:395
  29.9 0.8 %pick.1 = (bf16[256,1024]{1,0:T(8,128)(2,1)S(1)}, bf16[128,1024]{1,0:T(8,128)(2,1)S(1)}) custom-call(s32[3]{0:T(128)S(1)} %pad_add_fusion.here_ref.refs_0_, bf16[256,1024]{1,0:T(8,128)(2,1)S(1)} %collective-permute-done.1.inner_ref, bf16[256,1024]{1,0:T(8,128)(2,1)S(1)} %collective-permute-done.2.outer_ref), custom_call_target="tpu_custom_call" | custom-call | tf_op jit(solution)/shard_map/pick/pallas_call | solution.py:24
  30.7 0.6 collective-permute-start.3
  31.3 0.0 collective-permute-start.11
  31.3 2.6 %collective-permute-start.6 = (bf16[128,1024]{1,0:T(8,128)(2,1)S(1)}, bf16[128,1024]{1,0:T(8,128)(2,1)S(1)}, u32[]{:S(2)}, u32[]{:S(2)}) collective-permute-start(bf16[128,1024]{1,0:T(8,128)(2,1)S(1)} %get-tuple-element.55), channel_id=1, source_target_pairs={{0,5},{1,4},{4,1},{5,0},{8,13},{9,12},{12,9},{13,8},{2,7},{3,6},{6... | collective-permute-start | bytes 786440 | tf_op jit(solution)/shard_map/ppermute | solution.py:411
  33.9 0.0 collective-permute-done.5.refs_1_
  33.9 3.0 %project.5 = (bf16[256,1024]{1,0:T(8,128)(2,1)S(1)}, bf16[256,1024]{1,0:T(8,128)(2,1)S(1)}) custom-call(s32[3]{0:T(128)S(1)} %pad_add_fusion.here_ref.refs_0_, bf16[256,1024]{1,0:T(8,128)(2,1)S(1)} %collective-permute-done.4.refs_0_, bf16[256,1024]{1,0:T(8,128)(2,1)S(1)} %collective-permute-done.5.refs_1_, bf16[2048,1024]{1,0:T(8,128)(2,1)S(1)} %copy-done.1, ...), custom_call_target="tpu_custom_call" | custom-call | tf_op jit(solution)/shard_map/project/pallas_call | solution.py:24
  36.9 0.1 collective-permute-start.10
  37.0 0.5 collective-permute-start.9
  37.5 2.3 %attend.5 = (f32[8,256]{1,0:T(8,128)S(1)}, f32[8,256]{1,0:T(8,128)S(1)}, f32[1024,256]{1,0:T(8,128)S(1)}) custom-call(f32[26,256]{1,0:T(8,128)S(1)} %mask.1.bias_ref.refs_0_, bf16[1024,256]{1,0:T(8,128)(2,1)S(1)} %get-tuple-element.41.query_ref.refs_1_, bf16[256,1024]{1,0:T(8,128)(2,1)S(1)} %get-tuple-element.50.refs_0_, ...), custom_call_target="tpu_custom_call" | custom-call | tf_op jit(solution)/shard_map/attend/pallas_call | solution.py:24
  39.8 0.8 %collective-permute-done.6.refs_0_ = bf16[128,1024]{1,0:T(8,128)(2,1)S(1)} collective-permute-done((bf16[128,1024]{1,0:T(8,128)(2,1)S(1)}, bf16[128,1024]{1,0:T(8,128)(2,1)S(1)}, u32[]{:S(2)}, u32[]{:S(2)}) %collective-permute-start.6) | collective-permute-done | bytes 262176 | tf_op jit(solution)/shard_map/ppermute | solution.py:411
  40.6 2.4 %collective-permute-done.3.refs_1_ = bf16[256,1024]{1,0:T(8,128)(2,1)S(1)} collective-permute-done((bf16[256,1024]{1,0:T(8,128)(2,1)S(1)}, bf16[256,1024]{1,0:T(8,128)(2,1)S(1)}, u32[]{:S(2)}, u32[]{:S(2)}) %collective-permute-start.3) | collective-permute-done | bytes 524320 | tf_op jit(solution)/shard_map/ppermute | solution.py:378
  42.9 3.0 %project.6 = (bf16[256,1024]{1,0:T(8,128)(2,1)S(1)}, bf16[256,1024]{1,0:T(8,128)(2,1)S(1)}) custom-call(s32[3]{0:T(128)S(1)} %pad_add_fusion.here_ref.refs_0_, bf16[256,1024]{1,0:T(8,128)(2,1)S(1)} %get-tuple-element.47.refs_0_, bf16[256,1024]{1,0:T(8,128)(2,1)S(1)} %collective-permute-done.3.refs_1_, bf16[2048,1024]{1,0:T(8,128)(2,1)S(1)} %copy-done.1, ...), custom_call_target="tpu_custom_call" | custom-call | tf_op jit(solution)/shard_map/project/pallas_call | solution.py:24
  45.9 0.0 copy-start.5
  45.9 0.1 collective-permute-start.7
  46.0 0.5 collective-permute-start.8
  46.5 0.5 collective-permute-start.12
  47.1 3.7 %attend.6 = (f32[8,256]{1,0:T(8,128)S(1)}, f32[8,256]{1,0:T(8,128)S(1)}, f32[1024,256]{1,0:T(8,128)S(1)}) custom-call(f32[26,256]{1,0:T(8,128)S(1)} %mask.1.bias_ref.refs_0_, bf16[1024,256]{1,0:T(8,128)(2,1)S(1)} %get-tuple-element.41.query_ref.refs_1_, bf16[256,1024]{1,0:T(8,128)(2,1)S(1)} %collective-permute-done.9.refs_0_, ...), custom_call_target="tpu_custom_call" | custom-call | tf_op jit(solution)/shard_map/attend/pallas_call | solution.py:24
  50.8 0.0 copy-start.3
  50.8 0.0 collective-permute-done.7.refs_0_
  50.8 0.0 collective-permute-done.8.refs_1_
  50.8 2.3 %attend.7 = (f32[8,256]{1,0:T(8,128)S(1)}, f32[8,256]{1,0:T(8,128)S(1)}, f32[1024,256]{1,0:T(8,128)S(1)}) custom-call(f32[26,256]{1,0:T(8,128)S(1)} %mask.1.bias_ref.refs_0_, bf16[1024,256]{1,0:T(8,128)(2,1)S(1)} %get-tuple-element.41.query_ref.refs_1_, bf16[256,1024]{1,0:T(8,128)(2,1)S(1)} %collective-permute-done.7.refs_0_, ...), custom_call_target="tpu_custom_call" | custom-call | tf_op jit(solution)/shard_map/attend/pallas_call | solution.py:24
  53.1 1.4 %finish.2 = (bf16[128,1024]{1,0:T(8,128)(2,1)S(1)}, f32[128,1024]{1,0:T(8,128)S(1)}) custom-call(s32[3]{0:T(128)S(1)} %pad_add_fusion.here_ref.refs_0_, f32[8,256]{1,0:T(8,128)S(1)} %get-tuple-element.69.top_ref, f32[8,256]{1,0:T(8,128)S(1)} %get-tuple-element.66.total_ref, f32[1024,256]{1,0:T(8,128)S(1)} %get-tuple-element.67.mixed_ref, ...), custom_call_target="tpu_custom_call" | custom-call | tf_op jit(solution)/shard_map/finish/pallas_call | solution.py:24
  54.5 1.5 %collective-permute-start.14 = (bf16[128,1024]{1,0:T(8,128)(2,1)S(1)}, bf16[128,1024]{1,0:T(8,128)(2,1)S(1)}, u32[]{:S(2)}, u32[]{:S(2)}) collective-permute-start(bf16[128,1024]{1,0:T(8,128)(2,1)S(1)} %get-tuple-element.68), channel_id=1, source_target_pairs={{0,2},{2,0},{1,3},{3,1},{4,6},{6,4},{5,7},{7,5},{8,10},{10,8},{9,1... | collective-permute-start | bytes 786440 | tf_op jit(solution)/shard_map/ppermute | solution.py:378
  56.0 0.0 collective-permute-done.12.refs_1_
  56.0 1.9 %project.7 = (bf16[128,1024]{1,0:T(8,128)(2,1)S(1)}, bf16[128,1024]{1,0:T(8,128)(2,1)S(1)}) custom-call(s32[3]{0:T(128)S(1)} %pad_add_fusion.here_ref.refs_0_, bf16[128,1024]{1,0:T(8,128)(2,1)S(1)} %collective-permute-done.6.refs_0_, bf16[128,1024]{1,0:T(8,128)(2,1)S(1)} %collective-permute-done.12.refs_1_, bf16[2048,1024]{1,0:T(8,128)(2,1)S(1)} %copy-done.1, ...), custom_call_target="tpu_custom_call" | custom-call | tf_op jit(solution)/shard_map/project/pallas_call | solution.py:24
  58.0 1.7 %finish.3 = (bf16[128,1024]{1,0:T(8,128)(2,1)S(1)}, f32[128,1024]{1,0:T(8,128)S(1)}) custom-call(s32[3]{0:T(128)S(1)} %pad_add_fusion.here_ref.refs_0_, f32[8,256]{1,0:T(8,128)S(1)} %get-tuple-element.69.top_ref, f32[8,256]{1,0:T(8,128)S(1)} %get-tuple-element.66.total_ref, f32[1024,256]{1,0:T(8,128)S(1)} %get-tuple-element.67.mixed_ref, ...), custom_call_target="tpu_custom_call" | custom-call | tf_op jit(solution)/shard_map/finish/pallas_call | solution.py:24
  59.7 0.6 collective-permute-start.13
  60.3 2.9 %collective-permute-done.14.refs_1_ = bf16[128,1024]{1,0:T(8,128)(2,1)S(1)} collective-permute-done((bf16[128,1024]{1,0:T(8,128)(2,1)S(1)}, bf16[128,1024]{1,0:T(8,128)(2,1)S(1)}, u32[]{:S(2)}, u32[]{:S(2)}) %collective-permute-start.14) | collective-permute-done | bytes 262176 | tf_op jit(solution)/shard_map/ppermute | solution.py:378
  63.2 1.3 %settle.2.refs_2_ = bf16[256,1024]{1,0:T(8,128)(2,1)} custom-call(s32[3]{0:T(128)S(1)} %pad_add_fusion.here_ref.refs_0_, f32[128,1024]{1,0:T(8,128)S(1)} %get-tuple-element.76.refs_0_, bf16[128,1024]{1,0:T(8,128)(2,1)S(1)} %collective-permute-done.14.refs_1_), custom_call_target="tpu_custom_call" | custom-call | tf_op jit(solution)/shard_map/settle/pallas_call | solution.py:24
  64.5 3.7 %collective-permute-done.13.refs_1_ = bf16[128,1024]{1,0:T(8,128)(2,1)S(1)} collective-permute-done((bf16[128,1024]{1,0:T(8,128)(2,1)S(1)}, bf16[128,1024]{1,0:T(8,128)(2,1)S(1)}, u32[]{:S(2)}, u32[]{:S(2)}) %collective-permute-start.13) | collective-permute-done | bytes 262176 | tf_op jit(solution)/shard_map/ppermute | solution.py:378
  68.2 1.3 %settle.3 = bf16[256,1024]{1,0:T(8,128)(2,1)} custom-call(s32[3]{0:T(128)S(1)} %pad_add_fusion.here_ref.refs_0_, f32[128,1024]{1,0:T(8,128)S(1)} %get-tuple-element.74.refs_0_, bf16[128,1024]{1,0:T(8,128)(2,1)S(1)} %collective-permute-done.13.refs_1_, bf16[256,1024]{1,0:T(8,128)(2,1)} %settle.2.refs_2_), custom_call_target="tpu_custom_call", output_to_operand_aliasing={{}: (3, {})} | custom-call | tf_op jit(solution)/shard_map/settle/pallas_call | solution.py:24
  (16 shorter events, 0.0 us)
Async XLA Ops:
  0.0 17.4 %collective-permute-start.4 = (bf16[256,1024]{1,0:T(8,128)(2,1)}, bf16[256,1024]{1,0:T(8,128)(2,1)S(1)}, u32[]{:S(2)}, u32[]{:S(2)}) collective-permute-start(bf16[256,1024]{1,0:T(8,128)(2,1)} %refs_0_.2), channel_id=1, source_target_pairs={{0,4},{4,0},{8,12},{12,8},{1,5},{5,1},{9,13},{13,9},{2,6},{6,2},{1... | collective-permute-start | bytes 1572872 | tf_op jit(solution)/shard_map/ppermute | solution.py:390
  3.0 15.0 %collective-permute-start = (bf16[256,1024]{1,0:T(8,128)(2,1)}, bf16[256,1024]{1,0:T(8,128)(2,1)S(1)}, u32[]{:S(2)}, u32[]{:S(2)}) collective-permute-start(bf16[256,1024]{1,0:T(8,128)(2,1)} %refs_0_.2), channel_id=1, source_target_pairs={{0,2},{2,0},{1,3},{3,1},{4,6},{6,4},{5,7},{7,5},{8,10},{10,8},{9,1... | collective-permute-start | bytes 1572872 | tf_op jit(solution)/shard_map/ppermute | solution.py:378
  4.5 20.7 %collective-permute-start.1 = (bf16[256,1024]{1,0:T(8,128)(2,1)}, bf16[256,1024]{1,0:T(8,128)(2,1)S(1)}, u32[]{:S(2)}, u32[]{:S(2)}) collective-permute-start(bf16[256,1024]{1,0:T(8,128)(2,1)} %refs_0_.2), channel_id=1, source_target_pairs={{4,8},{8,4},{5,9},{9,5},{6,10},{10,6},{7,11},{11,7},{20,24},{24,20... | collective-permute-start | bytes 1572872 | tf_op jit(solution)/shard_map/ppermute | solution.py:393
  5.3 2.2 %copy-start = (bf16[2048,1024]{1,0:T(8,128)(2,1)S(1)}, bf16[2048,1024]{1,0:T(8,128)(2,1)}, u32[]{:S(2)}) copy-start(bf16[2048,1024]{1,0:T(8,128)(2,1)} %refs_2_.9) | copy-start | bytes 12582916
  7.5 2.2 %copy-start.2 = (bf16[2048,1024]{1,0:T(8,128)(2,1)S(1)}, bf16[2048,1024]{1,0:T(8,128)(2,1)}, u32[]{:S(2)}) copy-start(bf16[2048,1024]{1,0:T(8,128)(2,1)} %refs_3_.9) | copy-start | bytes 12582916
  9.7 2.2 %copy-start.4 = (bf16[2048,1024]{1,0:T(8,128)(2,1)S(1)}, bf16[2048,1024]{1,0:T(8,128)(2,1)}, u32[]{:S(2)}) copy-start(bf16[2048,1024]{1,0:T(8,128)(2,1)} %refs_3_.6) | copy-start | bytes 12582916
  11.9 1.0 %copy-start.6 = (bf16[256,1024]{1,0:T(8,128)(2,1)S(1)}, bf16[256,1024]{1,0:T(8,128)(2,1)}, u32[]{:S(2)}) copy-start(bf16[256,1024]{1,0:T(8,128)(2,1)} %refs_0_.2) | copy-start | bytes 1572868
  12.9 9.2 %copy-start.7 = (s32[4,20]{1,0:T(4,128)S(1)}, s32[4,20]{1,0:T(4,128)}, u32[]{:S(2)}) copy-start(s32[4,20]{1,0:T(4,128)} %partners_ref.1) | copy-start | bytes 964
  12.9 9.2 %copy-start.8 = (s32[4]{0:T(128)S(1)}, s32[4]{0:T(128)}, u32[]{:S(2)}) copy-start(s32[4]{0:T(128)} %counts_ref.1) | copy-start | bytes 52
  12.9 17.0 %collective-permute-start.2 = (bf16[256,1024]{1,0:T(8,128)(2,1)S(1)}, bf16[256,1024]{1,0:T(8,128)(2,1)S(1)}, u32[]{:S(2)}, u32[]{:S(2)}) collective-permute-start(bf16[256,1024]{1,0:T(8,128)(2,1)S(1)} %copy-done.6), channel_id=1, source_target_pairs={{0,12},{12,0},{1,13},{13,1},{2,14},{14,2},{3,15},{15,3},{16,28},{2... | collective-permute-start | bytes 1572872 | tf_op jit(solution)/shard_map/ppermute | solution.py:395
  17.4 16.5 %collective-permute-start.5 = (bf16[256,1024]{1,0:T(8,128)(2,1)S(1)}, bf16[256,1024]{1,0:T(8,128)(2,1)S(1)}, u32[]{:S(2)}, u32[]{:S(2)}) collective-permute-start(bf16[256,1024]{1,0:T(8,128)(2,1)S(1)} %collective-permute-done.4.refs_0_), channel_id=1, source_target_pairs={{0,2},{2,0},{1,3},{3,1},{4,6},{6,4},{5,7},{7,5},{8,10},{10,8},{9,1... | collective-permute-start | bytes 1572872 | tf_op jit(solution)/shard_map/ppermute | solution.py:378
  18.0 15.9 %copy-start.1 = (bf16[2048,1024]{1,0:T(8,128)(2,1)S(1)}, bf16[2048,1024]{1,0:T(8,128)(2,1)}, u32[]{:S(2)}) copy-start(bf16[2048,1024]{1,0:T(8,128)(2,1)} %refs_2_.9) | copy-start | bytes 12582916
  30.7 12.2 %collective-permute-start.3 = (bf16[256,1024]{1,0:T(8,128)(2,1)S(1)}, bf16[256,1024]{1,0:T(8,128)(2,1)S(1)}, u32[]{:S(2)}, u32[]{:S(2)}) collective-permute-start(bf16[256,1024]{1,0:T(8,128)(2,1)S(1)} %get-tuple-element.47.refs_0_), channel_id=1, source_target_pairs={{0,2},{2,0},{1,3},{3,1},{4,6},{6,4},{5,7},{7,5},{8,10},{10,8},{9,1... | collective-permute-start | bytes 1572872 | tf_op jit(solution)/shard_map/ppermute | solution.py:378
  31.3 15.8 %collective-permute-start.11 = (bf16[512,1024]{1,0:T(8,128)(2,1)S(1)}, bf16[512,1024]{1,0:T(8,128)(2,1)S(1)}, u32[]{:S(2)}, u32[]{:S(2)}) collective-permute-start(bf16[512,1024]{1,0:T(8,128)(2,1)S(1)} %get-tuple-element.43.refs_0_), channel_id=1, source_target_pairs={{0,1},{1,0},{2,3},{3,2},{4,5},{5,4},{6,7},{7,6},{8,9},{9,8},{10,11... | collective-permute-start | bytes 3145736 | tf_op jit(solution)/shard_map/ppermute | solution.py:384
  31.3 9.2 %collective-permute-start.6 = (bf16[128,1024]{1,0:T(8,128)(2,1)S(1)}, bf16[128,1024]{1,0:T(8,128)(2,1)S(1)}, u32[]{:S(2)}, u32[]{:S(2)}) collective-permute-start(bf16[128,1024]{1,0:T(8,128)(2,1)S(1)} %get-tuple-element.55), channel_id=1, source_target_pairs={{0,5},{1,4},{4,1},{5,0},{8,13},{9,12},{12,9},{13,8},{2,7},{3,6},{6... | collective-permute-start | bytes 786440 | tf_op jit(solution)/shard_map/ppermute | solution.py:411
  36.9 9.6 %collective-permute-start.10 = (bf16[256,1024]{1,0:T(8,128)(2,1)S(1)}, bf16[256,1024]{1,0:T(8,128)(2,1)S(1)}, u32[]{:S(2)}, u32[]{:S(2)}) collective-permute-start(bf16[256,1024]{1,0:T(8,128)(2,1)S(1)} %get-tuple-element.51.refs_1_), channel_id=1, source_target_pairs={{0,1},{1,0},{2,3},{3,2},{4,5},{5,4},{6,7},{7,6},{8,9},{9,8},{10,11... | collective-permute-start | bytes 1572872 | tf_op jit(solution)/shard_map/ppermute | solution.py:384
  37.0 10.1 %collective-permute-start.9 = (bf16[256,1024]{1,0:T(8,128)(2,1)S(1)}, bf16[256,1024]{1,0:T(8,128)(2,1)S(1)}, u32[]{:S(2)}, u32[]{:S(2)}) collective-permute-start(bf16[256,1024]{1,0:T(8,128)(2,1)S(1)} %get-tuple-element.50.refs_0_), channel_id=1, source_target_pairs={{0,1},{1,0},{2,3},{3,2},{4,5},{5,4},{6,7},{7,6},{8,9},{9,8},{10,11... | collective-permute-start | bytes 1572872 | tf_op jit(solution)/shard_map/ppermute | solution.py:384
  45.9 7.2 %copy-start.5 = (bf16[1024,2048]{1,0:T(8,128)(2,1)S(1)}, bf16[1024,2048]{1,0:T(8,128)(2,1)}, u32[]{:S(2)}) copy-start(bf16[1024,2048]{1,0:T(8,128)(2,1)} %refs_4_.3) | copy-start | bytes 12582916
  45.9 4.8 %collective-permute-start.7 = (bf16[256,1024]{1,0:T(8,128)(2,1)S(1)}, bf16[256,1024]{1,0:T(8,128)(2,1)S(1)}, u32[]{:S(2)}, u32[]{:S(2)}) collective-permute-start(bf16[256,1024]{1,0:T(8,128)(2,1)S(1)} %get-tuple-element.58.refs_3_), channel_id=1, source_target_pairs={{0,1},{1,0},{2,3},{3,2},{4,5},{5,4},{6,7},{7,6},{8,9},{9,8},{10,11... | collective-permute-start | bytes 1572872 | tf_op jit(solution)/shard_map/ppermute | solution.py:384
  46.0 4.8 %collective-permute-start.8 = (bf16[256,1024]{1,0:T(8,128)(2,1)S(1)}, bf16[256,1024]{1,0:T(8,128)(2,1)S(1)}, u32[]{:S(2)}, u32[]{:S(2)}) collective-permute-start(bf16[256,1024]{1,0:T(8,128)(2,1)S(1)} %get-tuple-element.59.refs_4_), channel_id=1, source_target_pairs={{0,1},{1,0},{2,3},{3,2},{4,5},{5,4},{6,7},{7,6},{8,9},{9,8},{10,11... | collective-permute-start | bytes 1572872 | tf_op jit(solution)/shard_map/ppermute | solution.py:384
  46.5 9.5 %collective-permute-start.12 = (bf16[128,1024]{1,0:T(8,128)(2,1)S(1)}, bf16[128,1024]{1,0:T(8,128)(2,1)S(1)}, u32[]{:S(2)}, u32[]{:S(2)}) collective-permute-start(bf16[128,1024]{1,0:T(8,128)(2,1)S(1)} %collective-permute-done.6.refs_0_), channel_id=1, source_target_pairs={{0,2},{2,0},{1,3},{3,1},{4,6},{6,4},{5,7},{7,5},{8,10},{10,8},{9,1... | collective-permute-start | bytes 786440 | tf_op jit(solution)/shard_map/ppermute | solution.py:378
  50.8 5.3 %copy-start.3 = (bf16[2048,1024]{1,0:T(8,128)(2,1)S(1)}, bf16[2048,1024]{1,0:T(8,128)(2,1)}, u32[]{:S(2)}) copy-start(bf16[2048,1024]{1,0:T(8,128)(2,1)} %refs_3_.9) | copy-start | bytes 12582916
  54.5 8.7 %collective-permute-start.14 = (bf16[128,1024]{1,0:T(8,128)(2,1)S(1)}, bf16[128,1024]{1,0:T(8,128)(2,1)S(1)}, u32[]{:S(2)}, u32[]{:S(2)}) collective-permute-start(bf16[128,1024]{1,0:T(8,128)(2,1)S(1)} %get-tuple-element.68), channel_id=1, source_target_pairs={{0,2},{2,0},{1,3},{3,1},{4,6},{6,4},{5,7},{7,5},{8,10},{10,8},{9,1... | collective-permute-start | bytes 786440 | tf_op jit(solution)/shard_map/ppermute | solution.py:378
  59.7 8.5 %collective-permute-start.13 = (bf16[128,1024]{1,0:T(8,128)(2,1)S(1)}, bf16[128,1024]{1,0:T(8,128)(2,1)S(1)}, u32[]{:S(2)}, u32[]{:S(2)}) collective-permute-start(bf16[128,1024]{1,0:T(8,128)(2,1)S(1)} %get-tuple-element.75), channel_id=1, source_target_pairs={{0,2},{2,0},{1,3},{3,1},{4,6},{6,4},{5,7},{7,5},{8,10},{10,8},{9,1... | collective-permute-start | bytes 786440 | tf_op jit(solution)/shard_map/ppermute | solution.py:378

commit v5 on v4

--- a/solution.py
+++ b/solution.py
@@ -87,20 +87,36 @@
     )
 
 
-def project_kernel(pieces, groups, parts, with_query, here_ref, *refs):
+def project_kernel(pieces, groups, parts, with_query, begun, here_ref, *refs):
     token_refs, refs = refs[: pieces * groups], refs[pieces * groups :]
     token_refs = [token_refs[k * groups : k * groups + groups] for k in range(pieces)]
     depth = token_refs[0][0].shape[1]
     spans = []
-    for step in range(pieces):
-        place = lax.rem(here_ref[SIDE] + pieces - step, pieces)
+    sides = refs[0].shape[0] // depth
+    for step in range(begun, begun + pieces):
+        place = lax.rem(here_ref[SIDE] + sides - step, sides)
         spans.append(pl.ds(pl.multiple_of(place * depth, depth), depth))
+
+    if begun:
+        weight_refs, refs = refs[:2], refs[2:]
+        sum_refs, refs = refs[:2], weight_refs + refs[2:]
+    elif parts == 0:
+        for weight_ref, sum_ref in zip(refs[:2], refs[2:]):
+            sum_ref[...] = jnp.dot(
+                jnp.concatenate([ref[...] for ref in token_refs[0]]),
+                weight_ref[spans[0], :],
+                preferred_element_type=jnp.float32,
+            )
+        return
 
     def products(weight_ref):
         width = weight_ref.shape[1]
         tile = min(512, width)
         for start in range(0, width, tile):
             total = None
+            if begun:
+                sum_ref = sum_refs[0 if weight_ref is refs[0] else 1]
+                total = sum_ref[:, start : start + tile]
             for group_refs, span in zip(token_refs, spans):
                 term = jnp.dot(
                     jnp.concatenate([ref[...] for ref in group_refs]),
@@ -137,7 +153,18 @@
     return block_refs[0].at[:rows], block_refs[0].at[rows:]
 
 
-def project(here, tokens, w_key, w_value, w_query=None, parts=2):
+def project_first(here, tokens, w_key, w_value):
+    rows = sum(a.shape[0] for a in tokens)
+    outs = [jax.ShapeDtypeStruct((rows, w_key.shape[1]), jnp.float32)] * 2
+    return call(
+        functools.partial(project_kernel, 1, len(tokens), 0, False, 0),
+        outs,
+        [here, *tokens, w_key, w_value],
+        name="project_first",
+    )
+
+
+def project(here, tokens, w_key, w_value, w_query=None, parts=2, begun=()):
     rows = sum(a.shape[0] for a in tokens[0])
     width = w_key.shape[1]
     weights = [w_key, w_value] + ([] if w_query is None else [w_query])
@@ -145,9 +172,11 @@
     if w_query is not None:
         outs += [jax.ShapeDtypeStruct((width, rows), jnp.bfloat16)]
     outs = call(
-        functools.partial(project_kernel, len(tokens), len(tokens[0]), parts, w_query is not None),
+        functools.partial(
+            project_kernel, len(tokens), len(tokens[0]), parts, w_query is not None, int(len(begun) > 0)
+        ),
         outs,
-        [here, *[a for piece in tokens for a in piece], *weights],
+        [here, *[a for piece in tokens for a in piece], *weights, *begun],
         name="project",
     )
     return (tuple(outs[:parts]), *outs[parts:])
@@ -236,39 +265,43 @@
     )
 
 
-def finish_kernel(sides, bias_start, inner, has_rim, here_ref, top_ref, total_ref, mixed_ref, *refs):
-    if has_rim:
-        bias_ref, query_ref, key_ref, value_ref, weight_ref = refs[:5]
-        refs = refs[5:]
-        hold = refs[-1]
-    else:
-        weight_ref = refs[0]
-        refs = refs[1:]
-    sent_refs, kept_ref, done = refs[: sides - 1], refs[sides - 1], refs[sides]
-    rows = kept_ref.shape[0]
-    part = kept_ref.shape[1]
+def finish_kernel(sides, blocks, inner, here_ref, top_ref, total_ref, mixed_ref, bias_ref, query_ref, *refs):
+    pairs = []
+    for parts, bias_start in blocks:
+        pairs.append((*halves_of(refs[:parts]), bias_start))
+        refs = refs[parts:]
+    weight_ref, refs = refs[0], refs[1:]
+    sent_refs, kept_ref, done, hold = refs[: sides - 1], *refs[sides - 1 :]
+    rows, part = kept_ref.shape
     spot = spot_of(here_ref, inner, rows, mixed_ref.shape[1])
     heads = mixed_ref.shape[0] // HD
     for head in range(heads):
         column = slice(head * HD, head * HD + HD)
         row = slice(head, head + 1)
-        total = total_ref[row, spot]
-        mixed = mixed_ref[column, spot]
-        if has_rim:
-            slot = hold.at[head % 2]
+        slot = hold.at[head % 2]
+        query = query_ref[column, spot]
+        before = top_ref[row, spot]
+        top, at = None, 0
+        for key_ref, _, bias_start in pairs:
             size = key_ref.shape[0]
-            before = top_ref[row, spot]
-            top = scores_of(
-                key_ref, 0, size, query_ref[column, spot], column,
-                bias_ref, bias_start, spot, slot, 0, None,
-            )
-            top = jnp.maximum(jnp.max(top, axis=0, keepdims=True), before)
-            shift = top * FACTOR
+            for first in range(0, size, 128):
+                top = scores_of(
+                    key_ref, first, first + 128, query, column,
+                    bias_ref, bias_start + first // L, spot, slot, at, top,
+                )
+                at += 128
+        top = jnp.maximum(jnp.max(top, axis=0, keepdims=True), before)
+        shift = top * FACTOR
+        keep = jnp.exp2(before * FACTOR - shift)
+        more = update = None
+        at = 0
+        for key_ref, value_ref, _ in pairs:
+            size = key_ref.shape[0]
             value = value_ref[value_place(head, size)]
-            more, update = weigh(slot, 0, size, shift, value, None, None)
-            keep = jnp.exp2(before * FACTOR - shift)
-            total = total * keep + jnp.sum(more, axis=0, keepdims=True)
-            mixed = mixed * keep + update
+            more, update = weigh(slot, at, size, shift, value, more, update)
+            at += size
+        total = total_ref[row, spot] * keep + jnp.sum(more, axis=0, keepdims=True)
+        mixed = mixed_ref[column, spot] * keep + update
         done[:, column] = (mixed / total).T.astype(done.dtype)
     for step in range(sides):
         step = (step + 1) % sides
@@ -314,24 +347,22 @@
     return pl.ds(pl.multiple_of(late * (rows - size), L), size)
 
 
-def finish(sides, here, inner, rows, state, weight, rim=None):
-    top, total, mixed = state
-    width = mixed.shape[0]
+def finish(sides, here, inner, rows, state, weight, bias, query, blocks):
+    width = query.shape[0]
     part = weight.shape[1] // sides
     outs = [jax.ShapeDtypeStruct((rows, part), jnp.bfloat16)] * (sides - 1)
     outs += [jax.ShapeDtypeStruct((rows, part), jnp.float32)]
-    scratch = [pltpu.VMEM((rows, width), jnp.bfloat16)]
-    ins = [here, top, total, mixed]
-    bias_start = 0
-    if rim is not None:
-        bias, bias_start, query, block = rim
-        ins += [bias, query, *block]
-        scratch += [pltpu.VMEM((2, block[0].shape[0], rows), jnp.float32)]
-    return call(
-        functools.partial(finish_kernel, sides, bias_start, inner, rim is not None),
+    span = sum(a.shape[0] for block, _ in blocks for a in block) // 2
+    return call(
+        functools.partial(
+            finish_kernel, sides, [(len(block), start) for block, start in blocks], inner
+        ),
         outs,
-        ins + [weight],
-        scratch=scratch,
+        [here, *state, bias, query, *[a for block, _ in blocks for a in block], weight],
+        scratch=[
+            pltpu.VMEM((rows, width), jnp.bfloat16),
+            pltpu.VMEM((2, span, rows), jnp.float32),
+        ],
         name="finish",
     )
 
@@ -415,18 +446,19 @@
     beyond = gather([beyond])
     state = attend(bias, views_here, query, [block], state)
     rim = gather([after(rim, state[0])])
-    beyond[1][0] = after(beyond[1][0], state[0], rim[0][0])
-    (block,) = project(here, beyond, w_key, w_value)
+    begun = project_first(here, [after(beyond[0][0], state[0])], w_key, w_value)
+    beyond[1][0] = after(beyond[1][0], begun[0], rim[0][0])
+    (block,) = project(here, beyond[1:], w_key, w_value, begun=begun)
     beyond_shared = share(block)
     state = attend(bias, 2 * views_here, query, [near_shared, own_shared, block], state)
-    state = attend(bias, 5 * views_here, query, [beyond_shared], state)
-
-    inner = finish(sides, here, True, rows - edge_rows, state, w_out)
-    (rim_block,) = project(here, [[after(a, inner[0]) for a in piece] for piece in rim], w_key, w_value)
-    outer = finish(
-        sides, here, False, edge_rows, [after(state[0], inner[0]), *state[1:]], w_out,
-        (bias, 6 * views_here, query, rim_block),
-    )
+
+    last = [(beyond_shared, 5 * views_here)]
+    inner = finish(sides, here, True, rows - edge_rows, state, w_out, bias, query, last)
+    rim = [[after(a, inner[0]) for a in piece] for piece in rim]
+    (rim_block,) = project(here, rim, w_key, w_value)
+    last.append((rim_block, 6 * views_here))
+    state = [after(state[0], inner[0]), *state[1:]]
+    outer = finish(sides, here, False, edge_rows, state, w_out, bias, query, last)
 
     def exchange(parts):
         return [parts[-1]] + [shift(part, step + 1) for step, part in enumerate(parts[:-1])]

time: 69.9 us -> 68.3 us (0.977)
  waiting for transfers between devices: 14.5 us -> 11.6 us
  Pallas kernels: 30.3 us -> 31 us
    ppermute x6, waiting for transfers between devices: 8.98 us -> 6.07 us  [shift(): lax.ppermute(a, 'heads', [(h, (h + step) % sides) for h in range(sides)])]
  transfers between devices with their start and end apart: 15 -> 15, of which waited for: 5 -> 6; matrix products, arithmetic and copies ran while one was open for 0% -> 0% of each run, Pallas kernels for 42% -> 44%
where the time goes in v5:
time: 68.3 us; the launch traced here: 68 us
  Pallas kernels  31 us (45%)
  starting transfers between devices  17.9 us (26%)
  waiting for transfers between devices  11.6 us (17%)
  local copies, waits for them, and re-layouts  7.08 us (10%)
    pallas_call x15, Pallas kernels, call(): pl.pallas_call(kernel, out_shape=outs, in_specs=[HBM if k in whole else S...  31 us
    unnamed x18, local copies, waits for them, and re-layouts  7.08 us
    ppermute x6, waiting for transfers between devices, shift(): lax.ppermute(a, 'heads', [(h, (h + step) % sides) for h in range(sides)])  6.07 us
    ppermute x6, starting transfers between devices, shift(): lax.ppermute(a, 'heads', [(h, (h + step) % sides) for h in range(sides)])  6.01 us
    ppermute x1, waiting for transfers between devices, shards(): outer = lax.ppermute(outer, 'views', [(0, 3), (3, 0)])  4.73 us
    ppermute x1, starting transfers between devices, shards(): outer = lax.ppermute(outer, 'views', [(0, 3), (3, 0)])  4.5 us
    ppermute x1, starting transfers between devices, shards(): near = lax.ppermute(tokens, 'views', pair)  3.02 us
    ppermute x1, starting transfers between devices, shards(): rim = lax.ppermute(rim, ('views', 'sub'), cross)  2.56 us
  transfers between devices with their start and end apart: 15, of which 6 were waited for; matrix products, arithmetic and copies ran while one was open for 0% of the time, Pallas kernels for 44%

profile of v5, /device:TPU:0, one launch (start us, length us, event | category | flops | bytes accessed | tf_op | source)
XLA Modules:
  0.0 68.0 jit_solution(1372018334018267928)
XLA Ops:
  0.0 3.0 %collective-permute-start.1 = (bf16[256,1024]{1,0:T(8,128)(2,1)}, bf16[256,1024]{1,0:T(8,128)(2,1)S(1)}, u32[]{:S(2)}, u32[]{:S(2)}) collective-permute-start(bf16[256,1024]{1,0:T(8,128)(2,1)} %refs_0_.1), channel_id=1, source_target_pairs={{0,4},{4,0},{8,12},{12,8},{1,5},{5,1},{9,13},{13,9},{2,6},{6,2},{1... | collective-permute-start | bytes 1572872 | tf_op jit(solution)/shard_map/ppermute | solution.py:421
  3.0 1.5 %collective-permute-start = (bf16[256,1024]{1,0:T(8,128)(2,1)}, bf16[256,1024]{1,0:T(8,128)(2,1)S(1)}, u32[]{:S(2)}, u32[]{:S(2)}) collective-permute-start(bf16[256,1024]{1,0:T(8,128)(2,1)} %refs_0_.1), channel_id=1, source_target_pairs={{0,2},{2,0},{1,3},{3,1},{4,6},{6,4},{5,7},{7,5},{8,10},{10,8},{9,1... | collective-permute-start | bytes 1572872 | tf_op jit(solution)/shard_map/ppermute | solution.py:409
  4.5 0.7 %collective-permute-start.3 = (bf16[256,1024]{1,0:T(8,128)(2,1)}, bf16[256,1024]{1,0:T(8,128)(2,1)S(1)}, u32[]{:S(2)}, u32[]{:S(2)}) collective-permute-start(bf16[256,1024]{1,0:T(8,128)(2,1)} %refs_0_.1), channel_id=1, source_target_pairs={{4,8},{8,4},{5,9},{9,5},{6,10},{10,6},{7,11},{11,7},{20,24},{24,20... | collective-permute-start | bytes 1572872 | tf_op jit(solution)/shard_map/ppermute | solution.py:424
  5.2 0.1 pad_add_fusion.here_ref.refs_0_
  5.3 2.2 %copy-done = bf16[2048,1024]{1,0:T(8,128)(2,1)S(1)} copy-done((bf16[2048,1024]{1,0:T(8,128)(2,1)S(1)}, bf16[2048,1024]{1,0:T(8,128)(2,1)}, u32[]{:S(2)}) %copy-start) | copy-done | bytes 4194328
  7.5 2.2 %copy-done.2 = bf16[2048,1024]{1,0:T(8,128)(2,1)S(1)} copy-done((bf16[2048,1024]{1,0:T(8,128)(2,1)S(1)}, bf16[2048,1024]{1,0:T(8,128)(2,1)}, u32[]{:S(2)}) %copy-start.2) | copy-done | bytes 4194328
  9.7 2.2 %copy-done.4 = bf16[2048,1024]{1,0:T(8,128)(2,1)S(1)} copy-done((bf16[2048,1024]{1,0:T(8,128)(2,1)S(1)}, bf16[2048,1024]{1,0:T(8,128)(2,1)}, u32[]{:S(2)}) %copy-start.4) | copy-done | bytes 4194328
  11.9 0.5 fetch.1.refs_0_
  12.4 0.5 copy-done.6
  12.9 4.5 %collective-permute-start.4 = (bf16[256,1024]{1,0:T(8,128)(2,1)S(1)}, bf16[256,1024]{1,0:T(8,128)(2,1)S(1)}, u32[]{:S(2)}, u32[]{:S(2)}) collective-permute-start(bf16[256,1024]{1,0:T(8,128)(2,1)S(1)} %copy-done.6), channel_id=1, source_target_pairs={{0,12},{12,0},{1,13},{13,1},{2,14},{14,2},{3,15},{15,3},{16,28},{2... | collective-permute-start | bytes 1572872 | tf_op jit(solution)/shard_map/ppermute | solution.py:426
  17.4 0.0 collective-permute-done.1.refs_0_
  17.4 0.6 collective-permute-start.2
  18.0 0.0 collective-permute-done.refs_1_
  18.0 4.1 %project.4 = (bf16[512,1024]{1,0:T(8,128)(2,1)S(1)}, bf16[1024,256]{1,0:T(8,128)(2,1)S(1)}) custom-call(s32[3]{0:T(128)S(1)} %pad_add_fusion.here_ref.refs_0_, bf16[256,1024]{1,0:T(8,128)(2,1)S(1)} %copy-done.6, bf16[256,1024]{1,0:T(8,128)(2,1)S(1)} %collective-permute-done.refs_1_, bf16[2048,1024]{1,0:T(8,128)(2,1)S(1)} %copy-done, ...), custom_call_target="tpu_custom_call" | custom-call | tf_op jit(solution)/shard_map/project/pallas_call | solution.py:24
  22.1 0.7 %mask.1.bias_ref = f32[26,256]{1,0:T(8,128)S(1)} custom-call(s32[3]{0:T(128)S(1)} %pad_add_fusion.here_ref.refs_0_, s32[4]{0:T(128)S(1)} %copy-done.8, s32[4,20]{1,0:T(4,128)S(1)} %copy-done.7, f32[8,128]{1,0:T(8,128)S(1)} %fetch.1.refs_0_), custom_call_target="tpu_custom_call" | custom-call | tf_op jit(solution)/shard_map/mask/pallas_call | solution.py:24
  22.9 2.3 %attend.3 = (f32[8,256]{1,0:T(8,128)S(1)}, f32[8,256]{1,0:T(8,128)S(1)}, f32[1024,256]{1,0:T(8,128)S(1)}) custom-call(f32[26,256]{1,0:T(8,128)S(1)} %mask.1.bias_ref, bf16[1024,256]{1,0:T(8,128)(2,1)S(1)} %get-tuple-element.41.query_ref, bf16[512,1024]{1,0:T(8,128)(2,1)S(1)} %get-tuple-element.44.refs_0_), custom_call_target="tpu_custom_call" | custom-call | tf_op jit(solution)/shard_map/attend/pallas_call | solution.py:24
  25.2 4.7 %collective-permute-done.4.outer_ref = bf16[256,1024]{1,0:T(8,128)(2,1)S(1)} collective-permute-done((bf16[256,1024]{1,0:T(8,128)(2,1)S(1)}, bf16[256,1024]{1,0:T(8,128)(2,1)S(1)}, u32[]{:S(2)}, u32[]{:S(2)}) %collective-permute-start.4) | collective-permute-done | bytes 524320 | tf_op jit(solution)/shard_map/ppermute | solution.py:426
  29.9 0.8 %pick.1 = (bf16[256,1024]{1,0:T(8,128)(2,1)S(1)}, bf16[128,1024]{1,0:T(8,128)(2,1)S(1)}) custom-call(s32[3]{0:T(128)S(1)} %pad_add_fusion.here_ref.refs_0_, bf16[256,1024]{1,0:T(8,128)(2,1)S(1)} %collective-permute-done.3.inner_ref, bf16[256,1024]{1,0:T(8,128)(2,1)S(1)} %collective-permute-done.4.outer_ref), custom_call_target="tpu_custom_call" | custom-call | tf_op jit(solution)/shard_map/pick/pallas_call | solution.py:24
  30.7 0.6 collective-permute-start.8
  31.3 0.0 collective-permute-start.7
  31.3 2.6 %collective-permute-start.9 = (bf16[128,1024]{1,0:T(8,128)(2,1)S(1)}, bf16[128,1024]{1,0:T(8,128)(2,1)S(1)}, u32[]{:S(2)}, u32[]{:S(2)}) collective-permute-start(bf16[128,1024]{1,0:T(8,128)(2,1)S(1)} %get-tuple-element.57), channel_id=1, source_target_pairs={{0,5},{1,4},{4,1},{5,0},{8,13},{9,12},{12,9},{13,8},{2,7},{3,6},{6... | collective-permute-start | bytes 786440 | tf_op jit(solution)/shard_map/ppermute | solution.py:442
  33.9 0.0 collective-permute-done.2.refs_1_
  33.9 3.0 %project.5 = (bf16[256,1024]{1,0:T(8,128)(2,1)S(1)}, bf16[256,1024]{1,0:T(8,128)(2,1)S(1)}) custom-call(s32[3]{0:T(128)S(1)} %pad_add_fusion.here_ref.refs_0_, bf16[256,1024]{1,0:T(8,128)(2,1)S(1)} %collective-permute-done.1.refs_0_, bf16[256,1024]{1,0:T(8,128)(2,1)S(1)} %collective-permute-done.2.refs_1_, bf16[2048,1024]{1,0:T(8,128)(2,1)S(1)} %copy-done.1, ...), custom_call_target="tpu_custom_call" | custom-call | tf_op jit(solution)/shard_map/project/pallas_call | solution.py:24
  36.9 0.1 collective-permute-start.5
  37.0 0.5 collective-permute-start.6
  37.5 2.3 %attend.4 = (f32[8,256]{1,0:T(8,128)S(1)}, f32[8,256]{1,0:T(8,128)S(1)}, f32[1024,256]{1,0:T(8,128)S(1)}) custom-call(f32[26,256]{1,0:T(8,128)S(1)} %mask.1.bias_ref, bf16[1024,256]{1,0:T(8,128)(2,1)S(1)} %get-tuple-element.41.query_ref, bf16[256,1024]{1,0:T(8,128)(2,1)S(1)} %get-tuple-element.50.refs_0_, bf16[256,1024]{1,0:T(8,128)(2,1)S(1)} %get-tuple-element.51.refs_1_, ...), custom_call_target="tpu_custom_call" | custom-call | tf_op jit(solution)/shard_map/attend/pallas_call | solution.py:24
  39.8 0.8 %collective-permute-done.9.refs_0_ = bf16[128,1024]{1,0:T(8,128)(2,1)S(1)} collective-permute-done((bf16[128,1024]{1,0:T(8,128)(2,1)S(1)}, bf16[128,1024]{1,0:T(8,128)(2,1)S(1)}, u32[]{:S(2)}, u32[]{:S(2)}) %collective-permute-start.9) | collective-permute-done | bytes 262176 | tf_op jit(solution)/shard_map/ppermute | solution.py:442
  40.6 1.8 %project_first.1 = (f32[256,1024]{1,0:T(8,128)S(1)}, f32[256,1024]{1,0:T(8,128)S(1)}) custom-call(s32[3]{0:T(128)S(1)} %pad_add_fusion.here_ref.refs_0_, bf16[256,1024]{1,0:T(8,128)(2,1)S(1)} %get-tuple-element.55.refs_0_, bf16[2048,1024]{1,0:T(8,128)(2,1)S(1)} %copy-done.1, bf16[2048,1024]{1,0:T(8,128)(2,1)S(1)} %copy-done.2), custom_call_target="tpu_custom_call" | custom-call | tf_op jit(solution)/shard_map/project_first/pallas_call | solution.py:24
  42.4 0.6 collective-permute-done.8.refs_0_
  42.9 2.0 %project.6 = (bf16[256,1024]{1,0:T(8,128)(2,1)S(1)}, bf16[256,1024]{1,0:T(8,128)(2,1)S(1)}) custom-call(s32[3]{0:T(128)S(1)} %pad_add_fusion.here_ref.refs_0_, bf16[256,1024]{1,0:T(8,128)(2,1)S(1)} %collective-permute-done.8.refs_0_, bf16[2048,1024]{1,0:T(8,128)(2,1)S(1)} %copy-done.1, bf16[2048,1024]{1,0:T(8,128)(2,1)S(1)} %copy-done.2, ...), custom_call_target="tpu_custom_call" | custom-call | tf_op jit(solution)/shard_map/project/pallas_call | solution.py:24
  44.9 0.0 copy-start.5
  44.9 0.1 collective-permute-start.10
  45.0 0.5 collective-permute-start.11
  45.5 0.9 %collective-permute-start.12 = (bf16[128,1024]{1,0:T(8,128)(2,1)S(1)}, bf16[128,1024]{1,0:T(8,128)(2,1)S(1)}, u32[]{:S(2)}, u32[]{:S(2)}) collective-permute-start(bf16[128,1024]{1,0:T(8,128)(2,1)S(1)} %collective-permute-done.9.refs_0_), channel_id=1, source_target_pairs={{0,2},{2,0},{1,3},{3,1},{4,6},{6,4},{5,7},{7,5},{8,10},{10,8},{9,1... | collective-permute-start | bytes 786440 | tf_op jit(solution)/shard_map/ppermute | solution.py:409
  46.4 3.7 %attend.5 = (f32[8,256]{1,0:T(8,128)S(1)}, f32[8,256]{1,0:T(8,128)S(1)}, f32[1024,256]{1,0:T(8,128)S(1)}) custom-call(f32[26,256]{1,0:T(8,128)S(1)} %mask.1.bias_ref, bf16[1024,256]{1,0:T(8,128)(2,1)S(1)} %get-tuple-element.41.query_ref, bf16[256,1024]{1,0:T(8,128)(2,1)S(1)} %collective-permute-done.5.refs_0_, ...), custom_call_target="tpu_custom_call" | custom-call | tf_op jit(solution)/shard_map/attend/pallas_call | solution.py:24
  50.2 0.0 copy-start.3
  50.2 0.0 collective-permute-done.10.refs_0_
  50.2 0.0 collective-permute-done.11.refs_1_
  50.2 1.9 %finish.2 = (bf16[128,1024]{1,0:T(8,128)(2,1)S(1)}, f32[128,1024]{1,0:T(8,128)S(1)}) custom-call(s32[3]{0:T(128)S(1)} %pad_add_fusion.here_ref.refs_0_, f32[8,256]{1,0:T(8,128)S(1)} %get-tuple-element.69.top_ref, f32[8,256]{1,0:T(8,128)S(1)} %get-tuple-element.66.total_ref, f32[1024,256]{1,0:T(8,128)S(1)} %get-tuple-element.67.mixed_ref, ...), custom_call_target="tpu_custom_call" | custom-call | tf_op jit(solution)/shard_map/finish/pallas_call | solution.py:24
  52.1 1.2 %collective-permute-start.14 = (bf16[128,1024]{1,0:T(8,128)(2,1)S(1)}, bf16[128,1024]{1,0:T(8,128)(2,1)S(1)}, u32[]{:S(2)}, u32[]{:S(2)}) collective-permute-start(bf16[128,1024]{1,0:T(8,128)(2,1)S(1)} %get-tuple-element.68), channel_id=1, source_target_pairs={{0,2},{2,0},{1,3},{3,1},{4,6},{6,4},{5,7},{7,5},{8,10},{10,8},{9,1... | collective-permute-start | bytes 786440 | tf_op jit(solution)/shard_map/ppermute | solution.py:409
  53.3 0.5 collective-permute-done.12.refs_1_
  53.8 1.9 %project.7 = (bf16[128,1024]{1,0:T(8,128)(2,1)S(1)}, bf16[128,1024]{1,0:T(8,128)(2,1)S(1)}) custom-call(s32[3]{0:T(128)S(1)} %pad_add_fusion.here_ref.refs_0_, bf16[128,1024]{1,0:T(8,128)(2,1)S(1)} %collective-permute-done.9.refs_0_, bf16[128,1024]{1,0:T(8,128)(2,1)S(1)} %collective-permute-done.12.refs_1_, bf16[2048,1024]{1,0:T(8,128)(2,1)S(1)} %copy-done.1, ...), custom_call_target="tpu_custom_call" | custom-call | tf_op jit(solution)/shard_map/project/pallas_call | solution.py:24
  55.7 3.3 %finish.3 = (bf16[128,1024]{1,0:T(8,128)(2,1)S(1)}, f32[128,1024]{1,0:T(8,128)S(1)}) custom-call(s32[3]{0:T(128)S(1)} %pad_add_fusion.here_ref.refs_0_, f32[8,256]{1,0:T(8,128)S(1)} %get-tuple-element.69.top_ref, f32[8,256]{1,0:T(8,128)S(1)} %get-tuple-element.66.total_ref, f32[1024,256]{1,0:T(8,128)S(1)} %get-tuple-element.67.mixed_ref, ...), custom_call_target="tpu_custom_call" | custom-call | tf_op jit(solution)/shard_map/finish/pallas_call | solution.py:24
  59.0 1.2 %collective-permute-start.13 = (bf16[128,1024]{1,0:T(8,128)(2,1)S(1)}, bf16[128,1024]{1,0:T(8,128)(2,1)S(1)}, u32[]{:S(2)}, u32[]{:S(2)}) collective-permute-start(bf16[128,1024]{1,0:T(8,128)(2,1)S(1)} %get-tuple-element.75), channel_id=1, source_target_pairs={{0,2},{2,0},{1,3},{3,1},{4,6},{6,4},{5,7},{7,5},{8,10},{10,8},{9,1... | collective-permute-start | bytes 786440 | tf_op jit(solution)/shard_map/ppermute | solution.py:409
  60.3 0.2 collective-permute-done.14.refs_1_
  60.4 1.3 %settle.2.refs_2_ = bf16[256,1024]{1,0:T(8,128)(2,1)} custom-call(s32[3]{0:T(128)S(1)} %pad_add_fusion.here_ref.refs_0_, f32[128,1024]{1,0:T(8,128)S(1)} %get-tuple-element.76.refs_0_, bf16[128,1024]{1,0:T(8,128)(2,1)S(1)} %collective-permute-done.14.refs_1_), custom_call_target="tpu_custom_call" | custom-call | tf_op jit(solution)/shard_map/settle/pallas_call | solution.py:24
  61.7 4.8 %collective-permute-done.13.refs_1_ = bf16[128,1024]{1,0:T(8,128)(2,1)S(1)} collective-permute-done((bf16[128,1024]{1,0:T(8,128)(2,1)S(1)}, bf16[128,1024]{1,0:T(8,128)(2,1)S(1)}, u32[]{:S(2)}, u32[]{:S(2)}) %collective-permute-start.13) | collective-permute-done | bytes 262176 | tf_op jit(solution)/shard_map/ppermute | solution.py:409
  66.6 1.3 %settle.3 = bf16[256,1024]{1,0:T(8,128)(2,1)} custom-call(s32[3]{0:T(128)S(1)} %pad_add_fusion.here_ref.refs_0_, f32[128,1024]{1,0:T(8,128)S(1)} %get-tuple-element.74.refs_0_, bf16[128,1024]{1,0:T(8,128)(2,1)S(1)} %collective-permute-done.13.refs_1_, bf16[256,1024]{1,0:T(8,128)(2,1)} %settle.2.refs_2_), custom_call_target="tpu_custom_call", output_to_operand_aliasing={{}: (3, {})} | custom-call | tf_op jit(solution)/shard_map/settle/pallas_call | solution.py:24
  (16 shorter events, 0.0 us)
Async XLA Ops:
  0.0 17.4 %collective-permute-start.1 = (bf16[256,1024]{1,0:T(8,128)(2,1)}, bf16[256,1024]{1,0:T(8,128)(2,1)S(1)}, u32[]{:S(2)}, u32[]{:S(2)}) collective-permute-start(bf16[256,1024]{1,0:T(8,128)(2,1)} %refs_0_.1), channel_id=1, source_target_pairs={{0,4},{4,0},{8,12},{12,8},{1,5},{5,1},{9,13},{13,9},{2,6},{6,2},{1... | collective-permute-start | bytes 1572872 | tf_op jit(solution)/shard_map/ppermute | solution.py:421
  3.0 15.0 %collective-permute-start = (bf16[256,1024]{1,0:T(8,128)(2,1)}, bf16[256,1024]{1,0:T(8,128)(2,1)S(1)}, u32[]{:S(2)}, u32[]{:S(2)}) collective-permute-start(bf16[256,1024]{1,0:T(8,128)(2,1)} %refs_0_.1), channel_id=1, source_target_pairs={{0,2},{2,0},{1,3},{3,1},{4,6},{6,4},{5,7},{7,5},{8,10},{10,8},{9,1... | collective-permute-start | bytes 1572872 | tf_op jit(solution)/shard_map/ppermute | solution.py:409
  4.5 20.7 %collective-permute-start.3 = (bf16[256,1024]{1,0:T(8,128)(2,1)}, bf16[256,1024]{1,0:T(8,128)(2,1)S(1)}, u32[]{:S(2)}, u32[]{:S(2)}) collective-permute-start(bf16[256,1024]{1,0:T(8,128)(2,1)} %refs_0_.1), channel_id=1, source_target_pairs={{4,8},{8,4},{5,9},{9,5},{6,10},{10,6},{7,11},{11,7},{20,24},{24,20... | collective-permute-start | bytes 1572872 | tf_op jit(solution)/shard_map/ppermute | solution.py:424
  5.3 2.2 %copy-start = (bf16[2048,1024]{1,0:T(8,128)(2,1)S(1)}, bf16[2048,1024]{1,0:T(8,128)(2,1)}, u32[]{:S(2)}) copy-start(bf16[2048,1024]{1,0:T(8,128)(2,1)} %refs_2_.13) | copy-start | bytes 12582916
  7.5 2.2 %copy-start.2 = (bf16[2048,1024]{1,0:T(8,128)(2,1)S(1)}, bf16[2048,1024]{1,0:T(8,128)(2,1)}, u32[]{:S(2)}) copy-start(bf16[2048,1024]{1,0:T(8,128)(2,1)} %refs_3_.7) | copy-start | bytes 12582916
  9.7 2.2 %copy-start.4 = (bf16[2048,1024]{1,0:T(8,128)(2,1)S(1)}, bf16[2048,1024]{1,0:T(8,128)(2,1)}, u32[]{:S(2)}) copy-start(bf16[2048,1024]{1,0:T(8,128)(2,1)} %refs_3_.5) | copy-start | bytes 12582916
  11.9 1.0 %copy-start.6 = (bf16[256,1024]{1,0:T(8,128)(2,1)S(1)}, bf16[256,1024]{1,0:T(8,128)(2,1)}, u32[]{:S(2)}) copy-start(bf16[256,1024]{1,0:T(8,128)(2,1)} %refs_0_.1) | copy-start | bytes 1572868
  12.9 9.2 %copy-start.7 = (s32[4,20]{1,0:T(4,128)S(1)}, s32[4,20]{1,0:T(4,128)}, u32[]{:S(2)}) copy-start(s32[4,20]{1,0:T(4,128)} %partners_ref.1) | copy-start | bytes 964
  12.9 9.2 %copy-start.8 = (s32[4]{0:T(128)S(1)}, s32[4]{0:T(128)}, u32[]{:S(2)}) copy-start(s32[4]{0:T(128)} %counts_ref.1) | copy-start | bytes 52
  12.9 17.0 %collective-permute-start.4 = (bf16[256,1024]{1,0:T(8,128)(2,1)S(1)}, bf16[256,1024]{1,0:T(8,128)(2,1)S(1)}, u32[]{:S(2)}, u32[]{:S(2)}) collective-permute-start(bf16[256,1024]{1,0:T(8,128)(2,1)S(1)} %copy-done.6), channel_id=1, source_target_pairs={{0,12},{12,0},{1,13},{13,1},{2,14},{14,2},{3,15},{15,3},{16,28},{2... | collective-permute-start | bytes 1572872 | tf_op jit(solution)/shard_map/ppermute | solution.py:426
  17.4 16.5 %collective-permute-start.2 = (bf16[256,1024]{1,0:T(8,128)(2,1)S(1)}, bf16[256,1024]{1,0:T(8,128)(2,1)S(1)}, u32[]{:S(2)}, u32[]{:S(2)}) collective-permute-start(bf16[256,1024]{1,0:T(8,128)(2,1)S(1)} %collective-permute-done.1.refs_0_), channel_id=1, source_target_pairs={{0,2},{2,0},{1,3},{3,1},{4,6},{6,4},{5,7},{7,5},{8,10},{10,8},{9,1... | collective-permute-start | bytes 1572872 | tf_op jit(solution)/shard_map/ppermute | solution.py:409
  18.0 15.9 %copy-start.1 = (bf16[2048,1024]{1,0:T(8,128)(2,1)S(1)}, bf16[2048,1024]{1,0:T(8,128)(2,1)}, u32[]{:S(2)}) copy-start(bf16[2048,1024]{1,0:T(8,128)(2,1)} %refs_2_.13) | copy-start | bytes 12582916
  30.7 12.2 %collective-permute-start.8 = (bf16[256,1024]{1,0:T(8,128)(2,1)S(1)}, bf16[256,1024]{1,0:T(8,128)(2,1)S(1)}, u32[]{:S(2)}, u32[]{:S(2)}) collective-permute-start(bf16[256,1024]{1,0:T(8,128)(2,1)S(1)} %get-tuple-element.55.refs_0_), channel_id=1, source_target_pairs={{0,2},{2,0},{1,3},{3,1},{4,6},{6,4},{5,7},{7,5},{8,10},{10,8},{9,1... | collective-permute-start | bytes 1572872 | tf_op jit(solution)/shard_map/ppermute | solution.py:409
  31.3 15.1 %collective-permute-start.7 = (bf16[512,1024]{1,0:T(8,128)(2,1)S(1)}, bf16[512,1024]{1,0:T(8,128)(2,1)S(1)}, u32[]{:S(2)}, u32[]{:S(2)}) collective-permute-start(bf16[512,1024]{1,0:T(8,128)(2,1)S(1)} %get-tuple-element.44.refs_0_), channel_id=1, source_target_pairs={{0,1},{1,0},{2,3},{3,2},{4,5},{5,4},{6,7},{7,6},{8,9},{9,8},{10,11... | collective-permute-start | bytes 3145736 | tf_op jit(solution)/shard_map/ppermute | solution.py:415
  31.3 9.2 %collective-permute-start.9 = (bf16[128,1024]{1,0:T(8,128)(2,1)S(1)}, bf16[128,1024]{1,0:T(8,128)(2,1)S(1)}, u32[]{:S(2)}, u32[]{:S(2)}) collective-permute-start(bf16[128,1024]{1,0:T(8,128)(2,1)S(1)} %get-tuple-element.57), channel_id=1, source_target_pairs={{0,5},{1,4},{4,1},{5,0},{8,13},{9,12},{12,9},{13,8},{2,7},{3,6},{6... | collective-permute-start | bytes 786440 | tf_op jit(solution)/shard_map/ppermute | solution.py:442
  36.9 8.6 %collective-permute-start.5 = (bf16[256,1024]{1,0:T(8,128)(2,1)S(1)}, bf16[256,1024]{1,0:T(8,128)(2,1)S(1)}, u32[]{:S(2)}, u32[]{:S(2)}) collective-permute-start(bf16[256,1024]{1,0:T(8,128)(2,1)S(1)} %get-tuple-element.50.refs_0_), channel_id=1, source_target_pairs={{0,1},{1,0},{2,3},{3,2},{4,5},{5,4},{6,7},{7,6},{8,9},{9,8},{10,11... | collective-permute-start | bytes 1572872 | tf_op jit(solution)/shard_map/ppermute | solution.py:415
  37.0 9.4 %collective-permute-start.6 = (bf16[256,1024]{1,0:T(8,128)(2,1)S(1)}, bf16[256,1024]{1,0:T(8,128)(2,1)S(1)}, u32[]{:S(2)}, u32[]{:S(2)}) collective-permute-start(bf16[256,1024]{1,0:T(8,128)(2,1)S(1)} %get-tuple-element.51.refs_1_), channel_id=1, source_target_pairs={{0,1},{1,0},{2,3},{3,2},{4,5},{5,4},{6,7},{7,6},{8,9},{9,8},{10,11... | collective-permute-start | bytes 1572872 | tf_op jit(solution)/shard_map/ppermute | solution.py:415
  44.9 5.3 %copy-start.5 = (bf16[1024,2048]{1,0:T(8,128)(2,1)S(1)}, bf16[1024,2048]{1,0:T(8,128)(2,1)}, u32[]{:S(2)}) copy-start(bf16[1024,2048]{1,0:T(8,128)(2,1)} %refs_4_.3) | copy-start | bytes 12582916
  44.9 5.3 %collective-permute-start.10 = (bf16[256,1024]{1,0:T(8,128)(2,1)S(1)}, bf16[256,1024]{1,0:T(8,128)(2,1)S(1)}, u32[]{:S(2)}, u32[]{:S(2)}) collective-permute-start(bf16[256,1024]{1,0:T(8,128)(2,1)S(1)} %get-tuple-element.61.refs_3_), channel_id=1, source_target_pairs={{0,1},{1,0},{2,3},{3,2},{4,5},{5,4},{6,7},{7,6},{8,9},{9,8},{10,11... | collective-permute-start | bytes 1572872 | tf_op jit(solution)/shard_map/ppermute | solution.py:415
  45.0 5.2 %collective-permute-start.11 = (bf16[256,1024]{1,0:T(8,128)(2,1)S(1)}, bf16[256,1024]{1,0:T(8,128)(2,1)S(1)}, u32[]{:S(2)}, u32[]{:S(2)}) collective-permute-start(bf16[256,1024]{1,0:T(8,128)(2,1)S(1)} %get-tuple-element.62.refs_4_), channel_id=1, source_target_pairs={{0,1},{1,0},{2,3},{3,2},{4,5},{5,4},{6,7},{7,6},{8,9},{9,8},{10,11... | collective-permute-start | bytes 1572872 | tf_op jit(solution)/shard_map/ppermute | solution.py:415
  45.5 8.3 %collective-permute-start.12 = (bf16[128,1024]{1,0:T(8,128)(2,1)S(1)}, bf16[128,1024]{1,0:T(8,128)(2,1)S(1)}, u32[]{:S(2)}, u32[]{:S(2)}) collective-permute-start(bf16[128,1024]{1,0:T(8,128)(2,1)S(1)} %collective-permute-done.9.refs_0_), channel_id=1, source_target_pairs={{0,2},{2,0},{1,3},{3,1},{4,6},{6,4},{5,7},{7,5},{8,10},{10,8},{9,1... | collective-permute-start | bytes 786440 | tf_op jit(solution)/shard_map/ppermute | solution.py:409
  50.2 3.6 %copy-start.3 = (bf16[2048,1024]{1,0:T(8,128)(2,1)S(1)}, bf16[2048,1024]{1,0:T(8,128)(2,1)}, u32[]{:S(2)}) copy-start(bf16[2048,1024]{1,0:T(8,128)(2,1)} %refs_3_.7) | copy-start | bytes 12582916
  52.1 8.3 %collective-permute-start.14 = (bf16[128,1024]{1,0:T(8,128)(2,1)S(1)}, bf16[128,1024]{1,0:T(8,128)(2,1)S(1)}, u32[]{:S(2)}, u32[]{:S(2)}) collective-permute-start(bf16[128,1024]{1,0:T(8,128)(2,1)S(1)} %get-tuple-element.68), channel_id=1, source_target_pairs={{0,2},{2,0},{1,3},{3,1},{4,6},{6,4},{5,7},{7,5},{8,10},{10,8},{9,1... | collective-permute-start | bytes 786440 | tf_op jit(solution)/shard_map/ppermute | solution.py:409
  59.0 7.5 %collective-permute-start.13 = (bf16[128,1024]{1,0:T(8,128)(2,1)S(1)}, bf16[128,1024]{1,0:T(8,128)(2,1)S(1)}, u32[]{:S(2)}, u32[]{:S(2)}) collective-permute-start(bf16[128,1024]{1,0:T(8,128)(2,1)S(1)} %get-tuple-element.75), channel_id=1, source_target_pairs={{0,2},{2,0},{1,3},{3,1},{4,6},{6,4},{5,7},{7,5},{8,10},{10,8},{9,1... | collective-permute-start | bytes 786440 | tf_op jit(solution)/shard_map/ppermute | solution.py:409

commit v6 on v5

--- a/solution.py
+++ b/solution.py
@@ -184,60 +184,82 @@
 
 def scores_of(key_ref, first, last, query, column, bias_ref, bias_row, lanes, hold_ref, at, top):
     scores = jnp.dot(key_ref[first:last, column], query, preferred_element_type=jnp.float32)
+    hold_ref[at : at + last - first, :] = scores
     for view in range((last - first) // L):
-        piece = scores[view * L : view * L + L] + bias_ref[bias_row + view : bias_row + view + 1, lanes]
-        hold_ref[at + view * L : at + view * L + L, :] = piece
+        piece = scores[view * L : view * L + L]
         best = jnp.max(piece.reshape(L // 8, 8, piece.shape[1]), axis=0)
+        best = best + bias_ref[bias_row + view : bias_row + view + 1, lanes]
         top = best if top is None else jnp.maximum(top, best)
     return top
 
 
-def weigh(hold_ref, at, size, shift, value, total, mixed):
-    weights = jnp.exp2(hold_ref[at : at + size, :] * FACTOR - shift)
-    term = jnp.sum(weights.reshape(size // 8, 8, weights.shape[1]), axis=0)
-    total = term if total is None else total + term
-    update = jnp.dot(value, weights.astype(jnp.bfloat16), preferred_element_type=jnp.float32)
+def weigh(hold_ref, at, size, bias_ref, bias_row, lanes, shift, value, total, mixed):
+    weights = []
+    for view in range(size // L):
+        offset = bias_ref[bias_row + view : bias_row + view + 1, lanes] - shift
+        piece = hold_ref[at + view * L : at + view * L + L, :] * FACTOR + offset
+        weights.append(jnp.exp2(piece))
+        term = jnp.sum(weights[-1].reshape(L // 8, 8, piece.shape[1]), axis=0)
+        total = term if total is None else total + term
+    weights = jnp.concatenate([w.astype(jnp.bfloat16) for w in weights])
+    update = jnp.dot(value, weights, preferred_element_type=jnp.float32)
     mixed = update if mixed is None else mixed + update
     return total, mixed
 
 
-def attend_kernel(blocks, bias_start, has_state, bias_ref, query_ref, *refs):
+def attend_head(head, pairs, query, bias_ref, lanes, hold_ref):
+    column = slice(head * HD, head * HD + HD)
+    top, at = None, 0
+    for key_ref, _, bias_row in pairs:
+        size = key_ref.shape[0]
+        for first in range(0, size, 128):
+            top = scores_of(
+                key_ref, first, first + 128, query, column,
+                bias_ref, bias_row + first // L, lanes, hold_ref, at, top,
+            )
+            at += 128
+
+    def weighed(shift):
+        total, mixed, at = None, None, 0
+        for key_ref, value_ref, bias_row in pairs:
+            size = key_ref.shape[0]
+            value = value_ref[value_place(head, size)]
+            total, mixed = weigh(
+                hold_ref, at, size, bias_ref, bias_row, lanes, shift, value, total, mixed
+            )
+            at += size
+        return jnp.sum(total, axis=0, keepdims=True), mixed
+
+    return jnp.max(top, axis=0, keepdims=True), weighed
+
+
+def attend_kernel(blocks, has_state, bias_ref, query_ref, *refs):
     pairs = []
-    for parts in blocks:
-        pairs.append(halves_of(refs[:parts]))
+    for parts, bias_row in blocks:
+        pairs.append((*halves_of(refs[:parts]), bias_row))
         refs = refs[parts:]
     if has_state:
         top_in, total_in, mixed_in, top_out, total_out, mixed_out, hold = refs
     else:
         top_out, total_out, mixed_out, hold = refs
     heads = query_ref.shape[0] // HD
-    everything = slice(None)
+
+    def begin(head):
+        query = query_ref[head * HD : head * HD + HD, :]
+        return attend_head(head, pairs, query, bias_ref, slice(None), hold.at[head % 2])
+
+    following = begin(0)
     for head in range(heads):
+        top, weighed = following
+        if head + 1 < heads:
+            following = begin(head + 1)
         column = slice(head * HD, head * HD + HD)
         row = slice(head, head + 1)
-        query = query_ref[column, :]
-        slot = hold.at[head % 2]
-        top, at, groups = None, 0, []
-        for key_ref, value_ref in pairs:
-            size = key_ref.shape[0]
-            step = min(128, size)
-            groups.append((at, size, value_ref))
-            for first in range(0, size, step):
-                top = scores_of(
-                    key_ref, first, first + step, query, column,
-                    bias_ref, bias_start + at // L, everything, slot, at, top,
-                )
-                at += step
-        top = jnp.max(top, axis=0, keepdims=True)
-        total = mixed = None
         if has_state:
             before = top_in[row, :]
             top = jnp.maximum(top, before)
         shift = top * FACTOR
-        for at, size, value_ref in groups:
-            value = value_ref[value_place(head, size)]
-            total, mixed = weigh(slot, at, size, shift, value, total, mixed)
-        total = jnp.sum(total, axis=0, keepdims=True)
+        total, mixed = weighed(shift)
         if has_state:
             keep = jnp.exp2(before * FACTOR - shift)
             total = total + total_in[row, :] * keep
@@ -250,14 +272,17 @@
 def attend(bias, bias_start, query, blocks, state):
     width, rows = query.shape
     heads = width // HD
-    span = sum(a.shape[0] for block in blocks for a in block) // 2
+    span, placed = 0, []
+    for block in blocks:
+        placed.append((len(block), bias_start + span // L))
+        span += sum(a.shape[0] for a in block) // 2
     outs = [
         jax.ShapeDtypeStruct((heads, rows), jnp.float32),
         jax.ShapeDtypeStruct((heads, rows), jnp.float32),
         jax.ShapeDtypeStruct((width, rows), jnp.float32),
     ]
     return call(
-        functools.partial(attend_kernel, [len(block) for block in blocks], bias_start, state is not None),
+        functools.partial(attend_kernel, placed, state is not None),
         outs,
         [bias, query, *[a for block in blocks for a in block], *(state or [])],
         scratch=[pltpu.VMEM((2, span, rows), jnp.float32)],
@@ -275,33 +300,25 @@
     rows, part = kept_ref.shape
     spot = spot_of(here_ref, inner, rows, mixed_ref.shape[1])
     heads = mixed_ref.shape[0] // HD
+
+    def begin(head):
+        query = query_ref[head * HD : head * HD + HD, spot]
+        return attend_head(head, pairs, query, bias_ref, spot, hold.at[head % 2])
+
+    following = begin(0)
     for head in range(heads):
+        top, weighed = following
+        if head + 1 < heads:
+            following = begin(head + 1)
         column = slice(head * HD, head * HD + HD)
         row = slice(head, head + 1)
-        slot = hold.at[head % 2]
-        query = query_ref[column, spot]
         before = top_ref[row, spot]
-        top, at = None, 0
-        for key_ref, _, bias_start in pairs:
-            size = key_ref.shape[0]
-            for first in range(0, size, 128):
-                top = scores_of(
-                    key_ref, first, first + 128, query, column,
-                    bias_ref, bias_start + first // L, spot, slot, at, top,
-                )
-                at += 128
-        top = jnp.maximum(jnp.max(top, axis=0, keepdims=True), before)
+        top = jnp.maximum(top, before)
         shift = top * FACTOR
         keep = jnp.exp2(before * FACTOR - shift)
-        more = update = None
-        at = 0
-        for key_ref, value_ref, _ in pairs:
-            size = key_ref.shape[0]
-            value = value_ref[value_place(head, size)]
-            more, update = weigh(slot, at, size, shift, value, more, update)
-            at += size
-        total = total_ref[row, spot] * keep + jnp.sum(more, axis=0, keepdims=True)
-        mixed = mixed_ref[column, spot] * keep + update
+        total, mixed = weighed(shift)
+        total = total_ref[row, spot] * keep + total
+        mixed = mixed_ref[column, spot] * keep + mixed
         done[:, column] = (mixed / total).T.astype(done.dtype)
     for step in range(sides):
         step = (step + 1) % sides
@@ -454,8 +471,9 @@
 
     last = [(beyond_shared, 5 * views_here)]
     inner = finish(sides, here, True, rows - edge_rows, state, w_out, bias, query, last)
-    rim = [[after(a, inner[0]) for a in piece] for piece in rim]
-    (rim_block,) = project(here, rim, w_key, w_value)
+    begun = project_first(here, [after(rim[0][0], inner[0])], w_key, w_value)
+    rim[1][0] = after(rim[1][0], begun[0])
+    (rim_block,) = project(here, rim[1:], w_key, w_value, begun=begun)
     last.append((rim_block, 6 * views_here))
     state = [after(state[0], inner[0]), *state[1:]]
     outer = finish(sides, here, False, edge_rows, state, w_out, bias, query, last)

time: 68.3 us -> 66.9 us (0.980)
  Pallas kernels: 31 us -> 27.2 us
  waiting for transfers between devices: 11.6 us -> 13.8 us
    pallas_call x15 -> x16, Pallas kernels: 31 us -> 27.2 us  [call(): pl.pallas_call(kernel, out_shape=outs, in_specs=[HBM if k in whole else S...]
    ppermute x1, waiting for transfers between devices: 4.73 us -> 5.77 us  [shards(): outer = lax.ppermute(outer, 'views', [(0, 3), (3, 0)])]
    ppermute x1, waiting for transfers between devices: 0.76 us -> 1.77 us  [shards(): rim = lax.ppermute(rim, ('views', 'sub'), cross)]
  transfers between devices with their start and end apart: 15 -> 15, of which waited for: 6 -> 5; matrix products, arithmetic and copies ran while one was open for 0% -> 0% of each run, Pallas kernels for 44% -> 39%
where the time goes in v6:
time: 66.9 us; the launch traced here: 66.6 us
  Pallas kernels  27.2 us (41%)
  starting transfers between devices  18 us (27%)
  waiting for transfers between devices  13.8 us (21%)
  local copies, waits for them, and re-layouts  7.08 us (11%)
    pallas_call x16, Pallas kernels, call(): pl.pallas_call(kernel, out_shape=outs, in_specs=[HBM if k in whole else S...  27.2 us
    unnamed x18, local copies, waits for them, and re-layouts  7.08 us
    ppermute x6, waiting for transfers between devices, shift(): lax.ppermute(a, 'heads', [(h, (h + step) % sides) for h in range(sides)])  6.23 us
    ppermute x6, starting transfers between devices, shift(): lax.ppermute(a, 'heads', [(h, (h + step) % sides) for h in range(sides)])  6.12 us
    ppermute x1, waiting for transfers between devices, shards(): outer = lax.ppermute(outer, 'views', [(0, 3), (3, 0)])  5.77 us
    ppermute x1, starting transfers between devices, shards(): outer = lax.ppermute(outer, 'views', [(0, 3), (3, 0)])  4.5 us
    ppermute x1, starting transfers between devices, shards(): near = lax.ppermute(tokens, 'views', pair)  3.02 us
    ppermute x1, starting transfers between devices, shards(): rim = lax.ppermute(rim, ('views', 'sub'), cross)  2.56 us
  transfers between devices with their start and end apart: 15, of which 5 were waited for; matrix products, arithmetic and copies ran while one was open for 0% of the time, Pallas kernels for 39%

profile of v6, /device:TPU:0, one launch (start us, length us, event | category | flops | bytes accessed | tf_op | source)
XLA Modules:
  0.0 66.6 jit_solution(1891980974191596144)
XLA Ops:
  0.0 3.0 %collective-permute-start.1 = (bf16[256,1024]{1,0:T(8,128)(2,1)}, bf16[256,1024]{1,0:T(8,128)(2,1)S(1)}, u32[]{:S(2)}, u32[]{:S(2)}) collective-permute-start(bf16[256,1024]{1,0:T(8,128)(2,1)} %refs_0_.1), channel_id=1, source_target_pairs={{0,4},{4,0},{8,12},{12,8},{1,5},{5,1},{9,13},{13,9},{2,6},{6,2},{1... | collective-permute-start | bytes 1572872 | tf_op jit(solution)/shard_map/ppermute | solution.py:438
  3.0 1.5 %collective-permute-start = (bf16[256,1024]{1,0:T(8,128)(2,1)}, bf16[256,1024]{1,0:T(8,128)(2,1)S(1)}, u32[]{:S(2)}, u32[]{:S(2)}) collective-permute-start(bf16[256,1024]{1,0:T(8,128)(2,1)} %refs_0_.1), channel_id=1, source_target_pairs={{0,2},{2,0},{1,3},{3,1},{4,6},{6,4},{5,7},{7,5},{8,10},{10,8},{9,1... | collective-permute-start | bytes 1572872 | tf_op jit(solution)/shard_map/ppermute | solution.py:426
  4.5 0.7 %collective-permute-start.3 = (bf16[256,1024]{1,0:T(8,128)(2,1)}, bf16[256,1024]{1,0:T(8,128)(2,1)S(1)}, u32[]{:S(2)}, u32[]{:S(2)}) collective-permute-start(bf16[256,1024]{1,0:T(8,128)(2,1)} %refs_0_.1), channel_id=1, source_target_pairs={{4,8},{8,4},{5,9},{9,5},{6,10},{10,6},{7,11},{11,7},{20,24},{24,20... | collective-permute-start | bytes 1572872 | tf_op jit(solution)/shard_map/ppermute | solution.py:441
  5.2 0.1 pad_add_fusion.here_ref.refs_0_
  5.3 2.2 %copy-done = bf16[2048,1024]{1,0:T(8,128)(2,1)S(1)} copy-done((bf16[2048,1024]{1,0:T(8,128)(2,1)S(1)}, bf16[2048,1024]{1,0:T(8,128)(2,1)}, u32[]{:S(2)}) %copy-start) | copy-done | bytes 4194328
  7.5 2.2 %copy-done.2 = bf16[2048,1024]{1,0:T(8,128)(2,1)S(1)} copy-done((bf16[2048,1024]{1,0:T(8,128)(2,1)S(1)}, bf16[2048,1024]{1,0:T(8,128)(2,1)}, u32[]{:S(2)}) %copy-start.2) | copy-done | bytes 4194328
  9.7 2.2 %copy-done.4 = bf16[2048,1024]{1,0:T(8,128)(2,1)S(1)} copy-done((bf16[2048,1024]{1,0:T(8,128)(2,1)S(1)}, bf16[2048,1024]{1,0:T(8,128)(2,1)}, u32[]{:S(2)}) %copy-start.4) | copy-done | bytes 4194328
  11.9 0.5 fetch.1.refs_0_
  12.4 0.5 copy-done.6
  12.9 4.5 %collective-permute-start.4 = (bf16[256,1024]{1,0:T(8,128)(2,1)S(1)}, bf16[256,1024]{1,0:T(8,128)(2,1)S(1)}, u32[]{:S(2)}, u32[]{:S(2)}) collective-permute-start(bf16[256,1024]{1,0:T(8,128)(2,1)S(1)} %copy-done.6), channel_id=1, source_target_pairs={{0,12},{12,0},{1,13},{13,1},{2,14},{14,2},{3,15},{15,3},{16,28},{2... | collective-permute-start | bytes 1572872 | tf_op jit(solution)/shard_map/ppermute | solution.py:443
  17.4 0.0 collective-permute-done.1.refs_0_
  17.4 0.6 collective-permute-start.2
  18.0 0.0 collective-permute-done.refs_1_
  18.0 4.1 %project.4 = (bf16[512,1024]{1,0:T(8,128)(2,1)S(1)}, bf16[1024,256]{1,0:T(8,128)(2,1)S(1)}) custom-call(s32[3]{0:T(128)S(1)} %pad_add_fusion.here_ref.refs_0_, bf16[256,1024]{1,0:T(8,128)(2,1)S(1)} %copy-done.6, bf16[256,1024]{1,0:T(8,128)(2,1)S(1)} %collective-permute-done.refs_1_, bf16[2048,1024]{1,0:T(8,128)(2,1)S(1)} %copy-done, ...), custom_call_target="tpu_custom_call" | custom-call | tf_op jit(solution)/shard_map/project/pallas_call | solution.py:24
  22.1 0.7 %mask.1.bias_ref = f32[26,256]{1,0:T(8,128)S(1)} custom-call(s32[3]{0:T(128)S(1)} %pad_add_fusion.here_ref.refs_0_, s32[4]{0:T(128)S(1)} %copy-done.8, s32[4,20]{1,0:T(4,128)S(1)} %copy-done.7, f32[8,128]{1,0:T(8,128)S(1)} %fetch.1.refs_0_), custom_call_target="tpu_custom_call" | custom-call | tf_op jit(solution)/shard_map/mask/pallas_call | solution.py:24
  22.9 1.3 %attend.3 = (f32[8,256]{1,0:T(8,128)S(1)}, f32[8,256]{1,0:T(8,128)S(1)}, f32[1024,256]{1,0:T(8,128)S(1)}) custom-call(f32[26,256]{1,0:T(8,128)S(1)} %mask.1.bias_ref, bf16[1024,256]{1,0:T(8,128)(2,1)S(1)} %get-tuple-element.43.query_ref, bf16[512,1024]{1,0:T(8,128)(2,1)S(1)} %get-tuple-element.46.refs_0_), custom_call_target="tpu_custom_call" | custom-call | tf_op jit(solution)/shard_map/attend/pallas_call | solution.py:24
  24.2 5.8 %collective-permute-done.4.outer_ref = bf16[256,1024]{1,0:T(8,128)(2,1)S(1)} collective-permute-done((bf16[256,1024]{1,0:T(8,128)(2,1)S(1)}, bf16[256,1024]{1,0:T(8,128)(2,1)S(1)}, u32[]{:S(2)}, u32[]{:S(2)}) %collective-permute-start.4) | collective-permute-done | bytes 524320 | tf_op jit(solution)/shard_map/ppermute | solution.py:443
  29.9 0.8 %pick.1 = (bf16[256,1024]{1,0:T(8,128)(2,1)S(1)}, bf16[128,1024]{1,0:T(8,128)(2,1)S(1)}) custom-call(s32[3]{0:T(128)S(1)} %pad_add_fusion.here_ref.refs_0_, bf16[256,1024]{1,0:T(8,128)(2,1)S(1)} %collective-permute-done.3.inner_ref, bf16[256,1024]{1,0:T(8,128)(2,1)S(1)} %collective-permute-done.4.outer_ref), custom_call_target="tpu_custom_call" | custom-call | tf_op jit(solution)/shard_map/pick/pallas_call | solution.py:24
  30.7 0.6 collective-permute-start.8
  31.3 0.0 collective-permute-start.7
  31.3 2.6 %collective-permute-start.9 = (bf16[128,1024]{1,0:T(8,128)(2,1)S(1)}, bf16[128,1024]{1,0:T(8,128)(2,1)S(1)}, u32[]{:S(2)}, u32[]{:S(2)}) collective-permute-start(bf16[128,1024]{1,0:T(8,128)(2,1)S(1)} %get-tuple-element.59), channel_id=1, source_target_pairs={{0,5},{1,4},{4,1},{5,0},{8,13},{9,12},{12,9},{13,8},{2,7},{3,6},{6... | collective-permute-start | bytes 786440 | tf_op jit(solution)/shard_map/ppermute | solution.py:459
  33.9 3.0 %project.5 = (bf16[256,1024]{1,0:T(8,128)(2,1)S(1)}, bf16[256,1024]{1,0:T(8,128)(2,1)S(1)}) custom-call(s32[3]{0:T(128)S(1)} %pad_add_fusion.here_ref.refs_0_, bf16[256,1024]{1,0:T(8,128)(2,1)S(1)} %collective-permute-done.1.refs_0_, bf16[256,1024]{1,0:T(8,128)(2,1)S(1)} %collective-permute-done.2.refs_1_, bf16[2048,1024]{1,0:T(8,128)(2,1)S(1)} %copy-done.1, ...), custom_call_target="tpu_custom_call" | custom-call | tf_op jit(solution)/shard_map/project/pallas_call | solution.py:24
  36.9 0.1 collective-permute-start.5
  37.0 0.5 collective-permute-start.6
  37.5 1.3 %attend.4 = (f32[8,256]{1,0:T(8,128)S(1)}, f32[8,256]{1,0:T(8,128)S(1)}, f32[1024,256]{1,0:T(8,128)S(1)}) custom-call(f32[26,256]{1,0:T(8,128)S(1)} %mask.1.bias_ref, bf16[1024,256]{1,0:T(8,128)(2,1)S(1)} %get-tuple-element.43.query_ref, bf16[256,1024]{1,0:T(8,128)(2,1)S(1)} %get-tuple-element.52.refs_0_, bf16[256,1024]{1,0:T(8,128)(2,1)S(1)} %get-tuple-element.53.refs_1_, ...), custom_call_target="tpu_custom_call" | custom-call | tf_op jit(solution)/shard_map/attend/pallas_call | solution.py:24
  38.8 1.8 %collective-permute-done.9.refs_0_ = bf16[128,1024]{1,0:T(8,128)(2,1)S(1)} collective-permute-done((bf16[128,1024]{1,0:T(8,128)(2,1)S(1)}, bf16[128,1024]{1,0:T(8,128)(2,1)S(1)}, u32[]{:S(2)}, u32[]{:S(2)}) %collective-permute-start.9) | collective-permute-done | bytes 262176 | tf_op jit(solution)/shard_map/ppermute | solution.py:459
  40.6 1.8 %project_first.2 = (f32[256,1024]{1,0:T(8,128)S(1)}, f32[256,1024]{1,0:T(8,128)S(1)}) custom-call(s32[3]{0:T(128)S(1)} %pad_add_fusion.here_ref.refs_0_, bf16[256,1024]{1,0:T(8,128)(2,1)S(1)} %get-tuple-element.57.refs_0_, bf16[2048,1024]{1,0:T(8,128)(2,1)S(1)} %copy-done.1, bf16[2048,1024]{1,0:T(8,128)(2,1)S(1)} %copy-done.2), custom_call_target="tpu_custom_call" | custom-call | tf_op jit(solution)/shard_map/project_first/pallas_call | solution.py:24
  42.4 0.6 collective-permute-done.8.refs_0_
  42.9 2.0 %project.6 = (bf16[256,1024]{1,0:T(8,128)(2,1)S(1)}, bf16[256,1024]{1,0:T(8,128)(2,1)S(1)}) custom-call(s32[3]{0:T(128)S(1)} %pad_add_fusion.here_ref.refs_0_, bf16[256,1024]{1,0:T(8,128)(2,1)S(1)} %collective-permute-done.8.refs_0_, bf16[2048,1024]{1,0:T(8,128)(2,1)S(1)} %copy-done.1, bf16[2048,1024]{1,0:T(8,128)(2,1)S(1)} %copy-done.2, ...), custom_call_target="tpu_custom_call" | custom-call | tf_op jit(solution)/shard_map/project/pallas_call | solution.py:24
  44.9 0.0 copy-start.5
  44.9 0.1 collective-permute-start.10
  45.0 0.5 collective-permute-start.11
  45.5 0.0 collective-permute-done.5.refs_0_
  45.5 0.9 %collective-permute-start.12 = (bf16[128,1024]{1,0:T(8,128)(2,1)S(1)}, bf16[128,1024]{1,0:T(8,128)(2,1)S(1)}, u32[]{:S(2)}, u32[]{:S(2)}) collective-permute-start(bf16[128,1024]{1,0:T(8,128)(2,1)S(1)} %collective-permute-done.9.refs_0_), channel_id=1, source_target_pairs={{0,2},{2,0},{1,3},{3,1},{4,6},{6,4},{5,7},{7,5},{8,10},{10,8},{9,1... | collective-permute-start | bytes 786440 | tf_op jit(solution)/shard_map/ppermute | solution.py:426
  46.4 0.0 collective-permute-done.6.refs_1_
  46.4 0.0 collective-permute-done.7.refs_2_
  46.4 2.2 %attend.5 = (f32[8,256]{1,0:T(8,128)S(1)}, f32[8,256]{1,0:T(8,128)S(1)}, f32[1024,256]{1,0:T(8,128)S(1)}) custom-call(f32[26,256]{1,0:T(8,128)S(1)} %mask.1.bias_ref, bf16[1024,256]{1,0:T(8,128)(2,1)S(1)} %get-tuple-element.43.query_ref, bf16[256,1024]{1,0:T(8,128)(2,1)S(1)} %collective-permute-done.5.refs_0_, ...), custom_call_target="tpu_custom_call" | custom-call | tf_op jit(solution)/shard_map/attend/pallas_call | solution.py:24
  48.6 0.0 copy-start.3
  48.7 1.9 %finish.2 = (bf16[128,1024]{1,0:T(8,128)(2,1)S(1)}, f32[128,1024]{1,0:T(8,128)S(1)}) custom-call(s32[3]{0:T(128)S(1)} %pad_add_fusion.here_ref.refs_0_, f32[8,256]{1,0:T(8,128)S(1)} %get-tuple-element.71.top_ref, f32[8,256]{1,0:T(8,128)S(1)} %get-tuple-element.68.total_ref, f32[1024,256]{1,0:T(8,128)S(1)} %get-tuple-element.69.mixed_ref, ...), custom_call_target="tpu_custom_call" | custom-call | tf_op jit(solution)/shard_map/finish/pallas_call | solution.py:24
  50.6 1.2 %collective-permute-start.14 = (bf16[128,1024]{1,0:T(8,128)(2,1)S(1)}, bf16[128,1024]{1,0:T(8,128)(2,1)S(1)}, u32[]{:S(2)}, u32[]{:S(2)}) collective-permute-start(bf16[128,1024]{1,0:T(8,128)(2,1)S(1)} %get-tuple-element.70), channel_id=1, source_target_pairs={{0,2},{2,0},{1,3},{3,1},{4,6},{6,4},{5,7},{7,5},{8,10},{10,8},{9,1... | collective-permute-start | bytes 786440 | tf_op jit(solution)/shard_map/ppermute | solution.py:426
  51.7 1.3 %project_first.3 = (f32[128,1024]{1,0:T(8,128)S(1)}, f32[128,1024]{1,0:T(8,128)S(1)}) custom-call(s32[3]{0:T(128)S(1)} %pad_add_fusion.here_ref.refs_0_, bf16[128,1024]{1,0:T(8,128)(2,1)S(1)} %collective-permute-done.9.refs_0_, bf16[2048,1024]{1,0:T(8,128)(2,1)S(1)} %copy-done.1, bf16[2048,1024]{1,0:T(8,128)(2,1)S(1)} %copy-done.3), custom_call_target="tpu_custom_call" | custom-call | tf_op jit(solution)/shard_map/project_first/pallas_call | solution.py:24
  53.0 1.3 %collective-permute-done.12.refs_0_ = bf16[128,1024]{1,0:T(8,128)(2,1)S(1)} collective-permute-done((bf16[128,1024]{1,0:T(8,128)(2,1)S(1)}, bf16[128,1024]{1,0:T(8,128)(2,1)S(1)}, u32[]{:S(2)}, u32[]{:S(2)}) %collective-permute-start.12) | collective-permute-done | bytes 262176 | tf_op jit(solution)/shard_map/ppermute | solution.py:426
  54.3 1.4 %project.7 = (bf16[128,1024]{1,0:T(8,128)(2,1)S(1)}, bf16[128,1024]{1,0:T(8,128)(2,1)S(1)}) custom-call(s32[3]{0:T(128)S(1)} %pad_add_fusion.here_ref.refs_0_, bf16[128,1024]{1,0:T(8,128)(2,1)S(1)} %collective-permute-done.12.refs_0_, bf16[2048,1024]{1,0:T(8,128)(2,1)S(1)} %copy-done.1, bf16[2048,1024]{1,0:T(8,128)(2,1)S(1)} %copy-done.3, ...), custom_call_target="tpu_custom_call" | custom-call | tf_op jit(solution)/shard_map/project/pallas_call | solution.py:24
  55.6 2.4 %finish.3 = (bf16[128,1024]{1,0:T(8,128)(2,1)S(1)}, f32[128,1024]{1,0:T(8,128)S(1)}) custom-call(s32[3]{0:T(128)S(1)} %pad_add_fusion.here_ref.refs_0_, f32[8,256]{1,0:T(8,128)S(1)} %get-tuple-element.71.top_ref, f32[8,256]{1,0:T(8,128)S(1)} %get-tuple-element.68.total_ref, f32[1024,256]{1,0:T(8,128)S(1)} %get-tuple-element.69.mixed_ref, ...), custom_call_target="tpu_custom_call" | custom-call | tf_op jit(solution)/shard_map/finish/pallas_call | solution.py:24
  58.1 1.3 %collective-permute-start.13 = (bf16[128,1024]{1,0:T(8,128)(2,1)S(1)}, bf16[128,1024]{1,0:T(8,128)(2,1)S(1)}, u32[]{:S(2)}, u32[]{:S(2)}) collective-permute-start(bf16[128,1024]{1,0:T(8,128)(2,1)S(1)} %get-tuple-element.79), channel_id=1, source_target_pairs={{0,2},{2,0},{1,3},{3,1},{4,6},{6,4},{5,7},{7,5},{8,10},{10,8},{9,1... | collective-permute-start | bytes 786440 | tf_op jit(solution)/shard_map/ppermute | solution.py:426
  59.4 1.3 %settle.2.refs_2_ = bf16[256,1024]{1,0:T(8,128)(2,1)} custom-call(s32[3]{0:T(128)S(1)} %pad_add_fusion.here_ref.refs_0_, f32[128,1024]{1,0:T(8,128)S(1)} %get-tuple-element.80.refs_0_, bf16[128,1024]{1,0:T(8,128)(2,1)S(1)} %collective-permute-done.14.refs_1_), custom_call_target="tpu_custom_call" | custom-call | tf_op jit(solution)/shard_map/settle/pallas_call | solution.py:24
  60.7 4.4 %collective-permute-done.13.refs_1_ = bf16[128,1024]{1,0:T(8,128)(2,1)S(1)} collective-permute-done((bf16[128,1024]{1,0:T(8,128)(2,1)S(1)}, bf16[128,1024]{1,0:T(8,128)(2,1)S(1)}, u32[]{:S(2)}, u32[]{:S(2)}) %collective-permute-start.13) | collective-permute-done | bytes 262176 | tf_op jit(solution)/shard_map/ppermute | solution.py:426
  65.1 1.3 %settle.3 = bf16[256,1024]{1,0:T(8,128)(2,1)} custom-call(s32[3]{0:T(128)S(1)} %pad_add_fusion.here_ref.refs_0_, f32[128,1024]{1,0:T(8,128)S(1)} %get-tuple-element.78.refs_0_, bf16[128,1024]{1,0:T(8,128)(2,1)S(1)} %collective-permute-done.13.refs_1_, bf16[256,1024]{1,0:T(8,128)(2,1)} %settle.2.refs_2_), custom_call_target="tpu_custom_call", output_to_operand_aliasing={{}: (3, {})} | custom-call | tf_op jit(solution)/shard_map/settle/pallas_call | solution.py:24
  (17 shorter events, 0.0 us)
Async XLA Ops:
  0.0 17.4 %collective-permute-start.1 = (bf16[256,1024]{1,0:T(8,128)(2,1)}, bf16[256,1024]{1,0:T(8,128)(2,1)S(1)}, u32[]{:S(2)}, u32[]{:S(2)}) collective-permute-start(bf16[256,1024]{1,0:T(8,128)(2,1)} %refs_0_.1), channel_id=1, source_target_pairs={{0,4},{4,0},{8,12},{12,8},{1,5},{5,1},{9,13},{13,9},{2,6},{6,2},{1... | collective-permute-start | bytes 1572872 | tf_op jit(solution)/shard_map/ppermute | solution.py:438
  3.0 15.0 %collective-permute-start = (bf16[256,1024]{1,0:T(8,128)(2,1)}, bf16[256,1024]{1,0:T(8,128)(2,1)S(1)}, u32[]{:S(2)}, u32[]{:S(2)}) collective-permute-start(bf16[256,1024]{1,0:T(8,128)(2,1)} %refs_0_.1), channel_id=1, source_target_pairs={{0,2},{2,0},{1,3},{3,1},{4,6},{6,4},{5,7},{7,5},{8,10},{10,8},{9,1... | collective-permute-start | bytes 1572872 | tf_op jit(solution)/shard_map/ppermute | solution.py:426
  4.5 19.6 %collective-permute-start.3 = (bf16[256,1024]{1,0:T(8,128)(2,1)}, bf16[256,1024]{1,0:T(8,128)(2,1)S(1)}, u32[]{:S(2)}, u32[]{:S(2)}) collective-permute-start(bf16[256,1024]{1,0:T(8,128)(2,1)} %refs_0_.1), channel_id=1, source_target_pairs={{4,8},{8,4},{5,9},{9,5},{6,10},{10,6},{7,11},{11,7},{20,24},{24,20... | collective-permute-start | bytes 1572872 | tf_op jit(solution)/shard_map/ppermute | solution.py:441
  5.3 2.2 %copy-start = (bf16[2048,1024]{1,0:T(8,128)(2,1)S(1)}, bf16[2048,1024]{1,0:T(8,128)(2,1)}, u32[]{:S(2)}) copy-start(bf16[2048,1024]{1,0:T(8,128)(2,1)} %refs_1_.9) | copy-start | bytes 12582916
  7.5 2.2 %copy-start.2 = (bf16[2048,1024]{1,0:T(8,128)(2,1)S(1)}, bf16[2048,1024]{1,0:T(8,128)(2,1)}, u32[]{:S(2)}) copy-start(bf16[2048,1024]{1,0:T(8,128)(2,1)} %refs_2_.15) | copy-start | bytes 12582916
  9.7 2.2 %copy-start.4 = (bf16[2048,1024]{1,0:T(8,128)(2,1)S(1)}, bf16[2048,1024]{1,0:T(8,128)(2,1)}, u32[]{:S(2)}) copy-start(bf16[2048,1024]{1,0:T(8,128)(2,1)} %refs_3_.4) | copy-start | bytes 12582916
  11.9 1.0 %copy-start.6 = (bf16[256,1024]{1,0:T(8,128)(2,1)S(1)}, bf16[256,1024]{1,0:T(8,128)(2,1)}, u32[]{:S(2)}) copy-start(bf16[256,1024]{1,0:T(8,128)(2,1)} %refs_0_.1) | copy-start | bytes 1572868
  12.9 9.2 %copy-start.7 = (s32[4,20]{1,0:T(4,128)S(1)}, s32[4,20]{1,0:T(4,128)}, u32[]{:S(2)}) copy-start(s32[4,20]{1,0:T(4,128)} %partners_ref.1) | copy-start | bytes 964
  12.9 9.2 %copy-start.8 = (s32[4]{0:T(128)S(1)}, s32[4]{0:T(128)}, u32[]{:S(2)}) copy-start(s32[4]{0:T(128)} %counts_ref.1) | copy-start | bytes 52
  12.9 17.0 %collective-permute-start.4 = (bf16[256,1024]{1,0:T(8,128)(2,1)S(1)}, bf16[256,1024]{1,0:T(8,128)(2,1)S(1)}, u32[]{:S(2)}, u32[]{:S(2)}) collective-permute-start(bf16[256,1024]{1,0:T(8,128)(2,1)S(1)} %copy-done.6), channel_id=1, source_target_pairs={{0,12},{12,0},{1,13},{13,1},{2,14},{14,2},{3,15},{15,3},{16,28},{2... | collective-permute-start | bytes 1572872 | tf_op jit(solution)/shard_map/ppermute | solution.py:443
  17.4 16.5 %collective-permute-start.2 = (bf16[256,1024]{1,0:T(8,128)(2,1)S(1)}, bf16[256,1024]{1,0:T(8,128)(2,1)S(1)}, u32[]{:S(2)}, u32[]{:S(2)}) collective-permute-start(bf16[256,1024]{1,0:T(8,128)(2,1)S(1)} %collective-permute-done.1.refs_0_), channel_id=1, source_target_pairs={{0,2},{2,0},{1,3},{3,1},{4,6},{6,4},{5,7},{7,5},{8,10},{10,8},{9,1... | collective-permute-start | bytes 1572872 | tf_op jit(solution)/shard_map/ppermute | solution.py:426
  18.0 15.9 %copy-start.1 = (bf16[2048,1024]{1,0:T(8,128)(2,1)S(1)}, bf16[2048,1024]{1,0:T(8,128)(2,1)}, u32[]{:S(2)}) copy-start(bf16[2048,1024]{1,0:T(8,128)(2,1)} %refs_1_.9) | copy-start | bytes 12582916
  30.7 12.2 %collective-permute-start.8 = (bf16[256,1024]{1,0:T(8,128)(2,1)S(1)}, bf16[256,1024]{1,0:T(8,128)(2,1)S(1)}, u32[]{:S(2)}, u32[]{:S(2)}) collective-permute-start(bf16[256,1024]{1,0:T(8,128)(2,1)S(1)} %get-tuple-element.57.refs_0_), channel_id=1, source_target_pairs={{0,2},{2,0},{1,3},{3,1},{4,6},{6,4},{5,7},{7,5},{8,10},{10,8},{9,1... | collective-permute-start | bytes 1572872 | tf_op jit(solution)/shard_map/ppermute | solution.py:426
  31.3 15.1 %collective-permute-start.7 = (bf16[512,1024]{1,0:T(8,128)(2,1)S(1)}, bf16[512,1024]{1,0:T(8,128)(2,1)S(1)}, u32[]{:S(2)}, u32[]{:S(2)}) collective-permute-start(bf16[512,1024]{1,0:T(8,128)(2,1)S(1)} %get-tuple-element.46.refs_0_), channel_id=1, source_target_pairs={{0,1},{1,0},{2,3},{3,2},{4,5},{5,4},{6,7},{7,6},{8,9},{9,8},{10,11... | collective-permute-start | bytes 3145736 | tf_op jit(solution)/shard_map/ppermute | solution.py:432
  31.3 9.2 %collective-permute-start.9 = (bf16[128,1024]{1,0:T(8,128)(2,1)S(1)}, bf16[128,1024]{1,0:T(8,128)(2,1)S(1)}, u32[]{:S(2)}, u32[]{:S(2)}) collective-permute-start(bf16[128,1024]{1,0:T(8,128)(2,1)S(1)} %get-tuple-element.59), channel_id=1, source_target_pairs={{0,5},{1,4},{4,1},{5,0},{8,13},{9,12},{12,9},{13,8},{2,7},{3,6},{6... | collective-permute-start | bytes 786440 | tf_op jit(solution)/shard_map/ppermute | solution.py:459
  36.9 8.6 %collective-permute-start.5 = (bf16[256,1024]{1,0:T(8,128)(2,1)S(1)}, bf16[256,1024]{1,0:T(8,128)(2,1)S(1)}, u32[]{:S(2)}, u32[]{:S(2)}) collective-permute-start(bf16[256,1024]{1,0:T(8,128)(2,1)S(1)} %get-tuple-element.52.refs_0_), channel_id=1, source_target_pairs={{0,1},{1,0},{2,3},{3,2},{4,5},{5,4},{6,7},{7,6},{8,9},{9,8},{10,11... | collective-permute-start | bytes 1572872 | tf_op jit(solution)/shard_map/ppermute | solution.py:432
  37.0 9.4 %collective-permute-start.6 = (bf16[256,1024]{1,0:T(8,128)(2,1)S(1)}, bf16[256,1024]{1,0:T(8,128)(2,1)S(1)}, u32[]{:S(2)}, u32[]{:S(2)}) collective-permute-start(bf16[256,1024]{1,0:T(8,128)(2,1)S(1)} %get-tuple-element.53.refs_1_), channel_id=1, source_target_pairs={{0,1},{1,0},{2,3},{3,2},{4,5},{5,4},{6,7},{7,6},{8,9},{9,8},{10,11... | collective-permute-start | bytes 1572872 | tf_op jit(solution)/shard_map/ppermute | solution.py:432
  44.9 3.8 %copy-start.5 = (bf16[1024,2048]{1,0:T(8,128)(2,1)S(1)}, bf16[1024,2048]{1,0:T(8,128)(2,1)}, u32[]{:S(2)}) copy-start(bf16[1024,2048]{1,0:T(8,128)(2,1)} %refs_4_.3) | copy-start | bytes 12582916
  44.9 3.7 %collective-permute-start.10 = (bf16[256,1024]{1,0:T(8,128)(2,1)S(1)}, bf16[256,1024]{1,0:T(8,128)(2,1)S(1)}, u32[]{:S(2)}, u32[]{:S(2)}) collective-permute-start(bf16[256,1024]{1,0:T(8,128)(2,1)S(1)} %get-tuple-element.63.refs_3_), channel_id=1, source_target_pairs={{0,1},{1,0},{2,3},{3,2},{4,5},{5,4},{6,7},{7,6},{8,9},{9,8},{10,11... | collective-permute-start | bytes 1572872 | tf_op jit(solution)/shard_map/ppermute | solution.py:432
  45.0 3.7 %collective-permute-start.11 = (bf16[256,1024]{1,0:T(8,128)(2,1)S(1)}, bf16[256,1024]{1,0:T(8,128)(2,1)S(1)}, u32[]{:S(2)}, u32[]{:S(2)}) collective-permute-start(bf16[256,1024]{1,0:T(8,128)(2,1)S(1)} %get-tuple-element.64.refs_4_), channel_id=1, source_target_pairs={{0,1},{1,0},{2,3},{3,2},{4,5},{5,4},{6,7},{7,6},{8,9},{9,8},{10,11... | collective-permute-start | bytes 1572872 | tf_op jit(solution)/shard_map/ppermute | solution.py:432
  45.5 8.8 %collective-permute-start.12 = (bf16[128,1024]{1,0:T(8,128)(2,1)S(1)}, bf16[128,1024]{1,0:T(8,128)(2,1)S(1)}, u32[]{:S(2)}, u32[]{:S(2)}) collective-permute-start(bf16[128,1024]{1,0:T(8,128)(2,1)S(1)} %collective-permute-done.9.refs_0_), channel_id=1, source_target_pairs={{0,2},{2,0},{1,3},{3,1},{4,6},{6,4},{5,7},{7,5},{8,10},{10,8},{9,1... | collective-permute-start | bytes 786440 | tf_op jit(solution)/shard_map/ppermute | solution.py:426
  48.6 3.1 %copy-start.3 = (bf16[2048,1024]{1,0:T(8,128)(2,1)S(1)}, bf16[2048,1024]{1,0:T(8,128)(2,1)}, u32[]{:S(2)}) copy-start(bf16[2048,1024]{1,0:T(8,128)(2,1)} %refs_2_.15) | copy-start | bytes 12582916
  50.6 8.9 %collective-permute-start.14 = (bf16[128,1024]{1,0:T(8,128)(2,1)S(1)}, bf16[128,1024]{1,0:T(8,128)(2,1)S(1)}, u32[]{:S(2)}, u32[]{:S(2)}) collective-permute-start(bf16[128,1024]{1,0:T(8,128)(2,1)S(1)} %get-tuple-element.70), channel_id=1, source_target_pairs={{0,2},{2,0},{1,3},{3,1},{4,6},{6,4},{5,7},{7,5},{8,10},{10,8},{9,1... | collective-permute-start | bytes 786440 | tf_op jit(solution)/shard_map/ppermute | solution.py:426
  58.1 7.0 %collective-permute-start.13 = (bf16[128,1024]{1,0:T(8,128)(2,1)S(1)}, bf16[128,1024]{1,0:T(8,128)(2,1)S(1)}, u32[]{:S(2)}, u32[]{:S(2)}) collective-permute-start(bf16[128,1024]{1,0:T(8,128)(2,1)S(1)} %get-tuple-element.79), channel_id=1, source_target_pairs={{0,2},{2,0},{1,3},{3,1},{4,6},{6,4},{5,7},{7,5},{8,10},{10,8},{9,1... | collective-permute-start | bytes 786440 | tf_op jit(solution)/shard_map/ppermute | solution.py:426

commit v7 on v6

--- a/solution.py
+++ b/solution.py
@@ -11,6 +11,8 @@
 L = 64
 EDGE = 2
 MB = 1 << 20
+FAKE = 10_000_000_000
+FAKE2 = 3_000_000_000
 FACTOR = HD ** (-0.5) * 1.4426950408889634
 ROWS_BY_ROWS = (((1,), (1,)), ((), ()))
 
@@ -20,7 +22,7 @@
 PLACE, CORE, SIDE = range(3)
 
 
-def call(kernel, outs, ins, scratch=(), name=None, out_specs=None, aliases=None, whole=()):
+def call(kernel, outs, ins, scratch=(), name=None, out_specs=None, aliases=None, whole=(), flops=0):
     return pl.pallas_call(
         kernel,
         out_shape=outs,
@@ -32,7 +34,7 @@
         scratch_shapes=list(scratch),
         input_output_aliases=aliases or {},
         compiler_params=pltpu.CompilerParams(vmem_limit_bytes=16 * MB),
-        cost_estimate=pl.CostEstimate(flops=0, bytes_accessed=0, transcendentals=0),
+        cost_estimate=pl.CostEstimate(flops=flops, bytes_accessed=0, transcendentals=0),
         name=name,
     )(*ins)
 
@@ -73,16 +75,18 @@
     refs[-1][...] = jnp.zeros_like(refs[-1])
 
 
-def fetch(*arrays):
-    return call(fetch_kernel, jax.ShapeDtypeStruct((8, 128), jnp.float32), arrays, name="fetch")
-
-
-def make_mask(chips, cores, here, counts, partners, fetched):
+def fetch(*arrays, flops=0):
+    return call(
+        fetch_kernel, jax.ShapeDtypeStruct((8, 128), jnp.float32), arrays, name="fetch", flops=flops
+    )
+
+
+def make_mask(chips, cores, here, counts, partners, *fetched):
     views = partners.shape[0]
     return call(
         functools.partial(mask_kernel, chips, cores),
         jax.ShapeDtypeStruct((6 * views + EDGE, views * L), jnp.float32),
-        [here, counts, partners, fetched],
+        [here, counts, partners, *fetched],
         name="mask",
     )
 
@@ -269,7 +273,7 @@
         mixed_out[column, :] = mixed
 
 
-def attend(bias, bias_start, query, blocks, state):
+def attend(bias, bias_start, query, blocks, state, flops=0):
     width, rows = query.shape
     heads = width // HD
     span, placed = 0, []
@@ -287,6 +291,7 @@
         [bias, query, *[a for block in blocks for a in block], *(state or [])],
         scratch=[pltpu.VMEM((2, span, rows), jnp.float32)],
         name="attend",
+        flops=flops,
     )
 
 
@@ -296,8 +301,8 @@
         pairs.append((*halves_of(refs[:parts]), bias_start))
         refs = refs[parts:]
     weight_ref, refs = refs[0], refs[1:]
-    sent_refs, kept_ref, done, hold = refs[: sides - 1], *refs[sides - 1 :]
-    rows, part = kept_ref.shape
+    sent_refs, done, hold = refs[: sides - 1], *refs[sides - 1 :]
+    rows, part = sent_refs[0].shape
     spot = spot_of(here_ref, inner, rows, mixed_ref.shape[1])
     heads = mixed_ref.shape[0] // HD
 
@@ -319,16 +324,29 @@
         total, mixed = weighed(shift)
         total = total_ref[row, spot] * keep + total
         mixed = mixed_ref[column, spot] * keep + mixed
-        done[:, column] = (mixed / total).T.astype(done.dtype)
-    for step in range(sides):
-        step = (step + 1) % sides
-        place = lax.rem(here_ref[SIDE] + step, sides)
-        columns = pl.ds(pl.multiple_of(place * part, part), part)
-        result = jnp.dot(done[...], weight_ref[:, columns], preferred_element_type=jnp.float32)
-        if step == 0:
-            kept_ref[...] = result
-        else:
-            sent_refs[step - 1][...] = result.astype(jnp.bfloat16)
+        done[:, column] = (mixed * (1.0 / total)).astype(done.dtype).T
+    for step, sent_ref in enumerate(sent_refs):
+        sent_ref[...] = output_part(here_ref, step + 1, sides, done, weight_ref).astype(jnp.bfloat16)
+
+
+def output_part(here_ref, step, sides, done_ref, weight_ref):
+    part = weight_ref.shape[1] // sides
+    place = lax.rem(here_ref[SIDE] + step, sides)
+    columns = pl.ds(pl.multiple_of(place * part, part), part)
+    return jnp.dot(done_ref[...], weight_ref[:, columns], preferred_element_type=jnp.float32)
+
+
+def keep_kernel(sides, here_ref, done_ref, weight_ref, kept_ref):
+    kept_ref[...] = output_part(here_ref, 0, sides, done_ref, weight_ref)
+
+
+def keep(sides, here, done, weight):
+    return call(
+        functools.partial(keep_kernel, sides),
+        jax.ShapeDtypeStruct((done.shape[0], weight.shape[1] // sides), jnp.float32),
+        [here, done, weight],
+        name="keep",
+    )
 
 
 def pick_kernel(here_ref, inner_ref, outer_ref, block_ref, edge_ref):
@@ -368,7 +386,7 @@
     width = query.shape[0]
     part = weight.shape[1] // sides
     outs = [jax.ShapeDtypeStruct((rows, part), jnp.bfloat16)] * (sides - 1)
-    outs += [jax.ShapeDtypeStruct((rows, part), jnp.float32)]
+    outs += [jax.ShapeDtypeStruct((rows, width), jnp.bfloat16)]
     span = sum(a.shape[0] for block, _ in blocks for a in block) // 2
     return call(
         functools.partial(
@@ -376,10 +394,7 @@
         ),
         outs,
         [here, *state, bias, query, *[a for block, _ in blocks for a in block], weight],
-        scratch=[
-            pltpu.VMEM((rows, width), jnp.bfloat16),
-            pltpu.VMEM((2, span, rows), jnp.float32),
-        ],
+        scratch=[pltpu.VMEM((2, span, rows), jnp.float32)],
         name="finish",
     )
 
@@ -448,10 +463,11 @@
         edge += [(2 * z, 2 * ((z - 2) % chips) + 1) for z in range(chips)]
         here = after(here, rim)
         rim = lax.ppermute(rim, ("views", "sub"), edge)
-    near = gather([after(near, fetched)])
-    block, query = project(here, own, w_key, w_value, w_query, parts=1)
+    landed = fetch(near, flops=FAKE2)
+    near = gather([after(near, fetched, landed)])
+    block, query = project(here, own, w_key, w_value, w_query)
     own_shared = share(block)
-    bias = make_mask(chips, cores, after(here, query), counts, partners, fetched)
+    bias = make_mask(chips, cores, after(here, query), counts, partners, fetched, landed)
     state = attend(bias, 0, query, [block], None)
     if chips == 4:
         beyond, rim = pick(here, after(inner, state[0]), outer)
@@ -467,9 +483,9 @@
     beyond[1][0] = after(beyond[1][0], begun[0], rim[0][0])
     (block,) = project(here, beyond[1:], w_key, w_value, begun=begun)
     beyond_shared = share(block)
-    state = attend(bias, 2 * views_here, query, [near_shared, own_shared, block], state)
-
-    last = [(beyond_shared, 5 * views_here)]
+    state = attend(bias, 3 * views_here, query, [own_shared, block], state, flops=FAKE)
+
+    last = [(near_shared, 2 * views_here), (beyond_shared, 5 * views_here)]
     inner = finish(sides, here, True, rows - edge_rows, state, w_out, bias, query, last)
     begun = project_first(here, [after(rim[0][0], inner[0])], w_key, w_value)
     rim[1][0] = after(rim[1][0], begun[0])
@@ -479,7 +495,8 @@
     outer = finish(sides, here, False, edge_rows, state, w_out, bias, query, last)
 
     def exchange(parts):
-        return [parts[-1]] + [shift(part, step + 1) for step, part in enumerate(parts[:-1])]
+        kept = keep(sides, here, parts[-1], w_out)
+        return [kept] + [shift(part, step + 1) for step, part in enumerate(parts[:-1])]
 
     inner, outer = exchange(inner), exchange(outer)
     attended = settle(here, True, inner, rows)

time: 66.9 us -> 67.2 us (level)
  waiting for transfers between devices: 13.8 us -> 11.8 us
  Pallas kernels: 27.2 us -> 29.1 us
    ppermute x6, waiting for transfers between devices: 6.23 us -> 3.99 us  [shift(): lax.ppermute(a, 'heads', [(h, (h + step) % sides) for h in range(sides)])]
    pallas_call x16 -> x19, Pallas kernels: 27.2 us -> 29.1 us  [call(): pl.pallas_call(kernel, out_shape=outs, in_specs=[HBM if k in whole else S...]
    ppermute x5 -> x6, starting transfers between devices: 1.14 us -> 2.1 us  [share(): return tuple((lax.ppermute(a, 'sub', [(0, 1), (1, 0)]) for a in block))]
  transfers between devices with their start and end apart: 15 -> 16, of which waited for: 5 -> 5; matrix products, arithmetic and copies ran while one was open for 0% -> 0% of each run, Pallas kernels for 39% -> 42%
where the time goes in v7:
time: 67.2 us; the launch traced here: 66.9 us
  Pallas kernels  29.1 us (43%)
  starting transfers between devices  18.4 us (27%)
  waiting for transfers between devices  11.8 us (18%)
  local copies, waits for them, and re-layouts  7.12 us (11%)
    pallas_call x19, Pallas kernels, call(): pl.pallas_call(kernel, out_shape=outs, in_specs=[HBM if k in whole else S...  29.1 us
    unnamed x18, local copies, waits for them, and re-layouts  7.12 us
    ppermute x6, starting transfers between devices, shift(): lax.ppermute(a, 'heads', [(h, (h + step) % sides) for h in range(sides)])  6.01 us
    ppermute x1, waiting for transfers between devices, shards(): outer = lax.ppermute(outer, 'views', [(0, 3), (3, 0)])  5.73 us
    ppermute x1, starting transfers between devices, shards(): outer = lax.ppermute(outer, 'views', [(0, 3), (3, 0)])  4.63 us
    ppermute x6, waiting for transfers between devices, shift(): lax.ppermute(a, 'heads', [(h, (h + step) % sides) for h in range(sides)])  3.99 us
    ppermute x1, starting transfers between devices, shards(): near = lax.ppermute(tokens, 'views', pair)  3.02 us
    ppermute x6, starting transfers between devices, share(): return tuple((lax.ppermute(a, 'sub', [(0, 1), (1, 0)]) for a in block))  2.1 us
  transfers between devices with their start and end apart: 16, of which 5 were waited for; matrix products, arithmetic and copies ran while one was open for 0% of the time, Pallas kernels for 42%

profile of v7, /device:TPU:0, one launch (start us, length us, event | category | flops | bytes accessed | tf_op | source)
XLA Modules:
  0.0 66.9 jit_solution(1082601231003932802)
XLA Ops:
  0.0 3.0 %collective-permute-start.1 = (bf16[256,1024]{1,0:T(8,128)(2,1)}, bf16[256,1024]{1,0:T(8,128)(2,1)S(1)}, u32[]{:S(2)}, u32[]{:S(2)}) collective-permute-start(bf16[256,1024]{1,0:T(8,128)(2,1)} %refs_0_.1), channel_id=1, source_target_pairs={{0,4},{4,0},{8,12},{12,8},{1,5},{5,1},{9,13},{13,9},{2,6},{6,2},{1... | collective-permute-start | bytes 1572872 | tf_op jit(solution)/shard_map/ppermute | solution.py:453
  3.0 1.5 %collective-permute-start = (bf16[256,1024]{1,0:T(8,128)(2,1)}, bf16[256,1024]{1,0:T(8,128)(2,1)S(1)}, u32[]{:S(2)}, u32[]{:S(2)}) collective-permute-start(bf16[256,1024]{1,0:T(8,128)(2,1)} %refs_0_.1), channel_id=1, source_target_pairs={{0,2},{2,0},{1,3},{3,1},{4,6},{6,4},{5,7},{7,5},{8,10},{10,8},{9,1... | collective-permute-start | bytes 1572872 | tf_op jit(solution)/shard_map/ppermute | solution.py:441
  4.5 0.7 %collective-permute-start.4 = (bf16[256,1024]{1,0:T(8,128)(2,1)}, bf16[256,1024]{1,0:T(8,128)(2,1)S(1)}, u32[]{:S(2)}, u32[]{:S(2)}) collective-permute-start(bf16[256,1024]{1,0:T(8,128)(2,1)} %refs_0_.1), channel_id=1, source_target_pairs={{4,8},{8,4},{5,9},{9,5},{6,10},{10,6},{7,11},{11,7},{20,24},{24,20... | collective-permute-start | bytes 1572872 | tf_op jit(solution)/shard_map/ppermute | solution.py:456
  5.2 0.1 pad_add_fusion.here_ref.refs_0_
  5.3 2.2 %copy-done = bf16[2048,1024]{1,0:T(8,128)(2,1)S(1)} copy-done((bf16[2048,1024]{1,0:T(8,128)(2,1)S(1)}, bf16[2048,1024]{1,0:T(8,128)(2,1)}, u32[]{:S(2)}) %copy-start) | copy-done | bytes 4194328
  7.5 2.2 %copy-done.2 = bf16[2048,1024]{1,0:T(8,128)(2,1)S(1)} copy-done((bf16[2048,1024]{1,0:T(8,128)(2,1)S(1)}, bf16[2048,1024]{1,0:T(8,128)(2,1)}, u32[]{:S(2)}) %copy-start.2) | copy-done | bytes 4194328
  9.7 2.2 %copy-done.5 = bf16[2048,1024]{1,0:T(8,128)(2,1)S(1)} copy-done((bf16[2048,1024]{1,0:T(8,128)(2,1)S(1)}, bf16[2048,1024]{1,0:T(8,128)(2,1)}, u32[]{:S(2)}) %copy-start.5) | copy-done | bytes 4194328
  11.9 0.5 fetch.2.refs_0_
  12.4 0.5 copy-done.6
  12.9 4.6 %collective-permute-start.5 = (bf16[256,1024]{1,0:T(8,128)(2,1)S(1)}, bf16[256,1024]{1,0:T(8,128)(2,1)S(1)}, u32[]{:S(2)}, u32[]{:S(2)}) collective-permute-start(bf16[256,1024]{1,0:T(8,128)(2,1)S(1)} %copy-done.6), channel_id=1, source_target_pairs={{0,12},{12,0},{1,13},{13,1},{2,14},{14,2},{3,15},{15,3},{16,28},{2... | collective-permute-start | bytes 1572872 | tf_op jit(solution)/shard_map/ppermute | solution.py:458
  17.5 0.0 collective-permute-done.1.refs_0_
  17.6 0.0 copy-start.7
  17.6 0.0 copy-start.8
  17.6 0.6 collective-permute-start.7
  18.2 4.1 %project.4 = (bf16[256,1024]{1,0:T(8,128)(2,1)S(1)}, bf16[256,1024]{1,0:T(8,128)(2,1)S(1)}, bf16[1024,256]{1,0:T(8,128)(2,1)S(1)}) custom-call(s32[3]{0:T(128)S(1)} %pad_add_fusion.here_ref.refs_0_, bf16[256,1024]{1,0:T(8,128)(2,1)S(1)} %copy-done.6, bf16[256,1024]{1,0:T(8,128)(2,1)S(1)} %collective-permute-done.refs_1_, bf16[2048,1024]{1,0:T(8,128)(2,1)S(1)} %copy-done.1, ...), custom_call_target="tpu_custom_call" | custom-call | tf_op jit(solution)/shard_map/project/pallas_call | solution.py:26
  22.3 0.7 %mask.1.bias_ref = f32[26,256]{1,0:T(8,128)S(1)} custom-call(s32[3]{0:T(128)S(1)} %pad_add_fusion.here_ref.refs_0_, s32[4]{0:T(128)S(1)} %copy-done.8, s32[4,20]{1,0:T(4,128)S(1)} %copy-done.7, f32[8,128]{1,0:T(8,128)S(1)} %fetch.2.refs_0_, f32[8,128]{1,0:T(8,128)S(1)} %fetch.3.refs_1_), custom_call_target="tpu_custom_call" | custom-call | tf_op jit(solution)/shard_map/mask/pallas_call | solution.py:26
  23.0 1.3 %attend.3 = (f32[8,256]{1,0:T(8,128)S(1)}, f32[8,256]{1,0:T(8,128)S(1)}, f32[1024,256]{1,0:T(8,128)S(1)}) custom-call(f32[26,256]{1,0:T(8,128)S(1)} %mask.1.bias_ref, bf16[1024,256]{1,0:T(8,128)(2,1)S(1)} %get-tuple-element.44.query_ref, bf16[256,1024]{1,0:T(8,128)(2,1)S(1)} %get-tuple-element.46.refs_0_, bf16[256,1024]{1,0:T(8,128)(2,1)S(1)} %get-tuple-element.47.refs_1_), custom_call_target="tpu_custom_call" | custom-call | tf_op jit(solution)/shard_map/attend/pallas_call | solution.py:26
  24.3 5.7 %collective-permute-done.5.outer_ref = bf16[256,1024]{1,0:T(8,128)(2,1)S(1)} collective-permute-done((bf16[256,1024]{1,0:T(8,128)(2,1)S(1)}, bf16[256,1024]{1,0:T(8,128)(2,1)S(1)}, u32[]{:S(2)}, u32[]{:S(2)}) %collective-permute-start.5) | collective-permute-done | bytes 524320 | tf_op jit(solution)/shard_map/ppermute | solution.py:458
  30.1 0.8 %pick.1 = (bf16[256,1024]{1,0:T(8,128)(2,1)S(1)}, bf16[128,1024]{1,0:T(8,128)(2,1)S(1)}) custom-call(s32[3]{0:T(128)S(1)} %pad_add_fusion.here_ref.refs_0_, bf16[256,1024]{1,0:T(8,128)(2,1)S(1)} %collective-permute-done.4.inner_ref, bf16[256,1024]{1,0:T(8,128)(2,1)S(1)} %collective-permute-done.5.outer_ref), custom_call_target="tpu_custom_call" | custom-call | tf_op jit(solution)/shard_map/pick/pallas_call | solution.py:26
  30.8 0.6 collective-permute-start.6
  31.4 0.5 collective-permute-start.3
  32.0 1.9 %collective-permute-start.8 = (bf16[128,1024]{1,0:T(8,128)(2,1)S(1)}, bf16[128,1024]{1,0:T(8,128)(2,1)S(1)}, u32[]{:S(2)}, u32[]{:S(2)}) collective-permute-start(bf16[128,1024]{1,0:T(8,128)(2,1)S(1)} %get-tuple-element.61), channel_id=1, source_target_pairs={{0,5},{1,4},{4,1},{5,0},{8,13},{9,12},{12,9},{13,8},{2,7},{3,6},{6... | collective-permute-start | bytes 786440 | tf_op jit(solution)/shard_map/ppermute | solution.py:475
  33.9 3.0 %project.5 = (bf16[256,1024]{1,0:T(8,128)(2,1)S(1)}, bf16[256,1024]{1,0:T(8,128)(2,1)S(1)}) custom-call(s32[3]{0:T(128)S(1)} %pad_add_fusion.here_ref.refs_0_, bf16[256,1024]{1,0:T(8,128)(2,1)S(1)} %collective-permute-done.1.refs_0_, bf16[256,1024]{1,0:T(8,128)(2,1)S(1)} %collective-permute-done.7.refs_1_, bf16[2048,1024]{1,0:T(8,128)(2,1)S(1)} %copy-done.1, ...), custom_call_target="tpu_custom_call" | custom-call | tf_op jit(solution)/shard_map/project/pallas_call | solution.py:26
  36.9 0.6 collective-permute-start.10
  37.5 1.3 %attend.4 = (f32[8,256]{1,0:T(8,128)S(1)}, f32[8,256]{1,0:T(8,128)S(1)}, f32[1024,256]{1,0:T(8,128)S(1)}) custom-call(f32[26,256]{1,0:T(8,128)S(1)} %mask.1.bias_ref, bf16[1024,256]{1,0:T(8,128)(2,1)S(1)} %get-tuple-element.44.query_ref, bf16[256,1024]{1,0:T(8,128)(2,1)S(1)} %get-tuple-element.54.refs_0_, bf16[256,1024]{1,0:T(8,128)(2,1)S(1)} %get-tuple-element.55.refs_1_, ...), custom_call_target="tpu_custom_call" | custom-call | tf_op jit(solution)/shard_map/attend/pallas_call | solution.py:26
  38.8 1.6 %collective-permute-done.8.refs_0_ = bf16[128,1024]{1,0:T(8,128)(2,1)S(1)} collective-permute-done((bf16[128,1024]{1,0:T(8,128)(2,1)S(1)}, bf16[128,1024]{1,0:T(8,128)(2,1)S(1)}, u32[]{:S(2)}, u32[]{:S(2)}) %collective-permute-start.8) | collective-permute-done | bytes 262176 | tf_op jit(solution)/shard_map/ppermute | solution.py:475
  40.4 0.5 collective-permute-start.9
  40.9 1.8 %project_first.2 = (f32[256,1024]{1,0:T(8,128)S(1)}, f32[256,1024]{1,0:T(8,128)S(1)}) custom-call(s32[3]{0:T(128)S(1)} %pad_add_fusion.here_ref.refs_0_, bf16[256,1024]{1,0:T(8,128)(2,1)S(1)} %get-tuple-element.59.refs_0_, bf16[2048,1024]{1,0:T(8,128)(2,1)S(1)} %copy-done.1, bf16[2048,1024]{1,0:T(8,128)(2,1)S(1)} %copy-done.2), custom_call_target="tpu_custom_call" | custom-call | tf_op jit(solution)/shard_map/project_first/pallas_call | solution.py:26
  42.7 0.4 collective-permute-done.6.refs_0_
  43.1 1.2 %collective-permute-start.13 = (bf16[128,1024]{1,0:T(8,128)(2,1)S(1)}, bf16[128,1024]{1,0:T(8,128)(2,1)S(1)}, u32[]{:S(2)}, u32[]{:S(2)}) collective-permute-start(bf16[128,1024]{1,0:T(8,128)(2,1)S(1)} %collective-permute-done.8.refs_0_), channel_id=1, source_target_pairs={{0,2},{2,0},{1,3},{3,1},{4,6},{6,4},{5,7},{7,5},{8,10},{10,8},{9,1... | collective-permute-start | bytes 786440 | tf_op jit(solution)/shard_map/ppermute | solution.py:441
  44.2 1.9 %project.6 = (bf16[256,1024]{1,0:T(8,128)(2,1)S(1)}, bf16[256,1024]{1,0:T(8,128)(2,1)S(1)}) custom-call(s32[3]{0:T(128)S(1)} %pad_add_fusion.here_ref.refs_0_, bf16[256,1024]{1,0:T(8,128)(2,1)S(1)} %collective-permute-done.6.refs_0_, bf16[2048,1024]{1,0:T(8,128)(2,1)S(1)} %copy-done.1, bf16[2048,1024]{1,0:T(8,128)(2,1)S(1)} %copy-done.2, ...), custom_call_target="tpu_custom_call" | custom-call | tf_op jit(solution)/shard_map/project/pallas_call | solution.py:26
  46.2 0.1 collective-permute-start.11
  46.2 0.5 collective-permute-start.12
  46.7 1.7 %attend.5 = (f32[8,256]{1,0:T(8,128)S(1)}, f32[8,256]{1,0:T(8,128)S(1)}, f32[1024,256]{1,0:T(8,128)S(1)}) custom-call(f32[26,256]{1,0:T(8,128)S(1)} %mask.1.bias_ref, bf16[1024,256]{1,0:T(8,128)(2,1)S(1)} %get-tuple-element.44.query_ref, bf16[256,1024]{1,0:T(8,128)(2,1)S(1)} %collective-permute-done.2.refs_0_, ...), custom_call_target="tpu_custom_call" | custom-call | flops 10000000000 | tf_op jit(solution)/shard_map/attend/pallas_call | solution.py:26
  48.4 0.0 copy-start.3
  48.4 0.4 collective-permute-done.12.refs_3_
  48.9 0.0 copy-done.4
  48.9 2.3 %finish.2 = (bf16[128,1024]{1,0:T(8,128)(2,1)S(1)}, bf16[128,1024]{1,0:T(8,128)(2,1)S(1)}) custom-call(s32[3]{0:T(128)S(1)} %pad_add_fusion.here_ref.refs_0_, f32[8,256]{1,0:T(8,128)S(1)} %get-tuple-element.73.top_ref, f32[8,256]{1,0:T(8,128)S(1)} %get-tuple-element.70.total_ref, f32[1024,256]{1,0:T(8,128)S(1)} %get-tuple-element.71.mixed_ref, ...), custom_call_target="tpu_custom_call" | custom-call | tf_op jit(solution)/shard_map/finish/pallas_call | solution.py:26
  51.3 0.9 %collective-permute-start.15 = (bf16[128,1024]{1,0:T(8,128)(2,1)S(1)}, bf16[128,1024]{1,0:T(8,128)(2,1)S(1)}, u32[]{:S(2)}, u32[]{:S(2)}) collective-permute-start(bf16[128,1024]{1,0:T(8,128)(2,1)S(1)} %get-tuple-element.72), channel_id=1, source_target_pairs={{0,2},{2,0},{1,3},{3,1},{4,6},{6,4},{5,7},{7,5},{8,10},{10,8},{9,1... | collective-permute-start | bytes 786440 | tf_op jit(solution)/shard_map/ppermute | solution.py:441
  52.2 1.3 %project_first.3 = (f32[128,1024]{1,0:T(8,128)S(1)}, f32[128,1024]{1,0:T(8,128)S(1)}) custom-call(s32[3]{0:T(128)S(1)} %pad_add_fusion.here_ref.refs_0_, bf16[128,1024]{1,0:T(8,128)(2,1)S(1)} %collective-permute-done.8.refs_0_, bf16[2048,1024]{1,0:T(8,128)(2,1)S(1)} %copy-done.1, bf16[2048,1024]{1,0:T(8,128)(2,1)S(1)} %copy-done.3), custom_call_target="tpu_custom_call" | custom-call | tf_op jit(solution)/shard_map/project_first/pallas_call | solution.py:26
  53.5 1.4 %project.7 = (bf16[128,1024]{1,0:T(8,128)(2,1)S(1)}, bf16[128,1024]{1,0:T(8,128)(2,1)S(1)}) custom-call(s32[3]{0:T(128)S(1)} %pad_add_fusion.here_ref.refs_0_, bf16[128,1024]{1,0:T(8,128)(2,1)S(1)} %collective-permute-done.13.refs_0_, bf16[2048,1024]{1,0:T(8,128)(2,1)S(1)} %copy-done.1, bf16[2048,1024]{1,0:T(8,128)(2,1)S(1)} %copy-done.3, ...), custom_call_target="tpu_custom_call" | custom-call | tf_op jit(solution)/shard_map/project/pallas_call | solution.py:26
  54.9 2.5 %finish.3 = (bf16[128,1024]{1,0:T(8,128)(2,1)S(1)}, bf16[128,1024]{1,0:T(8,128)(2,1)S(1)}) custom-call(s32[3]{0:T(128)S(1)} %pad_add_fusion.here_ref.refs_0_, f32[8,256]{1,0:T(8,128)S(1)} %get-tuple-element.73.top_ref, f32[8,256]{1,0:T(8,128)S(1)} %get-tuple-element.70.total_ref, f32[1024,256]{1,0:T(8,128)S(1)} %get-tuple-element.71.mixed_ref, ...), custom_call_target="tpu_custom_call" | custom-call | tf_op jit(solution)/shard_map/finish/pallas_call | solution.py:26
  57.3 1.2 %collective-permute-start.14 = (bf16[128,1024]{1,0:T(8,128)(2,1)S(1)}, bf16[128,1024]{1,0:T(8,128)(2,1)S(1)}, u32[]{:S(2)}, u32[]{:S(2)}) collective-permute-start(bf16[128,1024]{1,0:T(8,128)(2,1)S(1)} %get-tuple-element.81), channel_id=1, source_target_pairs={{0,2},{2,0},{1,3},{3,1},{4,6},{6,4},{5,7},{7,5},{8,10},{10,8},{9,1... | collective-permute-start | bytes 786440 | tf_op jit(solution)/shard_map/ppermute | solution.py:441
  58.6 1.0 %keep.3.refs_0_ = f32[128,1024]{1,0:T(8,128)S(1)} custom-call(s32[3]{0:T(128)S(1)} %pad_add_fusion.here_ref.refs_0_, bf16[128,1024]{1,0:T(8,128)(2,1)S(1)} %get-tuple-element.82.done_ref, bf16[1024,2048]{1,0:T(8,128)(2,1)S(1)} %copy-done.4), custom_call_target="tpu_custom_call" | custom-call | tf_op jit(solution)/shard_map/keep/pallas_call | solution.py:26
  59.6 1.0 %keep.2.refs_0_ = f32[128,1024]{1,0:T(8,128)S(1)} custom-call(s32[3]{0:T(128)S(1)} %pad_add_fusion.here_ref.refs_0_, bf16[128,1024]{1,0:T(8,128)(2,1)S(1)} %get-tuple-element.80.done_ref, bf16[1024,2048]{1,0:T(8,128)(2,1)S(1)} %copy-done.4), custom_call_target="tpu_custom_call" | custom-call | tf_op jit(solution)/shard_map/keep/pallas_call | solution.py:26
  60.6 1.3 %settle.2.refs_2_ = bf16[256,1024]{1,0:T(8,128)(2,1)} custom-call(s32[3]{0:T(128)S(1)} %pad_add_fusion.here_ref.refs_0_, f32[128,1024]{1,0:T(8,128)S(1)} %keep.3.refs_0_, bf16[128,1024]{1,0:T(8,128)(2,1)S(1)} %collective-permute-done.15.refs_1_), custom_call_target="tpu_custom_call" | custom-call | tf_op jit(solution)/shard_map/settle/pallas_call | solution.py:26
  61.9 3.6 %collective-permute-done.14.refs_1_ = bf16[128,1024]{1,0:T(8,128)(2,1)S(1)} collective-permute-done((bf16[128,1024]{1,0:T(8,128)(2,1)S(1)}, bf16[128,1024]{1,0:T(8,128)(2,1)S(1)}, u32[]{:S(2)}, u32[]{:S(2)}) %collective-permute-start.14) | collective-permute-done | bytes 262176 | tf_op jit(solution)/shard_map/ppermute | solution.py:441
  65.5 1.3 %settle.3 = bf16[256,1024]{1,0:T(8,128)(2,1)} custom-call(s32[3]{0:T(128)S(1)} %pad_add_fusion.here_ref.refs_0_, f32[128,1024]{1,0:T(8,128)S(1)} %keep.2.refs_0_, bf16[128,1024]{1,0:T(8,128)(2,1)S(1)} %collective-permute-done.14.refs_1_, bf16[256,1024]{1,0:T(8,128)(2,1)} %settle.2.refs_2_), custom_call_target="tpu_custom_call", output_to_operand_aliasing={{}: (3, {})} | custom-call | tf_op jit(solution)/shard_map/settle/pallas_call | solution.py:26
  (22 shorter events, 0.0 us)
Async XLA Ops:
  0.0 17.5 %collective-permute-start.1 = (bf16[256,1024]{1,0:T(8,128)(2,1)}, bf16[256,1024]{1,0:T(8,128)(2,1)S(1)}, u32[]{:S(2)}, u32[]{:S(2)}) collective-permute-start(bf16[256,1024]{1,0:T(8,128)(2,1)} %refs_0_.1), channel_id=1, source_target_pairs={{0,4},{4,0},{8,12},{12,8},{1,5},{5,1},{9,13},{13,9},{2,6},{6,2},{1... | collective-permute-start | bytes 1572872 | tf_op jit(solution)/shard_map/ppermute | solution.py:453
  3.0 15.2 %collective-permute-start = (bf16[256,1024]{1,0:T(8,128)(2,1)}, bf16[256,1024]{1,0:T(8,128)(2,1)S(1)}, u32[]{:S(2)}, u32[]{:S(2)}) collective-permute-start(bf16[256,1024]{1,0:T(8,128)(2,1)} %refs_0_.1), channel_id=1, source_target_pairs={{0,2},{2,0},{1,3},{3,1},{4,6},{6,4},{5,7},{7,5},{8,10},{10,8},{9,1... | collective-permute-start | bytes 1572872 | tf_op jit(solution)/shard_map/ppermute | solution.py:441
  4.5 19.8 %collective-permute-start.4 = (bf16[256,1024]{1,0:T(8,128)(2,1)}, bf16[256,1024]{1,0:T(8,128)(2,1)S(1)}, u32[]{:S(2)}, u32[]{:S(2)}) collective-permute-start(bf16[256,1024]{1,0:T(8,128)(2,1)} %refs_0_.1), channel_id=1, source_target_pairs={{4,8},{8,4},{5,9},{9,5},{6,10},{10,6},{7,11},{11,7},{20,24},{24,20... | collective-permute-start | bytes 1572872 | tf_op jit(solution)/shard_map/ppermute | solution.py:456
  5.3 2.2 %copy-start = (bf16[2048,1024]{1,0:T(8,128)(2,1)S(1)}, bf16[2048,1024]{1,0:T(8,128)(2,1)}, u32[]{:S(2)}) copy-start(bf16[2048,1024]{1,0:T(8,128)(2,1)} %refs_1_.9) | copy-start | bytes 12582916
  7.5 2.2 %copy-start.2 = (bf16[2048,1024]{1,0:T(8,128)(2,1)S(1)}, bf16[2048,1024]{1,0:T(8,128)(2,1)}, u32[]{:S(2)}) copy-start(bf16[2048,1024]{1,0:T(8,128)(2,1)} %refs_2_.13) | copy-start | bytes 12582916
  9.7 2.2 %copy-start.5 = (bf16[2048,1024]{1,0:T(8,128)(2,1)S(1)}, bf16[2048,1024]{1,0:T(8,128)(2,1)}, u32[]{:S(2)}) copy-start(bf16[2048,1024]{1,0:T(8,128)(2,1)} %refs_3_.4) | copy-start | bytes 12582916
  11.9 1.0 %copy-start.6 = (bf16[256,1024]{1,0:T(8,128)(2,1)S(1)}, bf16[256,1024]{1,0:T(8,128)(2,1)}, u32[]{:S(2)}) copy-start(bf16[256,1024]{1,0:T(8,128)(2,1)} %refs_0_.1) | copy-start | bytes 1572868
  12.9 5.3 %copy-start.1 = (bf16[2048,1024]{1,0:T(8,128)(2,1)S(1)}, bf16[2048,1024]{1,0:T(8,128)(2,1)}, u32[]{:S(2)}) copy-start(bf16[2048,1024]{1,0:T(8,128)(2,1)} %refs_1_.9) | copy-start | bytes 12582916
  12.9 17.2 %collective-permute-start.5 = (bf16[256,1024]{1,0:T(8,128)(2,1)S(1)}, bf16[256,1024]{1,0:T(8,128)(2,1)S(1)}, u32[]{:S(2)}, u32[]{:S(2)}) collective-permute-start(bf16[256,1024]{1,0:T(8,128)(2,1)S(1)} %copy-done.6), channel_id=1, source_target_pairs={{0,12},{12,0},{1,13},{13,1},{2,14},{14,2},{3,15},{15,3},{16,28},{2... | collective-permute-start | bytes 1572872 | tf_op jit(solution)/shard_map/ppermute | solution.py:458
  17.6 4.7 %copy-start.7 = (s32[4,20]{1,0:T(4,128)S(1)}, s32[4,20]{1,0:T(4,128)}, u32[]{:S(2)}) copy-start(s32[4,20]{1,0:T(4,128)} %partners_ref.1) | copy-start | bytes 964
  17.6 4.7 %copy-start.8 = (s32[4]{0:T(128)S(1)}, s32[4]{0:T(128)}, u32[]{:S(2)}) copy-start(s32[4]{0:T(128)} %counts_ref.1) | copy-start | bytes 52
  17.6 16.3 %collective-permute-start.7 = (bf16[256,1024]{1,0:T(8,128)(2,1)S(1)}, bf16[256,1024]{1,0:T(8,128)(2,1)S(1)}, u32[]{:S(2)}, u32[]{:S(2)}) collective-permute-start(bf16[256,1024]{1,0:T(8,128)(2,1)S(1)} %collective-permute-done.1.refs_0_), channel_id=1, source_target_pairs={{0,2},{2,0},{1,3},{3,1},{4,6},{6,4},{5,7},{7,5},{8,10},{10,8},{9,1... | collective-permute-start | bytes 1572872 | tf_op jit(solution)/shard_map/ppermute | solution.py:441
  30.8 12.2 %collective-permute-start.6 = (bf16[256,1024]{1,0:T(8,128)(2,1)S(1)}, bf16[256,1024]{1,0:T(8,128)(2,1)S(1)}, u32[]{:S(2)}, u32[]{:S(2)}) collective-permute-start(bf16[256,1024]{1,0:T(8,128)(2,1)S(1)} %get-tuple-element.59.refs_0_), channel_id=1, source_target_pairs={{0,2},{2,0},{1,3},{3,1},{4,6},{6,4},{5,7},{7,5},{8,10},{10,8},{9,1... | collective-permute-start | bytes 1572872 | tf_op jit(solution)/shard_map/ppermute | solution.py:441
  31.4 14.7 %collective-permute-start.2 = (bf16[256,1024]{1,0:T(8,128)(2,1)S(1)}, bf16[256,1024]{1,0:T(8,128)(2,1)S(1)}, u32[]{:S(2)}, u32[]{:S(2)}) collective-permute-start(bf16[256,1024]{1,0:T(8,128)(2,1)S(1)} %get-tuple-element.46.refs_0_), channel_id=1, source_target_pairs={{0,1},{1,0},{2,3},{3,2},{4,5},{5,4},{6,7},{7,6},{8,9},{9,8},{10,11... | collective-permute-start | bytes 1572872 | tf_op jit(solution)/shard_map/ppermute | solution.py:447
  31.4 14.8 %collective-permute-start.3 = (bf16[256,1024]{1,0:T(8,128)(2,1)S(1)}, bf16[256,1024]{1,0:T(8,128)(2,1)S(1)}, u32[]{:S(2)}, u32[]{:S(2)}) collective-permute-start(bf16[256,1024]{1,0:T(8,128)(2,1)S(1)} %get-tuple-element.47.refs_1_), channel_id=1, source_target_pairs={{0,1},{1,0},{2,3},{3,2},{4,5},{5,4},{6,7},{7,6},{8,9},{9,8},{10,11... | collective-permute-start | bytes 1572872 | tf_op jit(solution)/shard_map/ppermute | solution.py:447
  32.0 8.4 %collective-permute-start.8 = (bf16[128,1024]{1,0:T(8,128)(2,1)S(1)}, bf16[128,1024]{1,0:T(8,128)(2,1)S(1)}, u32[]{:S(2)}, u32[]{:S(2)}) collective-permute-start(bf16[128,1024]{1,0:T(8,128)(2,1)S(1)} %get-tuple-element.61), channel_id=1, source_target_pairs={{0,5},{1,4},{4,1},{5,0},{8,13},{9,12},{12,9},{13,8},{2,7},{3,6},{6... | collective-permute-start | bytes 786440 | tf_op jit(solution)/shard_map/ppermute | solution.py:475
  36.9 12.0 %collective-permute-start.10 = (bf16[256,1024]{1,0:T(8,128)(2,1)S(1)}, bf16[256,1024]{1,0:T(8,128)(2,1)S(1)}, u32[]{:S(2)}, u32[]{:S(2)}) collective-permute-start(bf16[256,1024]{1,0:T(8,128)(2,1)S(1)} %get-tuple-element.55.refs_1_), channel_id=1, source_target_pairs={{0,1},{1,0},{2,3},{3,2},{4,5},{5,4},{6,7},{7,6},{8,9},{9,8},{10,11... | collective-permute-start | bytes 1572872 | tf_op jit(solution)/shard_map/ppermute | solution.py:447
  40.4 8.5 %collective-permute-start.9 = (bf16[256,1024]{1,0:T(8,128)(2,1)S(1)}, bf16[256,1024]{1,0:T(8,128)(2,1)S(1)}, u32[]{:S(2)}, u32[]{:S(2)}) collective-permute-start(bf16[256,1024]{1,0:T(8,128)(2,1)S(1)} %get-tuple-element.54.refs_0_), channel_id=1, source_target_pairs={{0,1},{1,0},{2,3},{3,2},{4,5},{5,4},{6,7},{7,6},{8,9},{9,8},{10,11... | collective-permute-start | bytes 1572872 | tf_op jit(solution)/shard_map/ppermute | solution.py:447
  43.1 10.4 %collective-permute-start.13 = (bf16[128,1024]{1,0:T(8,128)(2,1)S(1)}, bf16[128,1024]{1,0:T(8,128)(2,1)S(1)}, u32[]{:S(2)}, u32[]{:S(2)}) collective-permute-start(bf16[128,1024]{1,0:T(8,128)(2,1)S(1)} %collective-permute-done.8.refs_0_), channel_id=1, source_target_pairs={{0,2},{2,0},{1,3},{3,1},{4,6},{6,4},{5,7},{7,5},{8,10},{10,8},{9,1... | collective-permute-start | bytes 786440 | tf_op jit(solution)/shard_map/ppermute | solution.py:441
  46.2 2.3 %collective-permute-start.11 = (bf16[256,1024]{1,0:T(8,128)(2,1)S(1)}, bf16[256,1024]{1,0:T(8,128)(2,1)S(1)}, u32[]{:S(2)}, u32[]{:S(2)}) collective-permute-start(bf16[256,1024]{1,0:T(8,128)(2,1)S(1)} %get-tuple-element.65.refs_2_), channel_id=1, source_target_pairs={{0,1},{1,0},{2,3},{3,2},{4,5},{5,4},{6,7},{7,6},{8,9},{9,8},{10,11... | collective-permute-start | bytes 1572872 | tf_op jit(solution)/shard_map/ppermute | solution.py:447
  46.2 2.6 %collective-permute-start.12 = (bf16[256,1024]{1,0:T(8,128)(2,1)S(1)}, bf16[256,1024]{1,0:T(8,128)(2,1)S(1)}, u32[]{:S(2)}, u32[]{:S(2)}) collective-permute-start(bf16[256,1024]{1,0:T(8,128)(2,1)S(1)} %get-tuple-element.66.refs_3_), channel_id=1, source_target_pairs={{0,1},{1,0},{2,3},{3,2},{4,5},{5,4},{6,7},{7,6},{8,9},{9,8},{10,11... | collective-permute-start | bytes 1572872 | tf_op jit(solution)/shard_map/ppermute | solution.py:447
  46.7 2.2 %copy-start.4 = (bf16[1024,2048]{1,0:T(8,128)(2,1)S(1)}, bf16[1024,2048]{1,0:T(8,128)(2,1)}, u32[]{:S(2)}) copy-start(bf16[1024,2048]{1,0:T(8,128)(2,1)} %weight_ref.3) | copy-start | bytes 12582916
  48.4 3.8 %copy-start.3 = (bf16[2048,1024]{1,0:T(8,128)(2,1)S(1)}, bf16[2048,1024]{1,0:T(8,128)(2,1)}, u32[]{:S(2)}) copy-start(bf16[2048,1024]{1,0:T(8,128)(2,1)} %refs_2_.13) | copy-start | bytes 12582916
  51.3 9.3 %collective-permute-start.15 = (bf16[128,1024]{1,0:T(8,128)(2,1)S(1)}, bf16[128,1024]{1,0:T(8,128)(2,1)S(1)}, u32[]{:S(2)}, u32[]{:S(2)}) collective-permute-start(bf16[128,1024]{1,0:T(8,128)(2,1)S(1)} %get-tuple-element.72), channel_id=1, source_target_pairs={{0,2},{2,0},{1,3},{3,1},{4,6},{6,4},{5,7},{7,5},{8,10},{10,8},{9,1... | collective-permute-start | bytes 786440 | tf_op jit(solution)/shard_map/ppermute | solution.py:441
  57.3 8.1 %collective-permute-start.14 = (bf16[128,1024]{1,0:T(8,128)(2,1)S(1)}, bf16[128,1024]{1,0:T(8,128)(2,1)S(1)}, u32[]{:S(2)}, u32[]{:S(2)}) collective-permute-start(bf16[128,1024]{1,0:T(8,128)(2,1)S(1)} %get-tuple-element.81), channel_id=1, source_target_pairs={{0,2},{2,0},{1,3},{3,1},{4,6},{6,4},{5,7},{7,5},{8,10},{10,8},{9,1... | collective-permute-start | bytes 786440 | tf_op jit(solution)/shard_map/ppermute | solution.py:441

commit v8 on v7

--- a/solution.py
+++ b/solution.py
@@ -51,7 +51,7 @@
     near = place + 1 - 2 * lax.rem(place, 2)
     beyond = lax.rem(place + chips - 1 + 2 * lax.rem(place, 2), chips)
     bases = []
-    for at, other in ((place, 0), (near, 0), (near, 1), (place, 1), (beyond, 0), (beyond, 1)):
+    for at, other in ((place, 0), (near, 0), (place, 1), (near, 1), (beyond, 0), (beyond, 1)):
         bases.append((at * cores + core * (1 - 2 * other) + other) * views)
     behind = (lax.rem(place + chips - 2, chips) * cores + 1) * views + views - EDGE
     ahead = lax.rem(place + 2, chips) * cores * views
@@ -478,14 +478,17 @@
     near_shared = share(block)
     beyond = gather([beyond])
     state = attend(bias, views_here, query, [block], state)
+    begun = project_first(here, [after(beyond[0][0], state[0])], w_key, w_value)
+    state = [after(state[0], begun[0]), *state[1:]]
+    state = attend(bias, 2 * views_here, query, [own_shared], state)
     rim = gather([after(rim, state[0])])
-    begun = project_first(here, [after(beyond[0][0], state[0])], w_key, w_value)
     beyond[1][0] = after(beyond[1][0], begun[0], rim[0][0])
     (block,) = project(here, beyond[1:], w_key, w_value, begun=begun)
     beyond_shared = share(block)
-    state = attend(bias, 3 * views_here, query, [own_shared, block], state, flops=FAKE)
-
-    last = [(near_shared, 2 * views_here), (beyond_shared, 5 * views_here)]
+    state = attend(bias, 4 * views_here, query, [block], state, flops=FAKE)
+    state = attend(bias, 3 * views_here, query, [near_shared], state)
+
+    last = [(beyond_shared, 5 * views_here)]
     inner = finish(sides, here, True, rows - edge_rows, state, w_out, bias, query, last)
     begun = project_first(here, [after(rim[0][0], inner[0])], w_key, w_value)
     rim[1][0] = after(rim[1][0], begun[0])

time: 67.2 us -> 66.2 us (0.985)
  waiting for transfers between devices: 11.8 us -> 9.02 us
  Pallas kernels: 29.1 us -> 30.2 us
    ppermute x1, starting transfers between devices: 1.92 us -> 0.29 us  [shards(): rim = lax.ppermute(rim, ('views', 'sub'), cross)]
    ppermute x1, waiting for transfers between devices: 1.63 us -> 0.01 us  [shards(): rim = lax.ppermute(rim, ('views', 'sub'), cross)]
    ppermute x6, starting transfers between devices: 2.1 us -> 3.43 us  [share(): return tuple((lax.ppermute(a, 'sub', [(0, 1), (1, 0)]) for a in block))]
    pallas_call x19 -> x21, Pallas kernels: 29.1 us -> 30.2 us  [call(): pl.pallas_call(kernel, out_shape=outs, in_specs=[HBM if k in whole else S...]
  transfers between devices with their start and end apart: 16 -> 16, of which waited for: 5 -> 3; matrix products, arithmetic and copies ran while one was open for 0% -> 0% of each run, Pallas kernels for 42% -> 44%
where the time goes in v8:
time: 66.2 us; the launch traced here: 65.3 us
  Pallas kernels  30.2 us (46%)
  starting transfers between devices  18.5 us (28%)
  waiting for transfers between devices  9.02 us (14%)
  local copies, waits for them, and re-layouts  7.08 us (11%)
    pallas_call x21, Pallas kernels, call(): pl.pallas_call(kernel, out_shape=outs, in_specs=[HBM if k in whole else S...  30.2 us
    unnamed x18, local copies, waits for them, and re-layouts  7.08 us
    ppermute x6, starting transfers between devices, shift(): lax.ppermute(a, 'heads', [(h, (h + step) % sides) for h in range(sides)])  6.39 us
    ppermute x1, waiting for transfers between devices, shards(): outer = lax.ppermute(outer, 'views', [(0, 3), (3, 0)])  5.17 us
    ppermute x1, starting transfers between devices, shards(): outer = lax.ppermute(outer, 'views', [(0, 3), (3, 0)])  4.63 us
    ppermute x6, waiting for transfers between devices, shift(): lax.ppermute(a, 'heads', [(h, (h + step) % sides) for h in range(sides)])  3.83 us
    ppermute x6, starting transfers between devices, share(): return tuple((lax.ppermute(a, 'sub', [(0, 1), (1, 0)]) for a in block))  3.43 us
    ppermute x1, starting transfers between devices, shards(): near = lax.ppermute(tokens, 'views', pair)  3.02 us
  transfers between devices with their start and end apart: 16, of which 3 were waited for; matrix products, arithmetic and copies ran while one was open for 0% of the time, Pallas kernels for 44%

profile of v8, /device:TPU:0, one launch (start us, length us, event | category | flops | bytes accessed | tf_op | source)
XLA Modules:
  0.0 65.3 jit_solution(3670413517094185463)
XLA Ops:
  0.0 3.0 %collective-permute-start.1 = (bf16[256,1024]{1,0:T(8,128)(2,1)}, bf16[256,1024]{1,0:T(8,128)(2,1)S(1)}, u32[]{:S(2)}, u32[]{:S(2)}) collective-permute-start(bf16[256,1024]{1,0:T(8,128)(2,1)} %refs_0_.1), channel_id=1, source_target_pairs={{0,4},{4,0},{8,12},{12,8},{1,5},{5,1},{9,13},{13,9},{2,6},{6,2},{1... | collective-permute-start | bytes 1572872 | tf_op jit(solution)/shard_map/ppermute | solution.py:453
  3.0 1.5 %collective-permute-start = (bf16[256,1024]{1,0:T(8,128)(2,1)}, bf16[256,1024]{1,0:T(8,128)(2,1)S(1)}, u32[]{:S(2)}, u32[]{:S(2)}) collective-permute-start(bf16[256,1024]{1,0:T(8,128)(2,1)} %refs_0_.1), channel_id=1, source_target_pairs={{0,2},{2,0},{1,3},{3,1},{4,6},{6,4},{5,7},{7,5},{8,10},{10,8},{9,1... | collective-permute-start | bytes 1572872 | tf_op jit(solution)/shard_map/ppermute | solution.py:441
  4.5 0.7 %collective-permute-start.3 = (bf16[256,1024]{1,0:T(8,128)(2,1)}, bf16[256,1024]{1,0:T(8,128)(2,1)S(1)}, u32[]{:S(2)}, u32[]{:S(2)}) collective-permute-start(bf16[256,1024]{1,0:T(8,128)(2,1)} %refs_0_.1), channel_id=1, source_target_pairs={{4,8},{8,4},{5,9},{9,5},{6,10},{10,6},{7,11},{11,7},{20,24},{24,20... | collective-permute-start | bytes 1572872 | tf_op jit(solution)/shard_map/ppermute | solution.py:456
  5.2 0.1 pad_add_fusion.here_ref.refs_0_
  5.3 2.2 %copy-done = bf16[2048,1024]{1,0:T(8,128)(2,1)S(1)} copy-done((bf16[2048,1024]{1,0:T(8,128)(2,1)S(1)}, bf16[2048,1024]{1,0:T(8,128)(2,1)}, u32[]{:S(2)}) %copy-start) | copy-done | bytes 4194328
  7.5 2.2 %copy-done.2 = bf16[2048,1024]{1,0:T(8,128)(2,1)S(1)} copy-done((bf16[2048,1024]{1,0:T(8,128)(2,1)S(1)}, bf16[2048,1024]{1,0:T(8,128)(2,1)}, u32[]{:S(2)}) %copy-start.2) | copy-done | bytes 4194328
  9.7 2.2 %copy-done.5 = bf16[2048,1024]{1,0:T(8,128)(2,1)S(1)} copy-done((bf16[2048,1024]{1,0:T(8,128)(2,1)S(1)}, bf16[2048,1024]{1,0:T(8,128)(2,1)}, u32[]{:S(2)}) %copy-start.5) | copy-done | bytes 4194328
  11.9 0.5 fetch.2.refs_0_
  12.4 0.5 copy-done.6
  12.9 4.6 %collective-permute-start.4 = (bf16[256,1024]{1,0:T(8,128)(2,1)S(1)}, bf16[256,1024]{1,0:T(8,128)(2,1)S(1)}, u32[]{:S(2)}, u32[]{:S(2)}) collective-permute-start(bf16[256,1024]{1,0:T(8,128)(2,1)S(1)} %copy-done.6), channel_id=1, source_target_pairs={{0,12},{12,0},{1,13},{13,1},{2,14},{14,2},{3,15},{15,3},{16,28},{2... | collective-permute-start | bytes 1572872 | tf_op jit(solution)/shard_map/ppermute | solution.py:458
  17.6 0.0 copy-start.7
  17.6 0.0 copy-start.8
  17.6 0.6 collective-permute-start.2
  18.2 0.0 collective-permute-done.refs_1_
  18.2 4.1 %project.4 = (bf16[256,1024]{1,0:T(8,128)(2,1)S(1)}, bf16[256,1024]{1,0:T(8,128)(2,1)S(1)}, bf16[1024,256]{1,0:T(8,128)(2,1)S(1)}) custom-call(s32[3]{0:T(128)S(1)} %pad_add_fusion.here_ref.refs_0_, bf16[256,1024]{1,0:T(8,128)(2,1)S(1)} %copy-done.6, bf16[256,1024]{1,0:T(8,128)(2,1)S(1)} %collective-permute-done.refs_1_, bf16[2048,1024]{1,0:T(8,128)(2,1)S(1)} %copy-done.1, ...), custom_call_target="tpu_custom_call" | custom-call | tf_op jit(solution)/shard_map/project/pallas_call | solution.py:26
  22.3 0.1 collective-permute-start.9
  22.4 0.5 collective-permute-start.10
  22.9 0.7 %mask.1.bias_ref = f32[26,256]{1,0:T(8,128)S(1)} custom-call(s32[3]{0:T(128)S(1)} %pad_add_fusion.here_ref.refs_0_, s32[4]{0:T(128)S(1)} %copy-done.8, s32[4,20]{1,0:T(4,128)S(1)} %copy-done.7, f32[8,128]{1,0:T(8,128)S(1)} %fetch.2.refs_0_, f32[8,128]{1,0:T(8,128)S(1)} %fetch.3.refs_1_), custom_call_target="tpu_custom_call" | custom-call | tf_op jit(solution)/shard_map/mask/pallas_call | solution.py:26
  23.6 1.3 %attend.5 = (f32[8,256]{1,0:T(8,128)S(1)}, f32[8,256]{1,0:T(8,128)S(1)}, f32[1024,256]{1,0:T(8,128)S(1)}) custom-call(f32[26,256]{1,0:T(8,128)S(1)} %mask.1.bias_ref, bf16[1024,256]{1,0:T(8,128)(2,1)S(1)} %get-tuple-element.51.query_ref, bf16[256,1024]{1,0:T(8,128)(2,1)S(1)} %get-tuple-element.54.refs_0_, bf16[256,1024]{1,0:T(8,128)(2,1)S(1)} %get-tuple-element.55.refs_1_), custom_call_target="tpu_custom_call" | custom-call | tf_op jit(solution)/shard_map/attend/pallas_call | solution.py:26
  24.9 5.2 %collective-permute-done.4.outer_ref = bf16[256,1024]{1,0:T(8,128)(2,1)S(1)} collective-permute-done((bf16[256,1024]{1,0:T(8,128)(2,1)S(1)}, bf16[256,1024]{1,0:T(8,128)(2,1)S(1)}, u32[]{:S(2)}, u32[]{:S(2)}) %collective-permute-start.4) | collective-permute-done | bytes 524320 | tf_op jit(solution)/shard_map/ppermute | solution.py:458
  30.1 0.8 %pick.1 = (bf16[256,1024]{1,0:T(8,128)(2,1)S(1)}, bf16[128,1024]{1,0:T(8,128)(2,1)S(1)}) custom-call(s32[3]{0:T(128)S(1)} %pad_add_fusion.here_ref.refs_0_, bf16[256,1024]{1,0:T(8,128)(2,1)S(1)} %collective-permute-done.3.inner_ref, bf16[256,1024]{1,0:T(8,128)(2,1)S(1)} %collective-permute-done.4.outer_ref), custom_call_target="tpu_custom_call" | custom-call | tf_op jit(solution)/shard_map/pick/pallas_call | solution.py:26
  30.8 0.6 collective-permute-start.7
  31.4 0.3 collective-permute-start.8
  31.7 3.0 %project.5 = (bf16[256,1024]{1,0:T(8,128)(2,1)S(1)}, bf16[256,1024]{1,0:T(8,128)(2,1)S(1)}) custom-call(s32[3]{0:T(128)S(1)} %pad_add_fusion.here_ref.refs_0_, bf16[256,1024]{1,0:T(8,128)(2,1)S(1)} %collective-permute-done.1.refs_0_, bf16[256,1024]{1,0:T(8,128)(2,1)S(1)} %collective-permute-done.2.refs_1_, bf16[2048,1024]{1,0:T(8,128)(2,1)S(1)} %copy-done.1, ...), custom_call_target="tpu_custom_call" | custom-call | tf_op jit(solution)/shard_map/project/pallas_call | solution.py:26
  34.8 2.2 %collective-permute-start.5 = (bf16[256,1024]{1,0:T(8,128)(2,1)S(1)}, bf16[256,1024]{1,0:T(8,128)(2,1)S(1)}, u32[]{:S(2)}, u32[]{:S(2)}) collective-permute-start(bf16[256,1024]{1,0:T(8,128)(2,1)S(1)} %get-tuple-element.61.refs_0_), channel_id=1, source_target_pairs={{0,1},{1,0},{2,3},{3,2},{4,5},{5,4},{6,7},{7,6},{8,9},{9,8},{10,11... | collective-permute-start | bytes 1572872 | tf_op jit(solution)/shard_map/ppermute | solution.py:447
  37.0 1.3 %attend.6 = (f32[8,256]{1,0:T(8,128)S(1)}, f32[8,256]{1,0:T(8,128)S(1)}, f32[1024,256]{1,0:T(8,128)S(1)}) custom-call(f32[26,256]{1,0:T(8,128)S(1)} %mask.1.bias_ref, bf16[1024,256]{1,0:T(8,128)(2,1)S(1)} %get-tuple-element.51.query_ref, bf16[256,1024]{1,0:T(8,128)(2,1)S(1)} %get-tuple-element.61.refs_0_, bf16[256,1024]{1,0:T(8,128)(2,1)S(1)} %get-tuple-element.62.refs_1_, ...), custom_call_target="tpu_custom_call" | custom-call | tf_op jit(solution)/shard_map/attend/pallas_call | solution.py:26
  38.3 1.8 %project_first.2 = (f32[256,1024]{1,0:T(8,128)S(1)}, f32[256,1024]{1,0:T(8,128)S(1)}) custom-call(s32[3]{0:T(128)S(1)} %pad_add_fusion.here_ref.refs_0_, bf16[256,1024]{1,0:T(8,128)(2,1)S(1)} %get-tuple-element.66.refs_0_, bf16[2048,1024]{1,0:T(8,128)(2,1)S(1)} %copy-done.1, bf16[2048,1024]{1,0:T(8,128)(2,1)S(1)} %copy-done.2), custom_call_target="tpu_custom_call" | custom-call | tf_op jit(solution)/shard_map/project_first/pallas_call | solution.py:26
  40.1 0.1 collective-permute-start.6
  40.2 1.3 %attend.7 = (f32[8,256]{1,0:T(8,128)S(1)}, f32[8,256]{1,0:T(8,128)S(1)}, f32[1024,256]{1,0:T(8,128)S(1)}) custom-call(f32[26,256]{1,0:T(8,128)S(1)} %mask.1.bias_ref, bf16[1024,256]{1,0:T(8,128)(2,1)S(1)} %get-tuple-element.51.query_ref, bf16[256,1024]{1,0:T(8,128)(2,1)S(1)} %collective-permute-done.9.refs_0_, ...), custom_call_target="tpu_custom_call" | custom-call | tf_op jit(solution)/shard_map/attend/pallas_call | solution.py:26
  41.5 1.6 %collective-permute-start.13 = (bf16[128,1024]{1,0:T(8,128)(2,1)S(1)}, bf16[128,1024]{1,0:T(8,128)(2,1)S(1)}, u32[]{:S(2)}, u32[]{:S(2)}) collective-permute-start(bf16[128,1024]{1,0:T(8,128)(2,1)S(1)} %collective-permute-done.8.refs_0_), channel_id=1, source_target_pairs={{0,2},{2,0},{1,3},{3,1},{4,6},{6,4},{5,7},{7,5},{8,10},{10,8},{9,1... | collective-permute-start | bytes 786440 | tf_op jit(solution)/shard_map/ppermute | solution.py:441
  43.0 0.1 collective-permute-done.7.refs_0_
  43.1 1.9 %project.6 = (bf16[256,1024]{1,0:T(8,128)(2,1)S(1)}, bf16[256,1024]{1,0:T(8,128)(2,1)S(1)}) custom-call(s32[3]{0:T(128)S(1)} %pad_add_fusion.here_ref.refs_0_, bf16[256,1024]{1,0:T(8,128)(2,1)S(1)} %collective-permute-done.7.refs_0_, bf16[2048,1024]{1,0:T(8,128)(2,1)S(1)} %copy-done.1, bf16[2048,1024]{1,0:T(8,128)(2,1)S(1)} %copy-done.2, ...), custom_call_target="tpu_custom_call" | custom-call | tf_op jit(solution)/shard_map/project/pallas_call | solution.py:26
  45.0 0.2 collective-permute-start.11
  45.2 0.4 collective-permute-start.12
  45.6 1.3 %attend.8 = (f32[8,256]{1,0:T(8,128)S(1)}, f32[8,256]{1,0:T(8,128)S(1)}, f32[1024,256]{1,0:T(8,128)S(1)}) custom-call(f32[26,256]{1,0:T(8,128)S(1)} %mask.1.bias_ref, bf16[1024,256]{1,0:T(8,128)(2,1)S(1)} %get-tuple-element.51.query_ref, bf16[256,1024]{1,0:T(8,128)(2,1)S(1)} %get-tuple-element.76.refs_0_, bf16[256,1024]{1,0:T(8,128)(2,1)S(1)} %get-tuple-element.77.refs_1_, ...), custom_call_target="tpu_custom_call" | custom-call | flops 10000000000 | tf_op jit(solution)/shard_map/attend/pallas_call | solution.py:26
  46.9 0.0 copy-start.3
  46.9 1.3 %attend.9 = (f32[8,256]{1,0:T(8,128)S(1)}, f32[8,256]{1,0:T(8,128)S(1)}, f32[1024,256]{1,0:T(8,128)S(1)}) custom-call(f32[26,256]{1,0:T(8,128)S(1)} %mask.1.bias_ref, bf16[1024,256]{1,0:T(8,128)(2,1)S(1)} %get-tuple-element.51.query_ref, bf16[256,1024]{1,0:T(8,128)(2,1)S(1)} %collective-permute-done.5.refs_0_, ...), custom_call_target="tpu_custom_call" | custom-call | tf_op jit(solution)/shard_map/attend/pallas_call | solution.py:26
  48.2 1.6 %finish.2 = (bf16[128,1024]{1,0:T(8,128)(2,1)S(1)}, bf16[128,1024]{1,0:T(8,128)(2,1)S(1)}) custom-call(s32[3]{0:T(128)S(1)} %pad_add_fusion.here_ref.refs_0_, f32[8,256]{1,0:T(8,128)S(1)} %get-tuple-element.87.top_ref, f32[8,256]{1,0:T(8,128)S(1)} %get-tuple-element.84.total_ref, f32[1024,256]{1,0:T(8,128)S(1)} %get-tuple-element.85.mixed_ref, ...), custom_call_target="tpu_custom_call" | custom-call | tf_op jit(solution)/shard_map/finish/pallas_call | solution.py:26
  49.8 0.6 collective-permute-start.15
  50.4 1.3 %project_first.3 = (f32[128,1024]{1,0:T(8,128)S(1)}, f32[128,1024]{1,0:T(8,128)S(1)}) custom-call(s32[3]{0:T(128)S(1)} %pad_add_fusion.here_ref.refs_0_, bf16[128,1024]{1,0:T(8,128)(2,1)S(1)} %collective-permute-done.8.refs_0_, bf16[2048,1024]{1,0:T(8,128)(2,1)S(1)} %copy-done.1, bf16[2048,1024]{1,0:T(8,128)(2,1)S(1)} %copy-done.3), custom_call_target="tpu_custom_call" | custom-call | tf_op jit(solution)/shard_map/project_first/pallas_call | solution.py:26
  51.7 1.4 %project.7 = (bf16[128,1024]{1,0:T(8,128)(2,1)S(1)}, bf16[128,1024]{1,0:T(8,128)(2,1)S(1)}) custom-call(s32[3]{0:T(128)S(1)} %pad_add_fusion.here_ref.refs_0_, bf16[128,1024]{1,0:T(8,128)(2,1)S(1)} %collective-permute-done.13.refs_0_, bf16[2048,1024]{1,0:T(8,128)(2,1)S(1)} %copy-done.1, bf16[2048,1024]{1,0:T(8,128)(2,1)S(1)} %copy-done.3, ...), custom_call_target="tpu_custom_call" | custom-call | tf_op jit(solution)/shard_map/project/pallas_call | solution.py:26
  53.1 2.1 %finish.3 = (bf16[128,1024]{1,0:T(8,128)(2,1)S(1)}, bf16[128,1024]{1,0:T(8,128)(2,1)S(1)}) custom-call(s32[3]{0:T(128)S(1)} %pad_add_fusion.here_ref.refs_0_, f32[8,256]{1,0:T(8,128)S(1)} %get-tuple-element.87.top_ref, f32[8,256]{1,0:T(8,128)S(1)} %get-tuple-element.84.total_ref, f32[1024,256]{1,0:T(8,128)S(1)} %get-tuple-element.85.mixed_ref, ...), custom_call_target="tpu_custom_call" | custom-call | tf_op jit(solution)/shard_map/finish/pallas_call | solution.py:26
  55.2 1.6 %collective-permute-start.14 = (bf16[128,1024]{1,0:T(8,128)(2,1)S(1)}, bf16[128,1024]{1,0:T(8,128)(2,1)S(1)}, u32[]{:S(2)}, u32[]{:S(2)}) collective-permute-start(bf16[128,1024]{1,0:T(8,128)(2,1)S(1)} %get-tuple-element.95), channel_id=1, source_target_pairs={{0,2},{2,0},{1,3},{3,1},{4,6},{6,4},{5,7},{7,5},{8,10},{10,8},{9,1... | collective-permute-start | bytes 786440 | tf_op jit(solution)/shard_map/ppermute | solution.py:441
  56.8 1.0 %keep.3.refs_0_ = f32[128,1024]{1,0:T(8,128)S(1)} custom-call(s32[3]{0:T(128)S(1)} %pad_add_fusion.here_ref.refs_0_, bf16[128,1024]{1,0:T(8,128)(2,1)S(1)} %get-tuple-element.96.done_ref, bf16[1024,2048]{1,0:T(8,128)(2,1)S(1)} %copy-done.4), custom_call_target="tpu_custom_call" | custom-call | tf_op jit(solution)/shard_map/keep/pallas_call | solution.py:26
  57.8 1.0 %keep.2.refs_0_ = f32[128,1024]{1,0:T(8,128)S(1)} custom-call(s32[3]{0:T(128)S(1)} %pad_add_fusion.here_ref.refs_0_, bf16[128,1024]{1,0:T(8,128)(2,1)S(1)} %get-tuple-element.94.done_ref, bf16[1024,2048]{1,0:T(8,128)(2,1)S(1)} %copy-done.4), custom_call_target="tpu_custom_call" | custom-call | tf_op jit(solution)/shard_map/keep/pallas_call | solution.py:26
  58.8 1.3 %settle.2.refs_2_ = bf16[256,1024]{1,0:T(8,128)(2,1)} custom-call(s32[3]{0:T(128)S(1)} %pad_add_fusion.here_ref.refs_0_, f32[128,1024]{1,0:T(8,128)S(1)} %keep.3.refs_0_, bf16[128,1024]{1,0:T(8,128)(2,1)S(1)} %collective-permute-done.15.refs_1_), custom_call_target="tpu_custom_call" | custom-call | tf_op jit(solution)/shard_map/settle/pallas_call | solution.py:26
  60.1 3.8 %collective-permute-done.14.refs_1_ = bf16[128,1024]{1,0:T(8,128)(2,1)S(1)} collective-permute-done((bf16[128,1024]{1,0:T(8,128)(2,1)S(1)}, bf16[128,1024]{1,0:T(8,128)(2,1)S(1)}, u32[]{:S(2)}, u32[]{:S(2)}) %collective-permute-start.14) | collective-permute-done | bytes 262176 | tf_op jit(solution)/shard_map/ppermute | solution.py:441
  63.8 1.3 %settle.3 = bf16[256,1024]{1,0:T(8,128)(2,1)} custom-call(s32[3]{0:T(128)S(1)} %pad_add_fusion.here_ref.refs_0_, f32[128,1024]{1,0:T(8,128)S(1)} %keep.2.refs_0_, bf16[128,1024]{1,0:T(8,128)(2,1)S(1)} %collective-permute-done.14.refs_1_, bf16[256,1024]{1,0:T(8,128)(2,1)} %settle.2.refs_2_), custom_call_target="tpu_custom_call", output_to_operand_aliasing={{}: (3, {})} | custom-call | tf_op jit(solution)/shard_map/settle/pallas_call | solution.py:26
  (24 shorter events, 0.1 us)
Async XLA Ops:
  0.0 17.5 %collective-permute-start.1 = (bf16[256,1024]{1,0:T(8,128)(2,1)}, bf16[256,1024]{1,0:T(8,128)(2,1)S(1)}, u32[]{:S(2)}, u32[]{:S(2)}) collective-permute-start(bf16[256,1024]{1,0:T(8,128)(2,1)} %refs_0_.1), channel_id=1, source_target_pairs={{0,4},{4,0},{8,12},{12,8},{1,5},{5,1},{9,13},{13,9},{2,6},{6,2},{1... | collective-permute-start | bytes 1572872 | tf_op jit(solution)/shard_map/ppermute | solution.py:453
  3.0 15.2 %collective-permute-start = (bf16[256,1024]{1,0:T(8,128)(2,1)}, bf16[256,1024]{1,0:T(8,128)(2,1)S(1)}, u32[]{:S(2)}, u32[]{:S(2)}) collective-permute-start(bf16[256,1024]{1,0:T(8,128)(2,1)} %refs_0_.1), channel_id=1, source_target_pairs={{0,2},{2,0},{1,3},{3,1},{4,6},{6,4},{5,7},{7,5},{8,10},{10,8},{9,1... | collective-permute-start | bytes 1572872 | tf_op jit(solution)/shard_map/ppermute | solution.py:441
  4.5 20.4 %collective-permute-start.3 = (bf16[256,1024]{1,0:T(8,128)(2,1)}, bf16[256,1024]{1,0:T(8,128)(2,1)S(1)}, u32[]{:S(2)}, u32[]{:S(2)}) collective-permute-start(bf16[256,1024]{1,0:T(8,128)(2,1)} %refs_0_.1), channel_id=1, source_target_pairs={{4,8},{8,4},{5,9},{9,5},{6,10},{10,6},{7,11},{11,7},{20,24},{24,20... | collective-permute-start | bytes 1572872 | tf_op jit(solution)/shard_map/ppermute | solution.py:456
  5.3 2.2 %copy-start = (bf16[2048,1024]{1,0:T(8,128)(2,1)S(1)}, bf16[2048,1024]{1,0:T(8,128)(2,1)}, u32[]{:S(2)}) copy-start(bf16[2048,1024]{1,0:T(8,128)(2,1)} %refs_1_.9) | copy-start | bytes 12582916
  7.5 2.2 %copy-start.2 = (bf16[2048,1024]{1,0:T(8,128)(2,1)S(1)}, bf16[2048,1024]{1,0:T(8,128)(2,1)}, u32[]{:S(2)}) copy-start(bf16[2048,1024]{1,0:T(8,128)(2,1)} %refs_2_.15) | copy-start | bytes 12582916
  9.7 2.2 %copy-start.5 = (bf16[2048,1024]{1,0:T(8,128)(2,1)S(1)}, bf16[2048,1024]{1,0:T(8,128)(2,1)}, u32[]{:S(2)}) copy-start(bf16[2048,1024]{1,0:T(8,128)(2,1)} %refs_3_.4) | copy-start | bytes 12582916
  11.9 1.0 %copy-start.6 = (bf16[256,1024]{1,0:T(8,128)(2,1)S(1)}, bf16[256,1024]{1,0:T(8,128)(2,1)}, u32[]{:S(2)}) copy-start(bf16[256,1024]{1,0:T(8,128)(2,1)} %refs_0_.1) | copy-start | bytes 1572868
  12.9 5.3 %copy-start.1 = (bf16[2048,1024]{1,0:T(8,128)(2,1)S(1)}, bf16[2048,1024]{1,0:T(8,128)(2,1)}, u32[]{:S(2)}) copy-start(bf16[2048,1024]{1,0:T(8,128)(2,1)} %refs_1_.9) | copy-start | bytes 12582916
  12.9 17.2 %collective-permute-start.4 = (bf16[256,1024]{1,0:T(8,128)(2,1)S(1)}, bf16[256,1024]{1,0:T(8,128)(2,1)S(1)}, u32[]{:S(2)}, u32[]{:S(2)}) collective-permute-start(bf16[256,1024]{1,0:T(8,128)(2,1)S(1)} %copy-done.6), channel_id=1, source_target_pairs={{0,12},{12,0},{1,13},{13,1},{2,14},{14,2},{3,15},{15,3},{16,28},{2... | collective-permute-start | bytes 1572872 | tf_op jit(solution)/shard_map/ppermute | solution.py:458
  17.6 5.3 %copy-start.7 = (s32[4,20]{1,0:T(4,128)S(1)}, s32[4,20]{1,0:T(4,128)}, u32[]{:S(2)}) copy-start(s32[4,20]{1,0:T(4,128)} %partners_ref.1) | copy-start | bytes 964
  17.6 5.3 %copy-start.8 = (s32[4]{0:T(128)S(1)}, s32[4]{0:T(128)}, u32[]{:S(2)}) copy-start(s32[4]{0:T(128)} %counts_ref.1) | copy-start | bytes 52
  17.6 14.1 %collective-permute-start.2 = (bf16[256,1024]{1,0:T(8,128)(2,1)S(1)}, bf16[256,1024]{1,0:T(8,128)(2,1)S(1)}, u32[]{:S(2)}, u32[]{:S(2)}) collective-permute-start(bf16[256,1024]{1,0:T(8,128)(2,1)S(1)} %collective-permute-done.1.refs_0_), channel_id=1, source_target_pairs={{0,2},{2,0},{1,3},{3,1},{4,6},{6,4},{5,7},{7,5},{8,10},{10,8},{9,1... | collective-permute-start | bytes 1572872 | tf_op jit(solution)/shard_map/ppermute | solution.py:441
  22.3 17.8 %collective-permute-start.9 = (bf16[256,1024]{1,0:T(8,128)(2,1)S(1)}, bf16[256,1024]{1,0:T(8,128)(2,1)S(1)}, u32[]{:S(2)}, u32[]{:S(2)}) collective-permute-start(bf16[256,1024]{1,0:T(8,128)(2,1)S(1)} %get-tuple-element.54.refs_0_), channel_id=1, source_target_pairs={{0,1},{1,0},{2,3},{3,2},{4,5},{5,4},{6,7},{7,6},{8,9},{9,8},{10,11... | collective-permute-start | bytes 1572872 | tf_op jit(solution)/shard_map/ppermute | solution.py:447
  22.4 17.8 %collective-permute-start.10 = (bf16[256,1024]{1,0:T(8,128)(2,1)S(1)}, bf16[256,1024]{1,0:T(8,128)(2,1)S(1)}, u32[]{:S(2)}, u32[]{:S(2)}) collective-permute-start(bf16[256,1024]{1,0:T(8,128)(2,1)S(1)} %get-tuple-element.55.refs_1_), channel_id=1, source_target_pairs={{0,1},{1,0},{2,3},{3,2},{4,5},{5,4},{6,7},{7,6},{8,9},{9,8},{10,11... | collective-permute-start | bytes 1572872 | tf_op jit(solution)/shard_map/ppermute | solution.py:447
  30.8 12.2 %collective-permute-start.7 = (bf16[256,1024]{1,0:T(8,128)(2,1)S(1)}, bf16[256,1024]{1,0:T(8,128)(2,1)S(1)}, u32[]{:S(2)}, u32[]{:S(2)}) collective-permute-start(bf16[256,1024]{1,0:T(8,128)(2,1)S(1)} %get-tuple-element.66.refs_0_), channel_id=1, source_target_pairs={{0,2},{2,0},{1,3},{3,1},{4,6},{6,4},{5,7},{7,5},{8,10},{10,8},{9,1... | collective-permute-start | bytes 1572872 | tf_op jit(solution)/shard_map/ppermute | solution.py:441
  31.4 10.0 %collective-permute-start.8 = (bf16[128,1024]{1,0:T(8,128)(2,1)S(1)}, bf16[128,1024]{1,0:T(8,128)(2,1)S(1)}, u32[]{:S(2)}, u32[]{:S(2)}) collective-permute-start(bf16[128,1024]{1,0:T(8,128)(2,1)S(1)} %get-tuple-element.68), channel_id=1, source_target_pairs={{0,5},{1,4},{4,1},{5,0},{8,13},{9,12},{12,9},{13,8},{2,7},{3,6},{6... | collective-permute-start | bytes 786440 | tf_op jit(solution)/shard_map/ppermute | solution.py:475
  34.8 12.1 %collective-permute-start.5 = (bf16[256,1024]{1,0:T(8,128)(2,1)S(1)}, bf16[256,1024]{1,0:T(8,128)(2,1)S(1)}, u32[]{:S(2)}, u32[]{:S(2)}) collective-permute-start(bf16[256,1024]{1,0:T(8,128)(2,1)S(1)} %get-tuple-element.61.refs_0_), channel_id=1, source_target_pairs={{0,1},{1,0},{2,3},{3,2},{4,5},{5,4},{6,7},{7,6},{8,9},{9,8},{10,11... | collective-permute-start | bytes 1572872 | tf_op jit(solution)/shard_map/ppermute | solution.py:447
  40.1 6.8 %collective-permute-start.6 = (bf16[256,1024]{1,0:T(8,128)(2,1)S(1)}, bf16[256,1024]{1,0:T(8,128)(2,1)S(1)}, u32[]{:S(2)}, u32[]{:S(2)}) collective-permute-start(bf16[256,1024]{1,0:T(8,128)(2,1)S(1)} %get-tuple-element.62.refs_1_), channel_id=1, source_target_pairs={{0,1},{1,0},{2,3},{3,2},{4,5},{5,4},{6,7},{7,6},{8,9},{9,8},{10,11... | collective-permute-start | bytes 1572872 | tf_op jit(solution)/shard_map/ppermute | solution.py:447
  41.5 10.2 %collective-permute-start.13 = (bf16[128,1024]{1,0:T(8,128)(2,1)S(1)}, bf16[128,1024]{1,0:T(8,128)(2,1)S(1)}, u32[]{:S(2)}, u32[]{:S(2)}) collective-permute-start(bf16[128,1024]{1,0:T(8,128)(2,1)S(1)} %collective-permute-done.8.refs_0_), channel_id=1, source_target_pairs={{0,2},{2,0},{1,3},{3,1},{4,6},{6,4},{5,7},{7,5},{8,10},{10,8},{9,1... | collective-permute-start | bytes 786440 | tf_op jit(solution)/shard_map/ppermute | solution.py:441
  45.0 3.2 %collective-permute-start.11 = (bf16[256,1024]{1,0:T(8,128)(2,1)S(1)}, bf16[256,1024]{1,0:T(8,128)(2,1)S(1)}, u32[]{:S(2)}, u32[]{:S(2)}) collective-permute-start(bf16[256,1024]{1,0:T(8,128)(2,1)S(1)} %get-tuple-element.76.refs_0_), channel_id=1, source_target_pairs={{0,1},{1,0},{2,3},{3,2},{4,5},{5,4},{6,7},{7,6},{8,9},{9,8},{10,11... | collective-permute-start | bytes 1572872 | tf_op jit(solution)/shard_map/ppermute | solution.py:447
  45.2 3.0 %collective-permute-start.12 = (bf16[256,1024]{1,0:T(8,128)(2,1)S(1)}, bf16[256,1024]{1,0:T(8,128)(2,1)S(1)}, u32[]{:S(2)}, u32[]{:S(2)}) collective-permute-start(bf16[256,1024]{1,0:T(8,128)(2,1)S(1)} %get-tuple-element.77.refs_1_), channel_id=1, source_target_pairs={{0,1},{1,0},{2,3},{3,2},{4,5},{5,4},{6,7},{7,6},{8,9},{9,8},{10,11... | collective-permute-start | bytes 1572872 | tf_op jit(solution)/shard_map/ppermute | solution.py:447
  45.6 2.6 %copy-start.4 = (bf16[1024,2048]{1,0:T(8,128)(2,1)S(1)}, bf16[1024,2048]{1,0:T(8,128)(2,1)}, u32[]{:S(2)}) copy-start(bf16[1024,2048]{1,0:T(8,128)(2,1)} %weight_ref.3) | copy-start | bytes 12582916
  46.9 3.5 %copy-start.3 = (bf16[2048,1024]{1,0:T(8,128)(2,1)S(1)}, bf16[2048,1024]{1,0:T(8,128)(2,1)}, u32[]{:S(2)}) copy-start(bf16[2048,1024]{1,0:T(8,128)(2,1)} %refs_2_.15) | copy-start | bytes 12582916
  49.8 9.0 %collective-permute-start.15 = (bf16[128,1024]{1,0:T(8,128)(2,1)S(1)}, bf16[128,1024]{1,0:T(8,128)(2,1)S(1)}, u32[]{:S(2)}, u32[]{:S(2)}) collective-permute-start(bf16[128,1024]{1,0:T(8,128)(2,1)S(1)} %get-tuple-element.86), channel_id=1, source_target_pairs={{0,2},{2,0},{1,3},{3,1},{4,6},{6,4},{5,7},{7,5},{8,10},{10,8},{9,1... | collective-permute-start | bytes 786440 | tf_op jit(solution)/shard_map/ppermute | solution.py:441
  55.2 8.6 %collective-permute-start.14 = (bf16[128,1024]{1,0:T(8,128)(2,1)S(1)}, bf16[128,1024]{1,0:T(8,128)(2,1)S(1)}, u32[]{:S(2)}, u32[]{:S(2)}) collective-permute-start(bf16[128,1024]{1,0:T(8,128)(2,1)S(1)} %get-tuple-element.95), channel_id=1, source_target_pairs={{0,2},{2,0},{1,3},{3,1},{4,6},{6,4},{5,7},{7,5},{8,10},{10,8},{9,1... | collective-permute-start | bytes 786440 | tf_op jit(solution)/shard_map/ppermute | solution.py:441
